TPU v7x, 32 devices: a whole 2x2x4 slice. The times are simulated.
32 devices in a mesh: rows: 8 (over z, y), keys: 4 (over x, core).
Axes of the slice: x: 2, y: 2, z: 4, core: 2. Of those that a mesh axis runs over, the one named last changes fastest.
Arguments:
- activations: bfloat16 [8, 896, 1024], P('rows', 'keys'), may hold values from -6 to 6
- segments: int32 [8, 896], P('rows'), may hold values from 0 to 15, never falling along the last dimension, each value on 1 to 256 neighbouring positions
- prefix_keys: bfloat16 [2, 64, 1024], P(None, 'keys'), may hold values from -6 to 6
- prefix_values: bfloat16 [2, 64, 1024], P(None, 'keys'), may hold values from -6 to 6
- w_query: bfloat16 [2, 1024, 1024], P(None, 'rows'), may hold values from -0.1875 to 0.1875
- w_key: bfloat16 [2, 1024, 1024], P(None, 'rows'), may hold values from -0.1875 to 0.1875
- w_value: bfloat16 [2, 1024, 1024], P(None, 'rows'), may hold values from -0.1875 to 0.1875
- w_out: bfloat16 [2, 1024, 1024], P(None, 'rows'), may hold values from -1.5 to 1.5
- w_up: bfloat16 [2, 1024, 4096], P(None, 'rows'), may hold values from -0.1875 to 0.1875
- ff_bias: float32 [2, 4096], replicated, may hold values from -3 to 3
- w_down: bfloat16 [2, 4096, 1024], P(None, 'rows'), may hold values from -0.09375 to 0.09375
- ln_gain: float32 [2, 2, 1024], replicated, may hold values from 0.5 to 1.5
- ln_bias: float32 [2, 2, 1024], replicated, may hold values from -1.2 to 1.2
- cotangent: bfloat16 [8, 896, 1024], P('rows', 'keys'), may hold values from -6 to 6
Outputs:
- block_output: bfloat16 [8, 896, 1024], P('rows', 'keys')
- input_grad: float32 [8, 896, 1024], P('rows', 'keys')
- prefix_key_grad: float32 [2, 64, 1024], P(None, 'keys')
- prefix_value_grad: float32 [2, 64, 1024], P(None, 'keys')
Inputs may be any that keep to these rules, and one draw needn't show every extreme that they name: `segments`: along each row the pair ids never fall, each pair covers 1 to 256 positions, and one pair of each row covers exactly 256.
All inputs are finite; a program needn't handle non-finite values.
Results may differ from a plain program's by a relative error of at most 0.025.
Values may be sent and summed in bfloat16 or wider, within the bound.
No kernel may reach another device: no remote copies, remote signals or barrier semaphores. Data moves between devices by JAX's collectives and lax.ppermute only.
A program may use at most 256 MiB of HBM per device.

v0:
```python
from functools import partial

import jax
import jax.numpy as jnp
from jax import lax
from jax.sharding import PartitionSpec as P

H = 16
HD = 64
LAYERS = 2


NORM_EPSILON = 1e-05
MASKED_SCORE = -1000000000.0
SCORE_SCALE = 0.125


def combined_all(part, axis, combine):
    gathered = lax.all_gather(part, axis)

    def take(source):
        return lax.dynamic_index_in_dim(gathered, source, 0, False)

    return lax.fori_loop(
        1, lax.axis_size(axis), lambda source, state: combine(state, take(source)), take(0)
    )


def layer_norm(hidden, gain, shift):
    centered = hidden - jnp.mean(hidden, -1, keepdims=True)
    inverse = lax.rsqrt(jnp.mean(centered * centered, -1, keepdims=True) + NORM_EPSILON)
    normed = centered * inverse
    return (normed * gain + shift, normed, inverse)


def norm_back(grad_out, gain, normed, inverse):
    scaled = grad_out * gain
    return inverse * (
        scaled
        - jnp.mean(scaled, -1, keepdims=True)
        - normed * jnp.mean(scaled * normed, -1, keepdims=True)
    )


def project(left, right):
    return jnp.einsum("rtd,de->rte", left, right, preferred_element_type=jnp.float32)


def project_back(left, right):
    return jnp.einsum("rte,de->rtd", left, right, preferred_element_type=jnp.float32)


def head_split(matrix):
    return matrix.reshape(matrix.shape[0], H, HD)


def log_add(first, second):
    larger = jnp.maximum(first, second)
    return larger + jnp.log(jnp.exp(first - larger) + jnp.exp(second - larger))


def fetch_weights(w_query, w_key, w_value, w_out, w_up, w_down, layer_index):
    return (
        lax.all_gather(w_query[layer_index], "rows", axis=0, tiled=True),
        lax.all_gather(w_key[layer_index], "rows", axis=0, tiled=True),
        lax.all_gather(w_value[layer_index], "rows", axis=0, tiled=True),
        lax.all_gather(w_out[layer_index], "rows", axis=0, tiled=True),
        lax.all_gather(w_up[layer_index], "rows", axis=0, tiled=True),
        lax.all_gather(w_down[layer_index], "rows", axis=0, tiled=True),
    )


def masked_scores(query_rows, key_rows, allowed_row):
    scores = jnp.einsum(
        "qhd,khd->hqk",
        head_split(query_rows),
        head_split(key_rows),
        preferred_element_type=jnp.float32,
    )
    return jnp.where(allowed_row[None], scores, MASKED_SCORE)


def score_lse(scores):
    maximum = jnp.max(scores, -1, keepdims=True)
    return (maximum + jnp.log(jnp.sum(jnp.exp(scores - maximum), -1, keepdims=True)))[:, :, 0]


def weighted_values(scores, lse_row, value_rows):
    attend = jnp.exp(scores - lse_row[:, :, None]).astype(jnp.bfloat16)
    result = jnp.einsum(
        "hqk,khd->qhd", attend, head_split(value_rows), preferred_element_type=jnp.float32
    )
    return result.reshape(result.shape[0], value_rows.shape[1])


def forward_layer(
    inputs, allowed, weights, prefix_key, prefix_value, up_bias, gain_pair, shift_pair
):
    query_weight, key_weight, value_weight, out_weight, up_weight, down_weight = weights
    inputs_low = inputs.astype(jnp.bfloat16)
    queries = (SCORE_SCALE * project(inputs_low, query_weight)).astype(jnp.bfloat16)
    keys_local = project(inputs_low, key_weight).astype(jnp.bfloat16)
    values_local = project(inputs_low, value_weight).astype(jnp.bfloat16)
    key_rows = jnp.concatenate([keys_local, prefix_key[None]], 1)
    value_rows = jnp.concatenate([values_local, prefix_value[None]], 1)
    query_set = lax.all_gather(queries, "keys", axis=1, tiled=True)
    key_set, value_set = (key_rows, value_rows)
    score_list = [masked_scores(query_set[0], key_set[0], allowed[0])]
    local_lse = jnp.stack([score_lse(scores) for scores in score_list])
    row_lse = combined_all(local_lse, "keys", log_add)
    partial_outs = jnp.stack([weighted_values(score_list[0], row_lse[0], value_set[0])])
    attended = lax.psum_scatter(partial_outs, "keys", scatter_dimension=1, tiled=True)
    middle, normed_one, inverse_one = layer_norm(
        inputs + project(attended.astype(jnp.bfloat16), out_weight), gain_pair[0], shift_pair[0]
    )
    pre_gelu = project(middle.astype(jnp.bfloat16), up_weight) + up_bias
    activated = jax.nn.gelu(pre_gelu, approximate=False).astype(jnp.bfloat16)
    output, normed_two, inverse_two = layer_norm(
        middle + project(activated, down_weight), gain_pair[1], shift_pair[1]
    )
    saved_state = (
        query_set,
        key_set,
        value_set,
        row_lse,
        normed_one,
        inverse_one,
        pre_gelu,
        normed_two,
        inverse_two,
    )
    return (output, saved_state)


def attention_back(query_set, key_set, value_set, grad_set, lse_set, allowed):
    model_width = query_set.shape[2]
    row_index = 0
    scores = masked_scores(query_set[row_index], key_set[row_index], allowed[row_index])
    attend = jnp.exp(scores - lse_set[row_index][:, :, None])
    grad_attend = jnp.einsum(
        "qhd,khd->hqk",
        head_split(grad_set[row_index]),
        head_split(value_set[row_index]),
        preferred_element_type=jnp.float32,
    )
    attend_list = [attend]
    grad_attend_list = [grad_attend]
    dot_list = [jnp.sum(attend * grad_attend, -1)]
    dots = jnp.stack(dot_list)
    dots = lax.psum(dots, "keys")
    row_index = 0
    attend = attend_list[row_index]
    grad_heads = head_split(grad_set[row_index])
    grad_values = jnp.einsum(
        "hqk,qhd->khd", attend.astype(jnp.bfloat16), grad_heads, preferred_element_type=jnp.float32
    )
    grad_scores = (attend * (grad_attend_list[row_index] - dots[row_index][:, :, None])).astype(
        jnp.bfloat16
    )
    query_part = jnp.einsum(
        "hqk,khd->qhd",
        grad_scores,
        head_split(key_set[row_index]),
        preferred_element_type=jnp.float32,
    )
    grad_keys = jnp.einsum(
        "hqk,qhd->khd",
        grad_scores,
        head_split(query_set[row_index]),
        preferred_element_type=jnp.float32,
    )
    query_list = [query_part.reshape(query_part.shape[0], model_width)]
    key_list = [grad_keys.reshape(grad_keys.shape[0], model_width)]
    value_list = [grad_values.reshape(grad_values.shape[0], model_width)]
    return (jnp.stack(query_list), jnp.stack(key_list), jnp.stack(value_list))


def backward_layer(gradient, saved_state, allowed, weights, gain_pair):
    query_weight, key_weight, value_weight, out_weight, up_weight, down_weight = weights
    (
        query_set,
        key_set,
        value_set,
        row_lse,
        normed_one,
        inverse_one,
        pre_gelu,
        normed_two,
        inverse_two,
    ) = saved_state
    rows_dev, local_len, model_width = gradient.shape
    grad_two = norm_back(gradient, gain_pair[1], normed_two, inverse_two)
    grad_hidden = project_back(grad_two.astype(jnp.bfloat16), down_weight)
    gelu_value, gelu_back = jax.vjp(partial(jax.nn.gelu, approximate=False), pre_gelu)
    grad_pre = gelu_back(grad_hidden)[0].astype(jnp.bfloat16)
    grad_one = norm_back(
        grad_two + project_back(grad_pre, up_weight), gain_pair[0], normed_one, inverse_one
    )
    grad_att = project_back(grad_one.astype(jnp.bfloat16), out_weight).astype(jnp.bfloat16)
    grad_all = lax.all_gather(grad_att, "keys", axis=1, tiled=True)
    query_terms, key_grads, value_grads = attention_back(
        query_set, key_set, value_set, grad_all, row_lse, allowed
    )
    grad_queries = lax.psum_scatter(
        query_terms.astype(jnp.bfloat16), "keys", scatter_dimension=1, tiled=True
    )
    grad_input = grad_one + SCORE_SCALE * project_back(grad_queries, query_weight)
    grad_input = grad_input + project_back(
        key_grads[:, :local_len].astype(jnp.bfloat16), key_weight
    )
    grad_input = grad_input + project_back(
        value_grads[:, :local_len].astype(jnp.bfloat16), value_weight
    )
    return (
        grad_input,
        jnp.sum(key_grads[:, local_len:], 0),
        jnp.sum(value_grads[:, local_len:], 0),
    )


def body(
    activations,
    segments,
    prefix_keys,
    prefix_values,
    w_query,
    w_key,
    w_value,
    w_out,
    w_up,
    ff_bias,
    w_down,
    ln_gain,
    ln_bias,
    cotangent,
):
    rows_dev, local_len, model_width = activations.shape
    key_start = lax.axis_index("keys") * local_len
    own_segments = lax.dynamic_slice_in_dim(segments, key_start, local_len, 1)
    prefix_count = prefix_keys.shape[1]
    allowed = jnp.concatenate(
        [
            segments[:, :, None] == own_segments[:, None, :],
            jnp.ones((rows_dev, segments.shape[1], prefix_count), dtype=bool),
        ],
        2,
    )
    inputs = activations.astype(jnp.float32)
    stored = []
    saved_list = []
    fetched = []
    for layer_index in range(LAYERS):
        weights = fetch_weights(w_query, w_key, w_value, w_out, w_up, w_down, layer_index)
        stored.append(inputs)
        inputs, saved_state = forward_layer(
            inputs,
            allowed,
            weights,
            prefix_keys[layer_index],
            prefix_values[layer_index],
            ff_bias[layer_index],
            ln_gain[layer_index],
            ln_bias[layer_index],
        )
        saved_list.append(saved_state)
        fetched.append(weights)
    result = inputs.astype(jnp.bfloat16)
    gradient = cotangent.astype(jnp.float32)
    key_parts = [None] * LAYERS
    value_parts = [None] * LAYERS
    for layer_index in range(LAYERS - 1, -1, -1):
        weights = fetch_weights(w_query, w_key, w_value, w_out, w_up, w_down, layer_index)
        unused_output, saved_state = forward_layer(
            stored[layer_index],
            allowed,
            weights,
            prefix_keys[layer_index],
            prefix_values[layer_index],
            ff_bias[layer_index],
            ln_gain[layer_index],
            ln_bias[layer_index],
        )
        gradient, key_part, value_part = backward_layer(
            gradient, saved_state, allowed, weights, ln_gain[layer_index]
        )
        key_part, value_part = (
            lax.psum(key_part.astype(jnp.bfloat16), "rows").astype(jnp.float32),
            lax.psum(value_part.astype(jnp.bfloat16), "rows").astype(jnp.float32),
        )
        key_parts[layer_index] = key_part
        value_parts[layer_index] = value_part
    key_total = jnp.stack(key_parts)
    value_total = jnp.stack(value_parts)
    return (result, gradient, key_total, value_total)


def solution(mesh):
    placed = (
        P("rows", "keys", None),
        P("rows", None),
        P(None, "keys", None),
        P(None, "keys", None),
        P(None, "rows", None),
        P(None, "rows", None),
        P(None, "rows", None),
        P(None, "rows", None),
        P(None, "rows", None),
        P(),
        P(None, "rows", None),
        P(),
        P(),
        P("rows", "keys", None),
    )
    return jax.shard_map(
        body,
        mesh=mesh,
        in_specs=placed,
        out_specs=(
            P("rows", "keys", None),
            P("rows", "keys", None),
            P(None, "keys", None),
            P(None, "keys", None),
        ),
        check_vma=False,
    )
```

profile of v0, /device:TPU:0, one launch (start us, length us, event | category | flops | bytes accessed | tf_op | source)
XLA Modules:
  0.0 1702.9 jit_solution(11375815969004791397)
XLA Ops:
  13.3 49.5 %all-gather.37.cloned.1.call-done = bf16[1,1024,1024]{2,1,0:T(8,128)(2,1)} async-done(((bf16[1,128,1024]{2,1,0:T(8,128)(2,1)}), bf16[1,1024,1024]{2,1,0:T(8,128)(2,1)}) %all-gather.37.cloned.1.call-update) | async-done | bytes 2097168 | tf_op jit(solution)/shard_map/all_gather | solution.py:64
  62.7 3.0 fusion.182
  68.3 3.0 fusion.301
  78.7 33.9 %all-gather.41.cloned.1.call-done = bf16[1,1024,1024]{2,1,0:T(8,128)(2,1)} async-done(((bf16[1,128,1024]{2,1,0:T(8,128)(2,1)}), bf16[1,1024,1024]{2,1,0:T(8,128)(2,1)}) %all-gather.41.cloned.1.call-update) | async-done | bytes 2097168 | tf_op jit(solution)/shard_map/all_gather | solution.py:65
  112.7 2.2 fusion.188
  115.1 47.5 %all-gather.35.cloned.1.call-done = bf16[1,1024,1024]{2,1,0:T(8,128)(2,1)} async-done(((bf16[1,128,1024]{2,1,0:T(8,128)(2,1)}), bf16[1,1024,1024]{2,1,0:T(8,128)(2,1)}) %all-gather.35.cloned.1.call-update) | async-done | bytes 2097168 | tf_op jit(solution)/shard_map/all_gather | solution.py:66
  162.6 2.2 fusion.185
  165.1 19.2 %all-gather.39.cloned.1.call-done = bf16[896,1024]{1,0:T(8,128)(2,1)} async-done(((bf16[224,1024]{1,0:T(8,128)(2,1)}), bf16[896,1024]{1,0:T(8,128)(2,1)}) %all-gather.39.cloned.1.call-update) | async-done | bytes 1835024 | tf_op jit(solution)/shard_map/all_gather | solution.py:106
  184.2 3.1 copy.74
  187.3 8.2 select_reduce_fusion.1
  195.6 7.3 exponential_reduce_fusion.1
  202.9 5.9 all-gather.4
  209.0 10.1 fusion.212
  219.2 9.8 copy.77
  229.0 496.4 %all-reduce.9 = bf16[1,896,1024]{2,0,1:T(2,128)(2,1)} all-reduce(f32[1,896,1024]{2,0,1:T(1,128)} %copy.77), channel_id=20, replica_groups=mesh['rows'=8,'keys'=4] {'keys'}, use_global_device_ids=true, to_apply=%region_4.5.clone | all-reduce | flops 917504 | bytes 5505024
  725.4 2.1 constant_dynamic-slice_fusion.1
  727.6 2.3 fusion.311
  730.2 7.3 fusion.30
  737.5 12.6 fusion.312
  750.5 3.1 fusion.179
  757.1 2.3 fusion.194
  759.7 2.6 fusion.197
  762.5 13.3 all-gather.53.cloned.1.call-done
  775.8 3.1 copy.81
  778.8 8.1 select_reduce_fusion
  787.0 7.3 exponential_reduce_fusion
  794.3 5.7 all-gather.12
  800.2 10.1 fusion.209
  810.3 9.8 copy.84
  820.1 496.6 %all-reduce.10 = bf16[1,896,1024]{2,0,1:T(2,128)(2,1)} all-reduce(f32[1,896,1024]{2,0,1:T(1,128)} %copy.84), channel_id=21, replica_groups=mesh['rows'=8,'keys'=4] {'keys'}, use_global_device_ids=true, to_apply=%region_13.14.clone | all-reduce | flops 917504 | bytes 5505024
  1316.7 3.0 constant_dynamic-slice_fusion
  1319.7 2.9 fusion.313
  1322.9 7.4 fusion.33
  1330.3 12.7 fusion.314
  1345.0 22.8 %fusion.299 = (f32[224]{0:T(256)S(1)}, f32[224]{0:T(256)S(1)}, f32[1,224,1024]{2,1,0:T(8,128)}) fusion(f32[224]{0:T(256)S(1)} %add_rsqrt_fusion.1, f32[1,224,1024]{2,1,0:T(8,128)S(1)} %get-tuple-element.258, f32[224]{0:T(256)S(1)} %broadcast_multiply_fusion.9, f32[1024]{0:T(1024)S(1)} %bitcast.486, ...), kind=kOutput, calls=%fused_computation.288 | convolution fusion | flops 3829661184 | bytes 23673856 | tf_op jit(solution)/shard_map/rte,de->rtd/dot_general | solution.py:50
  1367.8 3.5 fusion.200
  1371.4 22.0 %all-gather.63.cloned.1.call-done = bf16[896,1024]{1,0:T(8,128)(2,1)} async-done(((bf16[224,1024]{1,0:T(8,128)(2,1)}), bf16[896,1024]{1,0:T(8,128)(2,1)}) %all-gather.63.cloned.1.call-update) | async-done | bytes 1835024 | tf_op jit(solution)/shard_map/all_gather | solution.py:200
  1393.4 3.8 copy.86
  1397.3 14.4 multiply_reduce_fusion.1
  1411.7 11.3 psum.42
  1423.0 10.2 multiply_convert_fusion.1
  1433.2 3.3 convolution_convert_fusion.1
  1436.6 9.7 copy.92
  1446.3 4.0 copy.117
  1450.3 8.5 convolution_convert_fusion.4
  1460.6 6.3 convolution_convert_fusion.5
  1466.9 14.4 reduce-scatter.7.cloned.1.call-done
  1485.0 3.1 fusion.161
  1490.1 20.6 %fusion.297 = (f32[224]{0:T(256)S(1)}, f32[224]{0:T(256)S(1)}, f32[1,224,1024]{2,1,0:T(8,128)S(1)}) fusion(f32[224]{0:T(256)S(1)} %add_rsqrt_fusion.3, f32[1,224,1024]{2,1,0:T(8,128)S(1)} %copy-done.5, f32[224]{0:T(256)S(1)} %broadcast_multiply_fusion.11, f32[1024]{0:T(1024)S(1)} %bitcast.483, bf16[1,1024,4096]{2,1,0:T(8,128)(2,1)} %all-gather.45.cloned.1.call-done, ...), kind=kOutput, calls=%fused_computation.286 | convolution fusion | flops 3828743680 | bytes 24128512 | tf_op jit(solution)/shard_map/rte,de->rtd/dot_general | solution.py:50
  1510.8 3.6 fusion.191
  1518.9 16.8 all-gather.65.cloned.1.call-done
  1535.7 3.8 copy.87
  1539.5 14.7 multiply_reduce_fusion
  1554.3 4.4 convolution_convert_fusion.2
  1558.6 11.1 psum.43
  1569.8 10.1 multiply_convert_fusion
  1579.9 2.5 convolution_convert_fusion.3
  1584.5 5.8 convolution_convert_fusion
  1590.4 9.7 copy.94
  1600.1 4.0 copy.116
  1604.1 3.4 fusion.86
  1607.5 48.6 %all-reduce.8.cloned.1.call-done = (bf16[1,16,1024]{2,1,0:T(8,128)(2,1)}, bf16[1,16,1024]{2,1,0:T(8,128)(2,1)}, bf16[1,16,1024]{2,1,0:T(8,128)(2,1)}, bf16[1,16,1024]{2,1,0:T(8,128)(2,1)}) async-done(((bf16[1,16,1024]{2,1,0:T(8,128)(2,1)}, bf16[1,16,1024]{2,1,0:T(8,128)(2,1)}, bf16[1,16,1024]{2,1,0:T(8,128)(2,1)}, bf16[1,16,1024]{2,1,0:T(8,128)(2,1)}), (bf16[1,16,1024]{2,1,0:T(8,128)(2,1)}, ...) | async-done | bytes 131088 | tf_op jit(solution)/shard_map/psum | solution.py:287
  1659.0 28.8 %reduce-scatter.9.cloned.1.call-done = bf16[224,1024]{1,0:T(8,128)(2,1)} async-done(((bf16[896,1024]{1,0:T(8,128)(2,1)}), bf16[224,1024]{1,0:T(8,128)(2,1)}) %reduce-scatter.9.cloned.1.call-update) | async-done | bytes 458768
  1691.3 2.9 fusion.164
  (236 shorter events, 45.2 us)
Async XLA Ops:
  7.2 55.6 %copy-start.36 = (bf16[1,224,1024]{2,1,0:T(8,128)(2,1)S(1)}, bf16[1,224,1024]{2,1,0:T(8,128)(2,1)}, u32[]{:S(2)}) copy-start(bf16[1,224,1024]{2,1,0:T(8,128)(2,1)} %param.18) | copy-start | bytes 1376260
  7.2 55.6 %all-gather.37.cloned.1.call-start = ((), (), s32[]{:S(2)}) async-start(), calls=%async_computation.3 | async-start | bytes 2359296 | tf_op jit(solution)/shard_map/all_gather | solution.py:64
  9.1 56.7 %copy-start.34 = (bf16[2,128,1024]{2,1,0:T(8,128)(2,1)S(1)}, bf16[2,128,1024]{2,1,0:T(8,128)(2,1)}, u32[]{:S(2)}) copy-start(bf16[2,128,1024]{2,1,0:T(8,128)(2,1)} %param.25) | copy-start | bytes 1572868
  9.1 103.5 %all-gather.41.cloned.1.call-start = ((), (), s32[]{:S(2)}) async-start(), calls=%async_computation.5 | async-start | bytes 2359296 | tf_op jit(solution)/shard_map/all_gather | solution.py:65
  11.1 55.6 %copy-start.30 = (bf16[2,128,4096]{2,1,0:T(8,128)(2,1)S(1)}, bf16[2,128,4096]{2,1,0:T(8,128)(2,1)}, u32[]{:S(2)}) copy-start(bf16[2,128,4096]{2,1,0:T(8,128)(2,1)} %param.26) | copy-start | bytes 6291460
  11.1 151.5 %all-gather.35.cloned.1.call-start = ((), (), s32[]{:S(2)}) async-start(), calls=%async_computation.2 | async-start | bytes 2359296 | tf_op jit(solution)/shard_map/all_gather | solution.py:66
  13.2 171.0 %all-gather.39.cloned.1.call-start = ((), (), s32[]{:S(2)}) async-start(), calls=%async_computation.4 | async-start | bytes 2293760 | tf_op jit(solution)/shard_map/all_gather | solution.py:106
  65.8 661.8 %all-gather.43.cloned.1.call-start = ((), (), s32[]{:S(2)}) async-start(), calls=%async_computation.6 | async-start | bytes 2359296 | tf_op jit(solution)/shard_map/all_gather | solution.py:67
  66.7 663.5 %all-gather.45.cloned.1.call-start = ((), (), s32[]{:S(2)}) async-start(), calls=%async_computation.7 | async-start | bytes 9437184 | tf_op jit(solution)/shard_map/all_gather | solution.py:68
  68.2 5.3 copy-start.47
  68.2 5.7 copy-start.39
  68.2 6.5 copy-start.40
  68.2 7.3 copy-start.42
  68.2 8.0 copy-start.43
  68.2 8.6 copy-start.41
  68.2 9.2 copy-start.53
  68.3 669.3 %all-gather.47.cloned.1.call-start = ((), (), s32[]{:S(2)}) async-start(), calls=%async_computation.8 | async-start | bytes 9437184 | tf_op jit(solution)/shard_map/all_gather | solution.py:69
  71.4 679.1 %all-gather.51.cloned.1.call-start = ((), (), s32[]{:S(2)}) async-start(), calls=%async_computation.10 | async-start | bytes 2359296 | tf_op jit(solution)/shard_map/all_gather | solution.py:64
  72.1 685.0 %all-gather.49.cloned.1.call-start = ((), (), s32[]{:S(2)}) async-start(), calls=%async_computation.9 | async-start | bytes 2359296 | tf_op jit(solution)/shard_map/all_gather | solution.py:66
  72.8 686.8 %all-gather.55.cloned.1.call-start = ((), (), s32[]{:S(2)}) async-start(), calls=%async_computation.12 | async-start | bytes 2359296 | tf_op jit(solution)/shard_map/all_gather | solution.py:65
  73.4 702.4 %all-gather.53.cloned.1.call-start = ((), (), s32[]{:S(2)}) async-start(), calls=%async_computation.11 | async-start | bytes 2293760 | tf_op jit(solution)/shard_map/all_gather | solution.py:106
  75.5 133.5 %copy-start.26 = (bf16[1,16,1024]{1,2,0:T(8,128)(2,1)}, bf16[1,16,1024]{1,2,0:T(8,128)(2,1)S(1)}, u32[]{:S(2)}) copy-start(bf16[1,16,1024]{1,2,0:T(8,128)(2,1)S(1)} %copy.73) | copy-start | bytes 98308
  115.1 72.2 %copy-start.11 = (bf16[224,1024]{0,1:T(8,128)(2,1)}, bf16[224,1024]{0,1:T(8,128)(2,1)S(1)}, u32[]{:S(2)}) copy-start(bf16[224,1024]{0,1:T(8,128)(2,1)S(1)} %copy.75) | copy-start | bytes 1376260
  165.1 44.0 %copy-start.8 = (bf16[224,1024]{0,1:T(8,128)(2,1)}, bf16[224,1024]{0,1:T(8,128)(2,1)S(1)}, u32[]{:S(2)}) copy-start(bf16[224,1024]{0,1:T(8,128)(2,1)S(1)} %copy.72) | copy-start | bytes 1376260
  187.3 8.3 copy-start.2
  209.0 10.2 copy-start.15
  229.0 498.6 %copy-start.37 = (bf16[1,224,1024]{2,1,0:T(8,128)(2,1)S(1)}, bf16[1,224,1024]{2,1,0:T(8,128)(2,1)}, u32[]{:S(2)}) copy-start(bf16[1,224,1024]{2,1,0:T(8,128)(2,1)} %param.18) | copy-start | bytes 1376260
  725.4 4.8 copy-start.44
  725.4 4.8 copy-start.48
  725.4 4.8 copy-start.52
  729.9 7.6 copy-start.4
  750.2 9.5 copy-start.6
  750.4 6.5 copy-start.38
  750.4 9.3 copy-start.45
  753.6 566.1 %all-gather.57.cloned.1.call-start = ((), (), s32[]{:S(2)}) async-start(), calls=%async_computation.13 | async-start | bytes 2359296 | tf_op jit(solution)/shard_map/all_gather | solution.py:67
  754.2 568.7 %all-gather.59.cloned.1.call-start = ((), (), s32[]{:S(2)}) async-start(), calls=%async_computation.14 | async-start | bytes 9437184 | tf_op jit(solution)/shard_map/all_gather | solution.py:68
  754.9 575.4 %all-gather.61.cloned.1.call-start = ((), (), s32[]{:S(2)}) async-start(), calls=%async_computation.15 | async-start | bytes 9437184 | tf_op jit(solution)/shard_map/all_gather | solution.py:69
  755.5 637.9 %all-gather.63.cloned.1.call-start = ((), (), s32[]{:S(2)}) async-start(), calls=%async_computation.16 | async-start | bytes 2293760 | tf_op jit(solution)/shard_map/all_gather | solution.py:200
  759.7 40.5 %copy-start.10 = (bf16[224,1024]{0,1:T(8,128)(2,1)}, bf16[224,1024]{0,1:T(8,128)(2,1)S(1)}, u32[]{:S(2)}) copy-start(bf16[224,1024]{0,1:T(8,128)(2,1)S(1)} %copy.79) | copy-start | bytes 1376260
  762.5 24.5 %copy-start.13 = (bf16[224,1024]{0,1:T(8,128)(2,1)}, bf16[224,1024]{0,1:T(8,128)(2,1)S(1)}, u32[]{:S(2)}) copy-start(bf16[224,1024]{0,1:T(8,128)(2,1)S(1)} %copy.82) | copy-start | bytes 1376260
  820.1 499.6 %copy-start.46 = (f32[224]{0:T(256)S(1)}, f32[224]{0:T(256)}, u32[]{:S(2)}) copy-start(f32[224]{0:T(256)} %copy-done.45) | copy-start | bytes 2692
  1316.7 6.2 copy-start.50
  1316.7 6.2 copy-start.51
  1330.3 13.6 copy-start.35
  1371.4 110.0 %reduce-scatter.7.cloned.1.call-start = ((), (), s32[]{:S(2)}) async-start(), calls=%async_computation.18 | async-start | bytes 2293760
  1423.0 10.2 copy-start.14
  1423.0 10.2 copy-start.28
  1450.3 85.4 %all-gather.65.cloned.1.call-start = ((), (), s32[]{:S(2)}) async-start(), calls=%async_computation.17 | async-start | bytes 2293760 | tf_op jit(solution)/shard_map/all_gather | solution.py:200
  1450.3 8.5 copy-start.29
  1482.8 5.3 copy-start.7
  1510.7 4.6 copy-start.19
  1514.4 25.1 %copy-start.9 = (bf16[224,1024]{0,1:T(8,128)(2,1)S(1)}, bf16[224,1024]{0,1:T(8,128)(2,1)}, u32[]{:S(2)}) copy-start(bf16[224,1024]{0,1:T(8,128)(2,1)} %copy-done.8) | copy-start | bytes 1376260
  1514.4 25.1 %copy-start.16 = (f32[1,16,896]{2,1,0:T(8,128)S(1)}, f32[1,16,896]{2,1,0:T(8,128)}, u32[]{:S(2)}) copy-start(f32[1,16,896]{2,1,0:T(8,128)} %copy-done.15) | copy-start | bytes 172036
  1514.4 141.7 %all-reduce.8.cloned.1.call-start = ((), (), s32[]{:S(2)}) async-start(), calls=%async_computation.20 | async-start | bytes 262144 | tf_op jit(solution)/shard_map/psum | solution.py:287
  1516.4 37.8 %slice-start = ((s8[13762560]{0:T(1024)(128)(4,1)}), s8[1179648]{0:T(1024)(128)(4,1)S(1)}, s32[]{:S(2)}) async-start(s8[13762560]{0:T(1024)(128)(4,1)} %bitcast.414), calls=%async_computation.21 | async-start | bytes 2359296
  1539.5 14.7 slice-start.1
  1539.5 14.7 slice-start.2
  1539.5 14.7 slice-start.3
  1569.8 10.1 copy-start.3
  1579.9 4.6 copy-start.12
  1579.9 4.6 copy-start.27
  1582.7 7.7 copy-start.24
  1584.5 103.3 %reduce-scatter.9.cloned.1.call-start = ((), (), s32[]{:S(2)}) async-start(), calls=%async_computation.19 | async-start | bytes 2293760
  1604.1 87.2 %copy-start.20 = (f32[1,224,1024]{2,1,0:T(8,128)S(1)}, f32[1,224,1024]{2,1,0:T(8,128)}, u32[]{:S(2)}) copy-start(f32[1,224,1024]{2,1,0:T(8,128)} %copy-done.19) | copy-start | bytes 2752516
  (13 other events, 34.7 us)
Sparse Core Ops, SparseCore 0:
  10.7 51.9 all-gather.36
  64.9 47.7 all-gather.40
  114.8 47.7 all-gather.34
  164.6 19.5 all-gather.38
  186.8 49.2 all-gather.42
  238.1 123.4 all-gather.44
  363.7 123.1 all-gather.46
  488.9 47.4 all-gather.50
  538.6 47.7 all-gather.48
  588.3 47.7 all-gather.54
  753.7 22.0 all-gather.52
  777.8 49.3 all-gather.56
  829.3 123.3 all-gather.58
  954.7 123.1 all-gather.60
  1371.5 21.8 all-gather.62
  1450.4 30.9 reduce-scatter.6
  1514.5 21.1 all-gather.64
  1584.6 71.4 all-reduce.7
  1658.7 29.0 reduce-scatter.8
where the time goes:
time: 1710 us; the launch traced here: 1700 us
  blocking collectives  1030 us (60%)
  waiting for transfers between devices  298 us (17%)
  matrix products  223 us (13%)
  local copies, waits for them, and re-layouts  97.5 us (6%)
  other arithmetic  40.4 us (2%)
    unnamed x2, blocking collectives  993 us
    dot_general x10, matrix products, project_back(): jnp.einsum('rte,de->rtd', left, right, preferred_element_type=jnp.float32)  65.4 us
    dot_general x12, matrix products, project(): jnp.einsum('rtd,de->rte', left, right, preferred_element_type=jnp.float32)  60.6 us
    all_gather x2, waiting for transfers between devices, fetch_weights(): lax.all_gather(w_query[layer_index], 'rows', axis=0, tiled=True)  49.5 us
    psum x1, waiting for transfers between devices, body(): lax.psum(key_part.astype(jnp.bfloat16), 'rows').astype(jnp.float32)  48.6 us
    all_gather x2, waiting for transfers between devices, fetch_weights(): lax.all_gather(w_value[layer_index], 'rows', axis=0, tiled=True)  47.5 us
    unnamed x21, waiting for transfers between devices  47.1 us
    unnamed x131, local copies, waits for them, and re-layouts  45.4 us
  transfers between devices with their start and end apart: 19, of which 10 were waited for; matrix products, arithmetic and copies ran while one was open for 11% of the time, Pallas kernels for 0%

commit v1 on v0

v1 whole, which is shorter than its diff:
```python
from functools import partial

import jax
import jax.numpy as jnp
import numpy as np
from jax import lax
from jax.experimental import pallas as pl
from jax.experimental.pallas import tpu as pltpu
from jax.sharding import PartitionSpec as P

H = 16
HD = 64
LAYERS = 2
PAIRS = H // 2
EDGE = 32
LANES = 256
NORM_EPSILON = 1e-05
MASKED_SCORE = -1000000000.0
SCORE_SCALE = 0.125
F32 = jnp.float32
BF16 = jnp.bfloat16
MIB = 1 << 20


def nn(a, b):
    return lax.dot_general(a, b, (((1,), (0,)), ((), ())), preferred_element_type=F32)


def nt(a, b):
    return lax.dot_general(a, b, (((1,), (1,)), ((), ())), preferred_element_type=F32)


def ds(start, size):
    return pl.ds(pl.multiple_of(start, size), size)


def layer_norm(hidden, gain, shift):
    centered = hidden - jnp.mean(hidden, -1, keepdims=True)
    inverse = lax.rsqrt(jnp.mean(centered * centered, -1, keepdims=True) + NORM_EPSILON)
    normed = centered * inverse
    return normed * gain + shift, normed, inverse


def norm_back(grad_out, gain, normed, inverse):
    scaled = grad_out * gain
    return inverse * (
        scaled
        - jnp.mean(scaled, -1, keepdims=True)
        - normed * jnp.mean(scaled * normed, -1, keepdims=True)
    )


def start_loads(table, pieces, weights, sems):
    at = 0
    for piece in pieces:
        blocks, rows, width = piece.shape

        def start(i, carry, piece=piece, at=at, rows=rows, width=width):
            row = table[at + i]

            @pl.when(row >= 0)
            def _():
                pltpu.make_async_copy(
                    piece.at[i], weights.at[ds(row, rows)], sems.at[row // width]
                ).start()

            return carry

        lax.fori_loop(0, blocks, start, 0)
        at += blocks


def wait_load(weights, sems, index):
    width = weights.shape[1]
    part = weights.at[pl.ds(index * width, width)]
    pltpu.make_async_copy(part, part, sems.at[index]).wait()


def pair_blocks(half):
    zero = jnp.zeros((HD, LANES), half.dtype)
    return jnp.concatenate(
        [
            jnp.concatenate([half[:HD], zero], 1),
            jnp.concatenate([zero, half[HD:]], 1),
        ],
        0,
    )


def attention_kernel(count, *refs):
    (table, own, near, across, edge, residual, bias, prefix_k, prefix_v, gain, shift) = refs[:11]
    pieces = refs[11 : 11 + count]
    (middle, normed, inverse, query_t, value8, key_t, attend, heads_t) = refs[11 + count : 19 + count]
    (weights, window, key8, value_t, scores, sems) = refs[19 + count :]
    tokens, width = own.shape
    span = window.shape[0]
    keys = key8.shape[1]
    start_loads(table, pieces, weights, sems)
    window[pl.ds(0, tokens)] = own[...]
    window[pl.ds(tokens, tokens)] = near[...]
    window[pl.ds(2 * tokens, tokens)] = across[...]
    window[pl.ds(3 * tokens, EDGE)] = edge[...]
    pad = jnp.zeros((LANES - tokens, 256), BF16)
    for index in range(3):
        wait_load(weights, sems, index)

    def tile(j, carry):
        columns = ds(j * 256, 256)
        query = (SCORE_SCALE * nn(own[...], weights[pl.ds(0, width), columns])).astype(BF16)
        query_t[columns, :] = jnp.concatenate([query, pad], 0).T
        for row, prefix, split, turned in ((width, prefix_k, key8, key_t), (2 * width, prefix_v, value8, value_t)):
            local = nn(window[...], weights[pl.ds(row, width), columns]).astype(BF16)
            whole = jnp.concatenate([local, prefix[:, columns]], 0)
            split[2 * j] = whole[:, :128]
            split[2 * j + 1] = whole[:, 128:]
            turned[columns, :] = whole.T
        return carry

    lax.fori_loop(0, width // 256, tile, 0)
    wide = jnp.zeros((1, 2 * LANES), F32)
    step = 128

    def pair(p, carry):
        blocks = pair_blocks(query_t[ds(p * 128, 128), :])
        top = wide + 2 * MASKED_SCORE
        for c in range(0, keys, step):
            part = nn(key8[p, pl.ds(c, step), :], blocks)
            mask = bias[pl.ds(c, step), :]
            part = part + jnp.concatenate([mask, mask], 1)
            scores[pl.ds(c, step), :] = part
            top = jnp.maximum(top, jnp.max(part, 0, keepdims=True))
        total = wide
        for c in range(0, keys, step):
            part = jnp.exp(scores[pl.ds(c, step), :] - top)
            scores[pl.ds(c, step), :] = part
            total = total + jnp.sum(part, 0, keepdims=True)
        scale = 1.0 / total
        for c in range(0, keys, step):
            attend[p, pl.ds(c, step), :] = (scores[pl.ds(c, step), :] * scale).astype(BF16)
        for half in range(2):
            rows = pl.ds(pl.multiple_of(p * 128 + half * HD, HD), HD)
            heads_t[rows, :] = nn(value_t[rows, :], attend[p, :, pl.ds(half * LANES, LANES)])
        return carry

    lax.fori_loop(0, PAIRS, pair, 0)
    wait_load(weights, sems, 3)
    heads = heads_t[...].astype(BF16).T[:tokens]

    def out(j, carry):
        columns = ds(j * 256, 256)
        middle[:, columns] = residual[:, columns] + nn(heads, weights[pl.ds(3 * width, width), columns])
        return carry

    lax.fori_loop(0, width // 256, out, 0)
    result, n, r = layer_norm(middle[...], gain[...], shift[...])
    middle[...] = result
    normed[...] = n
    inverse[...] = r


def forward_kernel(count, *refs):
    (table, middle, up_bias, gain, shift) = refs[:5]
    pieces = refs[5 : 5 + count]
    (output, low, normed, inverse, slope) = refs[5 + count : 10 + count]
    (weights, middle_low, hidden, sems) = refs[10 + count :]
    tokens, width = middle.shape
    wide = up_bias.shape[1]
    start_loads(table, pieces, weights, sems)
    middle_low[...] = middle[...].astype(BF16)
    for block in range(wide // width):
        wait_load(weights, sems, block)

        def tile(j, carry, block=block):
            columns = ds(j * 256, 256)
            place = ds(block * width + j * 256, 256)
            u = nn(middle_low[...], weights[pl.ds(block * width, width), columns]) + up_bias[:, place]
            part = 0.5 + 0.5 * lax.erf(u * (0.5**0.5))
            hidden[:, place] = (u * part).astype(BF16)
            slope[:, place] = (part + u * (jnp.exp(-0.5 * u * u) * ((2 * np.pi) ** -0.5))).astype(BF16)
            return carry

        lax.fori_loop(0, width // 256, tile, 0)
    for block in range(wide // width):
        wait_load(weights, sems, wide // width + block)

    def down(j, carry):
        columns = ds(j * 256, 256)
        output[:, columns] = middle[:, columns] + nn(hidden[...], weights[pl.ds(wide, wide), columns])
        return carry

    lax.fori_loop(0, width // 256, down, 0)
    result, n, r = layer_norm(output[...], gain[...], shift[...])
    output[...] = result
    low[...] = result.astype(BF16)
    normed[...] = n
    inverse[...] = r


def forward_back_kernel(count, *refs):
    (table, grad, normed_two, inverse_two, gain_two, slope, normed_one, inverse_one, gain_one) = refs[:9]
    pieces = refs[9 : 9 + count]
    (grad_one, heads_grad) = refs[9 + count : 11 + count]
    (weights, low, hidden, sems) = refs[11 + count :]
    tokens, width = grad.shape
    wide = slope.shape[1]
    many = wide // width
    start_loads(table, pieces, weights, sems)
    grad_two = norm_back(grad[...], gain_two[...], normed_two[...], inverse_two[...])
    grad_one[...] = grad_two
    low[pl.ds(0, tokens), :] = grad_two.astype(BF16)
    low[pl.ds(tokens, LANES - tokens), :] = jnp.zeros((LANES - tokens, width), BF16)
    for block in range(many):
        wait_load(weights, sems, many + block)

        def tile(j, carry, block=block):
            place = ds(block * width + j * 256, 256)
            back = nt(low[pl.ds(0, tokens), :], weights[pl.ds(pl.multiple_of(wide + block * width + j * 256, 256), 256), :])
            hidden[:, place] = (back * slope[:, place].astype(F32)).astype(BF16)
            return carry

        lax.fori_loop(0, width // 256, tile, 0)
    for block in range(many):
        wait_load(weights, sems, block)

    def up(j, carry):
        columns = ds(j * 256, 256)
        total = grad_one[:, columns]
        for block in range(many):
            rows = pl.ds(pl.multiple_of(block * width + j * 256, 256), 256)
            total = total + nt(hidden[:, pl.ds(block * width, width)], weights[rows, :])
        grad_one[:, columns] = total
        return carry

    lax.fori_loop(0, width // 256, up, 0)
    back = norm_back(grad_one[...], gain_one[...], normed_one[...], inverse_one[...])
    grad_one[...] = back
    low[pl.ds(0, tokens), :] = back.astype(BF16)
    wait_load(weights, sems, 2 * many)

    def out(j, carry):
        rows = ds(j * 256, 256)
        place = pl.ds(pl.multiple_of(2 * wide + j * 256, 256), 256)
        heads_grad[rows, :] = nt(weights[place, :], low[...]).astype(BF16)
        return carry

    lax.fori_loop(0, width // 256, out, 0)


def attention_back_kernel(count, *refs):
    (table, heads_grad, heads_t, query_t, value8, key_t, attend_hbm) = refs[:7]
    pieces = refs[7 : 7 + count]
    (query_grad, key_own, value_own, halo, prefix_grad) = refs[7 + count : 12 + count]
    (weights, attend, key_grad, value_grad, query_grad_t, steps, sems, attend_sems) = refs[12 + count :]
    tokens, width = query_grad.shape
    keys = attend.shape[1]
    prefix = prefix_grad.shape[1]
    span = keys - prefix
    for p in range(PAIRS):
        pltpu.make_async_copy(attend_hbm.at[p], attend.at[p], attend_sems.at[p]).start()
    start_loads(table, pieces, weights, sems)
    step = 128

    def pair(p, carry):
        pltpu.make_async_copy(attend_hbm.at[p], attend.at[p], attend_sems.at[p]).wait()
        rows = ds(p * 128, 128)
        grad_t = heads_grad[rows, :]
        product = grad_t.astype(F32) * heads_t[rows, :]
        dots = jnp.concatenate(
            [jnp.sum(product[:HD], 0, keepdims=True), jnp.sum(product[HD:], 0, keepdims=True)], 1
        )
        blocks = pair_blocks(grad_t)
        for c in range(0, keys, step):
            part = nn(value8[p, pl.ds(c, step), :], blocks) - dots
            steps[pl.ds(c, step), :] = (attend[p, pl.ds(c, step), :].astype(F32) * part).astype(BF16)
        columns = ds(p * 128, 128)
        grad_v = nt(attend[p], blocks)
        value_grad[:, columns] = grad_v.astype(BF16)
        prefix_grad[1, :, columns] = grad_v[span:]
        grad_k = nt(steps[...], pair_blocks(query_t[rows, :]))
        key_grad[:, columns] = grad_k.astype(BF16)
        prefix_grad[0, :, columns] = grad_k[span:]
        for half in range(2):
            place = pl.ds(pl.multiple_of(p * 128 + half * HD, HD), HD)
            query_grad_t[place, :] = nn(key_t[place, :], steps[:, pl.ds(half * LANES, LANES)]).astype(BF16)
        return carry

    lax.fori_loop(0, PAIRS, pair, 0)
    query_grad[...] = query_grad_t[...].T[:tokens]
    key_own[...] = key_grad[pl.ds(0, tokens), :]
    value_own[...] = value_grad[pl.ds(0, tokens), :]
    wait_load(weights, sems, 0)
    wait_load(weights, sems, 1)

    def outer(j, carry):
        columns = ds(j * 256, 256)
        place = pl.ds(pl.multiple_of(width + j * 256, 256), 256)
        halo[:, columns] = (
            nt(key_grad[pl.ds(tokens, span - tokens), :], weights[columns, :])
            + nt(value_grad[pl.ds(tokens, span - tokens), :], weights[place, :])
        ).astype(BF16)
        return carry

    lax.fori_loop(0, width // 256, outer, 0)


def input_back_kernel(count, *refs):
    (table, grad_one, query_grad, key_own, value_own) = refs[:5]
    pieces = refs[5 : 5 + count]
    grad_input = refs[5 + count]
    (weights, sems) = refs[6 + count :]
    width = grad_one.shape[1]
    start_loads(table, pieces, weights, sems)
    for index in range(3):
        wait_load(weights, sems, index)

    def tile(j, carry):
        columns = ds(j * 256, 256)
        rows = [pl.ds(pl.multiple_of(i * width + j * 256, 256), 256) for i in range(3)]
        grad_input[:, columns] = (
            grad_one[:, columns]
            + SCORE_SCALE * nt(query_grad[...], weights[rows[0], :])
            + nt(key_own[...], weights[rows[1], :])
            + nt(value_own[...], weights[rows[2], :])
        )
        return carry

    lax.fori_loop(0, width // 256, tile, 0)


VMEM = pl.BlockSpec(memory_space=pltpu.VMEM)
SMEM = pl.BlockSpec(memory_space=pltpu.SMEM)
ANY = pl.BlockSpec(memory_space=pl.ANY)


def call(kernel, table, operands, kept, pieces, outs, scratch, limit, flops, any_outs=()):
    moved = sum(x.size * x.dtype.itemsize for x in pieces) + sum(x.size * x.dtype.itemsize for x in operands)
    return pl.pallas_call(
        partial(kernel, len(pieces)),
        out_shape=outs,
        in_specs=[SMEM] + [VMEM] * len(operands) + [ANY] * (len(kept) + len(pieces)),
        out_specs=[ANY if i in any_outs else VMEM for i in range(len(outs))],
        scratch_shapes=scratch,
        compiler_params=pltpu.CompilerParams(vmem_limit_bytes=limit * MIB),
        cost_estimate=pl.CostEstimate(flops=flops, bytes_accessed=moved, transcendentals=0),
    )(table, *operands, *kept, *pieces)


def shape(*sizes, dtype=BF16):
    return jax.ShapeDtypeStruct(sizes, dtype)


def attention_forward(inputs, inputs_low, around, bias, prefix_k, prefix_v, gain, shift, table, pieces):
    tokens, width = inputs.shape
    keys = bias.shape[0]
    span = keys - prefix_k.shape[0]
    return call(
        attention_kernel,
        table,
        [inputs_low, *around, inputs, bias, prefix_k, prefix_v, gain, shift],
        [],
        pieces,
        [
            shape(tokens, width, dtype=F32),
            shape(tokens, width, dtype=F32),
            shape(tokens, 1, dtype=F32),
            shape(width, LANES),
            shape(PAIRS, keys, 128),
            shape(width, keys),
            shape(PAIRS, keys, 2 * LANES),
            shape(width, LANES, dtype=F32),
        ],
        [
            pltpu.VMEM((4 * width, width), BF16),
            pltpu.VMEM((span, width), BF16),
            pltpu.VMEM((PAIRS, keys, 128), BF16),
            pltpu.VMEM((width, keys), BF16),
            pltpu.VMEM((keys, 2 * LANES), F32),
            pltpu.SemaphoreType.DMA((4,)),
        ],
        40,
        2 * tokens * width * width * 8,
    )


def feed_forward(middle, up_bias, gain, shift, table, pieces):
    tokens, width = middle.shape
    wide = up_bias.shape[1]
    many = wide // width
    return call(
        forward_kernel,
        table,
        [middle, up_bias, gain, shift],
        [],
        pieces,
        [
            shape(tokens, width, dtype=F32),
            shape(tokens, width),
            shape(tokens, width, dtype=F32),
            shape(tokens, 1, dtype=F32),
            shape(tokens, wide),
        ],
        [
            pltpu.VMEM((2 * wide, width), BF16),
            pltpu.VMEM((tokens, width), BF16),
            pltpu.VMEM((tokens, wide), BF16),
            pltpu.SemaphoreType.DMA((2 * many,)),
        ],
        40,
        4 * tokens * width * wide,
    )


def feed_back(grad, saved_two, gain_two, slope, saved_one, gain_one, table, pieces):
    tokens, width = grad.shape
    wide = slope.shape[1]
    many = wide // width
    return call(
        forward_back_kernel,
        table,
        [grad, *saved_two, gain_two, slope, *saved_one, gain_one],
        [],
        pieces,
        [shape(tokens, width, dtype=F32), shape(width, LANES)],
        [
            pltpu.VMEM((2 * wide + width, width), BF16),
            pltpu.VMEM((LANES, width), BF16),
            pltpu.VMEM((tokens, wide), BF16),
            pltpu.SemaphoreType.DMA((2 * many + 1,)),
        ],
        40,
        4 * tokens * width * wide + 2 * tokens * width * width,
    )


def attention_back(heads_grad, heads_t, query_t, value8, key_t, attend, tokens, prefix, table, pieces):
    width = heads_grad.shape[0]
    keys = attend.shape[1]
    span = keys - prefix
    return call(
        attention_back_kernel,
        table,
        [heads_grad, heads_t, query_t, value8, key_t],
        [attend],
        pieces,
        [
            shape(tokens, width),
            shape(tokens, width),
            shape(tokens, width),
            shape(span - tokens, width),
            shape(2, prefix, width, dtype=F32),
        ],
        [
            pltpu.VMEM((2 * width, width), BF16),
            pltpu.VMEM(attend.shape, BF16),
            pltpu.VMEM((keys, width), BF16),
            pltpu.VMEM((keys, width), BF16),
            pltpu.VMEM((width, LANES), BF16),
            pltpu.VMEM((keys, 2 * LANES), BF16),
            pltpu.SemaphoreType.DMA((2,)),
            pltpu.SemaphoreType.DMA((PAIRS,)),
        ],
        40,
        2 * tokens * width * keys * 8,
    )


def input_back(grad_one, query_grad, key_own, value_own, table, pieces):
    tokens, width = grad_one.shape
    return call(
        input_back_kernel,
        table,
        [grad_one, query_grad, key_own, value_own],
        [],
        pieces,
        [shape(tokens, width, dtype=F32)],
        [pltpu.VMEM((3 * width, width), BF16), pltpu.SemaphoreType.DMA((3,))],
        30,
        6 * tokens * width * width,
    )[0]


def xor_pairs(count, bit):
    return [(i, i ^ bit) for i in range(count)]


def body(
    activations,
    segments,
    prefix_keys,
    prefix_values,
    w_query,
    w_key,
    w_value,
    w_out,
    w_up,
    ff_bias,
    w_down,
    ln_gain,
    ln_bias,
    cotangent,
):
    _, tokens, width = activations.shape
    wide = w_up.shape[2]
    ratio = wide // width
    places = lax.axis_size("keys")
    parts = lax.axis_size("rows")
    rows = width // parts
    place = lax.axis_index("keys")
    prefix = prefix_keys.shape[1] * places
    first_half = place < places // 2

    def blocks_of(layer):
        up = [w_up[layer][:, i * width : (i + 1) * width] for i in range(ratio)]
        down = [w_down[layer][i * rows : (i + 1) * rows] for i in range(ratio)]
        return (
            jnp.stack([w_query[layer], w_key[layer], w_value[layer], w_out[layer]]),
            jnp.stack(up + down),
        )

    def gather(blocks):
        share = blocks.shape[0] // places
        own = lax.dynamic_slice_in_dim(blocks, place * share, share, 0)
        return [lax.all_gather(own, ("rows", "keys"), axis=0, tiled=True)]

    packs = [blocks_of(layer) for layer in range(LAYERS)]
    groups = [[gather(part) for part in pack] for pack in packs]

    owner = np.repeat(np.arange(parts), 4)
    kind = np.tile(np.arange(4), parts)
    attention_rows = kind * width + owner * rows
    owner = np.repeat(np.arange(parts), 2 * ratio)
    part = np.tile(np.arange(2 * ratio), parts)
    feed_rows = np.where(
        part < ratio,
        part * width + owner * rows,
        wide + owner * rows * ratio + (part - ratio) * rows,
    )

    def only(*kinds):
        table = np.full(4 * parts, -1)
        for i, which in enumerate(kinds):
            table = np.where(kind == which, attention_rows + (i - which) * width, table)
        return table

    def as_table(values):
        return jnp.asarray(values, jnp.int32)

    def exchange(low):
        near = lax.ppermute(low, "keys", xor_pairs(places, 1))
        across = lax.ppermute(low, "keys", [(1, 2), (2, 1)])
        edge = lax.ppermute(
            jnp.where(first_half, low[tokens - EDGE :], low[:EDGE]), "keys", xor_pairs(places, 2)
        )
        return near, across, edge

    line = segments[0]

    def ids(where, start, size):
        return lax.dynamic_slice_in_dim(line, where * tokens + start, size, 0)

    own_ids = ids(place, 0, tokens)
    across_ids = jnp.where(
        (place == 1) | (place == 2), ids(jnp.clip(3 - place, 0, places - 1), 0, tokens), -1
    )
    edge_ids = ids(place ^ 2, jnp.where(first_half, 0, tokens - EDGE), EDGE)
    key_ids = jnp.concatenate([own_ids, ids(place ^ 1, 0, tokens), across_ids, edge_ids])
    allowed = jnp.concatenate([key_ids[:, None] == own_ids[None, :], jnp.ones((prefix, tokens), bool)], 0)
    bias = jnp.pad(jnp.where(allowed, 0.0, MASKED_SCORE).astype(F32), ((0, 0), (0, LANES - tokens)))

    prefixes = lax.all_gather(jnp.stack([prefix_keys, prefix_values]), "keys", axis=2, tiled=True)

    low = activations[0]
    hidden = low.astype(F32)
    saved = []
    for layer in range(LAYERS):
        gains, shifts = ln_gain[layer][:, None], ln_bias[layer][:, None]
        around = exchange(low)
        middle, normed_one, inverse_one, query_t, value8, key_t, attend, heads_t = attention_forward(
            hidden,
            low,
            around,
            bias,
            prefixes[0, layer],
            prefixes[1, layer],
            gains[0],
            shifts[0],
            as_table(attention_rows),
            groups[layer][0],
        )
        hidden, low, normed_two, inverse_two, slope = feed_forward(
            middle, ff_bias[layer][None], gains[1], shifts[1], as_table(feed_rows), groups[layer][1]
        )
        saved.append(
            ((normed_one, inverse_one), (normed_two, inverse_two), slope, heads_t, query_t, value8, key_t, attend)
        )
    result = low

    gradient = cotangent[0].astype(F32)
    prefix_parts = [None] * LAYERS
    for layer in range(LAYERS - 1, -1, -1):
        saved_one, saved_two, slope, heads_t, query_t, value8, key_t, attend = saved[layer]
        gains = ln_gain[layer][:, None]
        grad_one, heads_grad = feed_back(
            gradient,
            saved_two,
            gains[1],
            slope,
            saved_one,
            gains[0],
            as_table(np.concatenate([feed_rows, only(3) + 2 * wide * (only(3) >= 0)])),
            groups[layer][1] + groups[layer][0],
        )
        query_grad, key_own, value_own, halo, prefix_grad = attention_back(
            heads_grad, heads_t, query_t, value8, key_t, attend, tokens, prefix, as_table(only(1, 2)), groups[layer][0]
        )
        near = lax.ppermute(halo[:tokens], "keys", xor_pairs(places, 1))
        across = lax.ppermute(halo[tokens : 2 * tokens], "keys", [(1, 2), (2, 1)])
        edge = lax.ppermute(halo[2 * tokens :], "keys", xor_pairs(places, 2)).astype(F32)
        gradient = input_back(grad_one, query_grad, key_own, value_own, as_table(only(0, 1, 2)), groups[layer][0])
        lead = jnp.where(first_half, 0.0, edge)
        tail = jnp.where(first_half, edge, 0.0)
        gradient = (
            gradient
            + near.astype(F32)
            + across.astype(F32)
            + jnp.concatenate([lead, jnp.zeros((tokens - 2 * EDGE, width), F32), tail], 0)
        )
        share = prefix // places
        split = prefix_grad.reshape(2, places, share, width).transpose(1, 0, 2, 3)
        split = lax.all_to_all(split, "keys", 0, 0)
        prefix_parts[layer] = lax.psum(jnp.sum(split, 0).astype(BF16), "rows").astype(F32)
    return (
        result[None],
        gradient[None],
        jnp.stack([part[0] for part in prefix_parts]),
        jnp.stack([part[1] for part in prefix_parts]),
    )


def solution(mesh):
    placed = (
        P("rows", "keys", None),
        P("rows", None),
        P(None, "keys", None),
        P(None, "keys", None),
        P(None, "rows", None),
        P(None, "rows", None),
        P(None, "rows", None),
        P(None, "rows", None),
        P(None, "rows", None),
        P(),
        P(None, "rows", None),
        P(),
        P(),
        P("rows", "keys", None),
    )
    return jax.shard_map(
        body,
        mesh=mesh,
        in_specs=placed,
        out_specs=(
            P("rows", "keys", None),
            P("rows", "keys", None),
            P(None, "keys", None),
            P(None, "keys", None),
        ),
        check_vma=False,
    )
```

time: 1710 us -> 602 us (0.35)
  blocking collectives: 1030 us -> 11 us
  matrix products: 223 us -> 0 us
  Pallas kernels: 0 us -> 132 us
  waiting for transfers between devices: 298 us -> 344 us
  local copies, waits for them, and re-layouts: 97.5 us -> 58.4 us
  other arithmetic: 40.4 us -> 13.1 us
  starting transfers between devices: 1.23 us -> 27.5 us
    unnamed x2 -> x0, blocking collectives: 993 us -> none
    dot_general x34 -> x0, matrix products: 223 us -> none  [the longest x10 65.4 us: project_back(): jnp.einsum('rte,de->rtd', left, right, preferred_element_type=jnp.float32)]
    pallas_call x0 -> x10, Pallas kernels: none -> 132 us  [call(): pl.pallas_call(partial(kernel, len(pieces)), out_shape=outs, in_specs=[SM...]
    all_gather x16 -> x4, waiting for transfers between devices: 202 us -> 278 us  [gather(): return [lax.all_gather(own, ('rows', 'keys'), axis=0, tiled=True)]]
    unnamed x21 -> x5, waiting for transfers between devices: 47.1 us -> 0.08 us
    psum x2 -> x0, blocking collectives: 22.4 us -> none  [attention_back(): dots = lax.psum(dots, 'keys')]
    convert_element_type x2, other arithmetic: 20.3 us -> 0.17 us  [the longest x1 0.09 us: body(): hidden = low.astype(F32)]
    another operation x2, local copies, waits for them, and re-layouts: 19.6 us -> 0.73 us  [the longest x1 0.73 us: blocks_of(): jnp.stack(up + down)]
  transfers between devices with their start and end apart: 19 -> 19, of which waited for: 10 -> 5; matrix products, arithmetic and copies ran while one was open for 11% -> 4% of each run, Pallas kernels for 0% -> 15%
where the time goes in v1:
time: 602 us; the launch traced here: 601 us
  waiting for transfers between devices  344 us (57%)
  Pallas kernels  132 us (22%)
  local copies, waits for them, and re-layouts  58.4 us (10%)
  starting transfers between devices  27.5 us (5%)
  between operations  14.7 us (2%)
  other arithmetic  13.1 us (2%)
  blocking collectives  11 us (2%)
    all_gather x4, waiting for transfers between devices, gather(): return [lax.all_gather(own, ('rows', 'keys'), axis=0, tiled=True)]  278 us
    pallas_call x10, Pallas kernels, call(): pl.pallas_call(partial(kernel, len(pieces)), out_shape=outs, in_specs=[SM...  132 us
    psum x1, waiting for transfers between devices, body(): lax.psum(jnp.sum(split, 0).astype(BF16), 'rows').astype(F32)  65.9 us
    unnamed x178, local copies, waits for them, and re-layouts  45.9 us
  transfers between devices with their start and end apart: 19, of which 5 were waited for; matrix products, arithmetic and copies ran while one was open for 4% of the time, Pallas kernels for 15%

profile of v1, /device:TPU:0, one launch (start us, length us, event | category | flops | bytes accessed | tf_op | source)
XLA Modules:
  0.0 600.6 jit_solution(12218687148747908342)
XLA Ops:
  7.2 1.4 fusion.20
  8.8 0.9 fusion.6
  16.5 0.9 constant_dynamic-slice_fusion.1
  17.5 0.9 fusion.3
  18.5 1.9 constant_dynamic-slice_fusion
  22.3 3.7 collective-permute-start.2
  26.3 11.0 %all_gather.15 = bf16[2,2,64,1024]{3,2,1,0:T(8,128)(2,1)S(1)} all-gather(bf16[2,2,16,1024]{3,2,1,0:T(8,128)(2,1)S(1)} %pad_maximum_fusion), channel_id=1, replica_groups=mesh['rows'=8,'keys'=4] {'keys'}, dimensions={2}, use_global_device_ids=true | all-gather | bytes 655360 | tf_op jit(solution)/shard_map/all_gather | solution.py:570
  39.8 51.7 %all-gather.5.cloned.1.call-done.refs_11_.refs_10_.refs_7_.refs_5_ = bf16[32,128,1024]{2,1,0:T(8,128)(2,1)} async-done(((bf16[1,128,1024]{2,1,0:T(8,128)(2,1)}), bf16[32,128,1024]{2,1,0:T(8,128)(2,1)}) %all-gather.5.cloned.1.call-update) | async-done | bytes 8388624 | tf_op jit(solution)/shard_map/all_gather | solution.py:523
  91.5 20.5 %shard_map.255 = (f32[224,1024]{1,0:T(8,128)S(1)}, f32[224,1024]{1,0:T(8,128)S(1)}, f32[224,1]{1,0:T(8,128)S(1)}, bf16[1024,256]{1,0:T(8,128)(2,1)S(1)}, bf16[8,...) custom-call(s32[32]{0:T(128)S(1)} %copy-done.67, ...), custom_call_target="tpu_custom_call" | custom-call | flops 3758096384 | bytes 11804672 | tf_op jit(solution)/shard_map/pallas_call | solution.py:337
  112.0 1.1 copy-done.2
  113.1 1.1 copy-done.4
  114.3 1.0 copy-done.10
  115.2 1.0 copy-done.18
  116.2 0.9 copy-done.26
  118.6 89.2 %all-gather.7.cloned.1.call-done.refs_5_.refs_9_ = bf16[64,128,1024]{2,1,0:T(8,128)(2,1)} async-done(((bf16[2,128,1024]{2,1,0:T(8,128)(2,1)}), bf16[64,128,1024]{2,1,0:T(8,128)(2,1)}) %all-gather.7.cloned.1.call-update) | async-done | bytes 16777232 | tf_op jit(solution)/shard_map/all_gather | solution.py:523
  207.8 1.2 copy-done.27
  211.7 15.8 %shard_map.256 = (f32[224,1024]{1,0:T(8,128)S(1)}, bf16[224,1024]{1,0:T(8,128)(2,1)}, f32[224,1024]{1,0:T(8,128)S(1)}, f32[224,1]{1,0:T(8,128)S(1)}, bf16[224,4096]{1,0:T(8,128)(2,1)S(1)}) custom-call(s32[64]{0:T(128)S(1)} %copy-done.62, f32[224,1024]{1,0:T(8,128)S(1)} %copy-done.27, f32[1,4096]{1,0:T(1,128)S(1)} %copy-done.49, f32[1,1024]{1,0:T(1,128)S(1)} %copy-done.50, ...), custom_call_target="tpu_custom_call" | custom-call | flops 3758096384 | bytes 17719296 | tf_op jit(solution)/shard_map/pallas_call | solution.py:337
  227.5 0.9 copy-done.20
  228.5 0.9 copy-done.65
  229.6 1.5 collective-permute-start.4
  231.1 1.5 slice_select_fusion
  232.6 2.5 collective-permute-start.5
  235.2 54.0 %all-gather.9.cloned.1.call-done.refs_11_.refs_10_.refs_7_.refs_5_ = bf16[32,128,1024]{2,1,0:T(8,128)(2,1)} async-done(((bf16[1,128,1024]{2,1,0:T(8,128)(2,1)}), bf16[32,128,1024]{2,1,0:T(8,128)(2,1)}) %all-gather.9.cloned.1.call-update) | async-done | bytes 8388624 | tf_op jit(solution)/shard_map/all_gather | solution.py:523
  289.2 0.9 copy-done.41
  290.1 0.9 copy-done.42
  292.4 1.2 copy-done.66
  294.2 21.6 %shard_map.257 = (f32[224,1024]{1,0:T(8,128)S(1)}, f32[224,1024]{1,0:T(8,128)S(1)}, f32[224,1]{1,0:T(8,128)S(1)}, bf16[1024,256]{1,0:T(8,128)(2,1)S(1)}, bf16[8,...) custom-call(s32[32]{0:T(128)S(1)} %copy-done.68, ...), custom_call_target="tpu_custom_call" | custom-call | flops 3758096384 | bytes 11804672 | tf_op jit(solution)/shard_map/pallas_call | solution.py:337
  315.8 1.2 copy-done.6
  317.0 1.2 copy-done.8
  318.1 1.0 copy-done.12
  319.2 1.0 copy-done.22
  320.1 0.9 copy-done.24
  321.1 0.8 copy-done.31
  322.5 82.9 %all-gather.11.cloned.1.call-done.refs_5_.refs_9_ = bf16[64,128,1024]{2,1,0:T(8,128)(2,1)} async-done(((bf16[2,128,1024]{2,1,0:T(8,128)(2,1)}), bf16[64,128,1024]{2,1,0:T(8,128)(2,1)}) %all-gather.11.cloned.1.call-update) | async-done | bytes 16777232 | tf_op jit(solution)/shard_map/all_gather | solution.py:523
  405.4 1.2 copy-done.25
  408.6 16.0 %shard_map.258 = (f32[224,1024]{1,0:T(8,128)}, bf16[224,1024]{1,0:T(8,128)(2,1)}, f32[224,1024]{1,0:T(8,128)S(1)}, f32[224,1]{1,0:T(8,128)S(1)}, bf16[224,4096]{1,0:T(8,128)(2,1)S(1)}) custom-call(s32[64]{0:T(128)S(1)} %copy-done.63, f32[224,1024]{1,0:T(8,128)S(1)} %copy-done.25, f32[1,4096]{1,0:T(1,128)S(1)} %get-tuple-element.118.refs_2_, ...), custom_call_target="tpu_custom_call" | custom-call | flops 3758096384 | bytes 17719296 | tf_op jit(solution)/shard_map/pallas_call | solution.py:337
  424.7 13.5 %shard_map.259 = (f32[224,1024]{1,0:T(8,128)S(1)}, bf16[1024,256]{1,0:T(8,128)(2,1)S(1)}) custom-call(s32[96]{0:T(128)S(1)} %copy-done.64, f32[224,1024]{1,0:T(8,128)S(1)} %bitcast_convert_fusion.refs_1_, f32[224,1024]{1,0:T(8,128)S(1)} %get-tuple-element.48.refs_2_, f32[224,1]{1,0:T(8,128)S(1)} %get-tuple-element.49.refs_3_, f32[1,1024]{1,0:T(1,128)S(1)} %copy-done.52, ...), custom_call_target="tpu_custom_call" | custom-call | flops 4227858432 | bytes 29763328 | tf_op jit(solution)/shard_map/pallas_call | solution.py:337
  438.3 11.5 %shard_map.260 = (bf16[224,1024]{1,0:T(8,128)(2,1)S(1)}, bf16[224,1024]{1,0:T(8,128)(2,1)S(1)}, bf16[224,1024]{1,0:T(8,128)(2,1)S(1)}, bf16[480,1024]{1,0:T(8,128)(2,1)S(1)}, f32[2,64,1024]{2,1,0:T(8,128)S(1)}) custom-call(s32[32]{0:T(128)S(1)} %copy-done.61, bf16[1024,256]{1,0:T(8,128)(2,1)S(1)} %get-tuple-element.54.refs_1_, f32[1024,256]{1,0:T(8,128)S(1)} %copy-done.13, ...), custom_call_target="tpu_custom_call" | custom-call | flops 2818572288 | bytes 13631488 | tf_op jit(solution)/shard_map/pallas_call | solution.py:337
  449.8 1.0 fusion.17
  450.8 1.4 collective-permute-start.7
  452.3 1.9 collective-permute-start.6
  454.8 0.9 copy.32
  455.7 4.4 all-to-all-start.1
  460.1 3.4 copy-done.1
  463.5 1.0 copy-done.38
  464.5 1.0 copy-done.40
  465.5 4.0 shard_map.261
  469.7 1.5 maximum_add_fusion.refs_1_
  471.4 13.5 %shard_map.262 = (f32[224,1024]{1,0:T(8,128)S(1)}, bf16[1024,256]{1,0:T(8,128)(2,1)S(1)}) custom-call(s32[96]{0:T(128)S(1)} %copy-done.64, f32[224,1024]{1,0:T(8,128)S(1)} %maximum_add_fusion.refs_1_, f32[224,1024]{1,0:T(8,128)S(1)} %copy-done.21, f32[224,1]{1,0:T(8,128)S(1)} %copy-done.46, f32[1,1024]{1,0:T(1,128)S(1)} %copy-done.51, ...), custom_call_target="tpu_custom_call" | custom-call | flops 4227858432 | bytes 29763328 | tf_op jit(solution)/shard_map/pallas_call | solution.py:337
  485.0 11.5 %shard_map.263 = (bf16[224,1024]{1,0:T(8,128)(2,1)S(1)}, bf16[224,1024]{1,0:T(8,128)(2,1)S(1)}, bf16[224,1024]{1,0:T(8,128)(2,1)S(1)}, bf16[480,1024]{1,0:T(8,128)(2,1)S(1)}, f32[2,64,1024]{2,1,0:T(8,128)S(1)}) custom-call(s32[32]{0:T(128)S(1)} %copy-done.61, bf16[1024,256]{1,0:T(8,128)(2,1)S(1)} %get-tuple-element.70.refs_1_, f32[1024,256]{1,0:T(8,128)S(1)} %copy-done.11, ...), custom_call_target="tpu_custom_call" | custom-call | flops 2818572288 | bytes 13631488 | tf_op jit(solution)/shard_map/pallas_call | solution.py:337
  498.1 1.0 fusion.16
  499.1 1.4 collective-permute-start.10
  500.5 2.4 collective-permute-start.9
  502.9 0.8 copy.33
  503.8 4.1 all-to-all-start
  508.0 1.7 reduce_sum.19
  509.7 1.9 collective-permute-start.11
  511.6 3.4 copy-done
  515.0 1.0 copy-done.34
  516.0 1.0 copy-done.36
  517.0 4.1 shard_map.264
  521.2 1.7 reduce_sum.18
  523.0 2.3 fusion
  525.2 65.9 %all-reduce.5.cloned.1.call-done = (bf16[2,16,1024]{2,1,0:T(8,128)(2,1)}, bf16[2,16,1024]{2,1,0:T(8,128)(2,1)}) async-done(((bf16[2,16,1024]{2,1,0:T(8,128)(2,1)}, bf16[2,16,1024]{2,1,0:T(8,128)(2,1)}), (bf16[2,16,1024]{2,1,0:T(8,128)(2,1)}, bf16[2,16,1024]{2,1,0:T(8,128)(2,1)})) %all-reduce.5.cloned.1.call-update) | async-done | bytes 131088 | tf_op jit(solution)/shard_map/psum | solution.py:631
  (210 shorter events, 26.3 us)
Async XLA Ops:
  7.2 84.3 %all-gather.5.cloned.1.call-start = ((), (), s32[]{:S(2)}) async-start(), calls=%async_computation.2 | async-start | bytes 8650752 | tf_op jit(solution)/shard_map/all_gather | solution.py:523
  8.7 1.7 copy-start.69
  9.8 198.0 %all-gather.7.cloned.1.call-start = ((), (), s32[]{:S(2)}) async-start(), calls=%async_computation.3 | async-start | bytes 17301504 | tf_op jit(solution)/shard_map/all_gather | solution.py:523
  10.6 3.0 copy-start.70
  17.4 3.0 copy-start.28
  17.4 8.6 %copy-start.79 = (s32[1,896]{1,0:T(1,128)S(1)}, s32[1,896]{1,0:T(1,128)}, u32[]{:S(2)}) copy-start(s32[1,896]{1,0:T(1,128)} %param.25) | copy-start | bytes 10756
  17.4 8.9 %copy-start.74 = (bf16[2,16,1024]{2,1,0:T(8,128)(2,1)S(1)}, bf16[2,16,1024]{2,1,0:T(8,128)(2,1)}, u32[]{:S(2)}) copy-start(bf16[2,16,1024]{2,1,0:T(8,128)(2,1)} %param.27) | copy-start | bytes 196612
  17.4 8.9 %copy-start.75 = (bf16[2,16,1024]{2,1,0:T(8,128)(2,1)S(1)}, bf16[2,16,1024]{2,1,0:T(8,128)(2,1)}, u32[]{:S(2)}) copy-start(bf16[2,16,1024]{2,1,0:T(8,128)(2,1)} %param.26) | copy-start | bytes 196612
  17.4 271.7 %all-gather.9.cloned.1.call-start = ((), (), s32[]{:S(2)}) async-start(), calls=%async_computation.4 | async-start | bytes 8650752 | tf_op jit(solution)/shard_map/all_gather | solution.py:523
  18.4 19.8 %copy-start.76 = (f32[2,4096]{1,0:T(2,128)S(1)}, f32[2,4096]{1,0:T(2,128)}, u32[]{:S(2)}) copy-start(f32[2,4096]{1,0:T(2,128)} %param.33) | copy-start | bytes 98308
  18.4 20.4 %copy-start.77 = (f32[2,2,1024]{2,1,0:T(2,128)S(1)}, f32[2,2,1024]{2,1,0:T(2,128)}, u32[]{:S(2)}) copy-start(f32[2,2,1024]{2,1,0:T(2,128)} %param.36) | copy-start | bytes 49156
  18.4 20.4 %copy-start.78 = (f32[2,2,1024]{2,1,0:T(2,128)S(1)}, f32[2,2,1024]{2,1,0:T(2,128)}, u32[]{:S(2)}) copy-start(f32[2,2,1024]{2,1,0:T(2,128)} %param.35) | copy-start | bytes 49156
  18.5 386.9 %all-gather.11.cloned.1.call-start = ((), (), s32[]{:S(2)}) async-start(), calls=%async_computation.5 | async-start | bytes 17301504 | tf_op jit(solution)/shard_map/all_gather | solution.py:523
  20.4 19.3 %collective-permute-start = (bf16[224,1024]{1,0:T(8,128)(2,1)S(1)}, bf16[224,1024]{1,0:T(8,128)(2,1)S(1)}, u32[]{:S(2)}, u32[]{:S(2)}) collective-permute-start(bf16[224,1024]{1,0:T(8,128)(2,1)S(1)} %bitcast.89), channel_id=1, source_target_pairs={{0,1},{1,0},{2,3},{3,2},{4,5},{5,4},{6,7},{7,6},{8,9},{9,8},{10,11... | collective-permute-start | bytes 1376264 | tf_op jit(solution)/shard_map/ppermute | solution.py:549
  21.0 18.8 %collective-permute-start.1 = (bf16[224,1024]{1,0:T(8,128)(2,1)S(1)}, bf16[224,1024]{1,0:T(8,128)(2,1)S(1)}, u32[]{:S(2)}, u32[]{:S(2)}) collective-permute-start(bf16[224,1024]{1,0:T(8,128)(2,1)S(1)} %bitcast.90), channel_id=1, source_target_pairs={{1,2},{2,1},{5,6},{6,5},{9,10},{10,9},{13,14},{14,13},{17,18},{18,... | collective-permute-start | bytes 1376264 | tf_op jit(solution)/shard_map/ppermute | solution.py:550
  22.3 17.4 %collective-permute-start.2 = (bf16[32,1024]{1,0:T(8,128)(2,1)}, bf16[32,1024]{1,0:T(8,128)(2,1)S(1)}, u32[]{:S(2)}, u32[]{:S(2)}) collective-permute-start(bf16[32,1024]{1,0:T(8,128)(2,1)} %select_bitcast_fusion), channel_id=1, source_target_pairs={{0,2},{1,3},{2,0},{3,1},{4,6},{5,7},{6,4},{7,5},{8,10},{9,11},{10,... | collective-permute-start | bytes 196616 | tf_op jit(solution)/shard_map/ppermute | solution.py:551
  38.2 53.2 %copy-start.67 = (s32[32]{0:T(128)S(1)}, s32[32]{0:T(128)}, u32[]{:S(2)}) copy-start(s32[32]{0:T(128)} %constant.46.clone.refs_0_) | copy-start | bytes 388
  39.5 72.5 %copy-start.55 = (f32[1,1024]{1,0:T(1,128)}, f32[1,1024]{1,0:T(1,128)S(1)}, u32[]{:S(2)}) copy-start(f32[1,1024]{1,0:T(1,128)S(1)} %get-tuple-element.136.refs_9_.refs_8_) | copy-start | bytes 12292
  211.7 23.4 %copy-start.73 = (bf16[1,224,1024]{2,1,0:T(8,128)(2,1)S(1)}, bf16[1,224,1024]{2,1,0:T(8,128)(2,1)}, u32[]{:S(2)}) copy-start(bf16[1,224,1024]{2,1,0:T(8,128)(2,1)} %param.37) | copy-start | bytes 1376260
  229.4 3.2 copy-start.45
  229.4 59.8 %collective-permute-start.3 = (bf16[224,1024]{1,0:T(8,128)(2,1)}, bf16[224,1024]{1,0:T(8,128)(2,1)}, u32[]{:S(2)}, u32[]{:S(2)}) collective-permute-start(bf16[224,1024]{1,0:T(8,128)(2,1)} %get-tuple-element.44.refs_1_), channel_id=1, source_target_pairs={{0,1},{1,0},{2,3},{3,2},{4,5},{5,4},{6,7},{7,6},{8,9},{9,8},{10,11... | collective-permute-start | bytes 1376264 | tf_op jit(solution)/shard_map/ppermute | solution.py:549
  229.6 59.5 %collective-permute-start.4 = (bf16[224,1024]{1,0:T(8,128)(2,1)}, bf16[224,1024]{1,0:T(8,128)(2,1)}, u32[]{:S(2)}, u32[]{:S(2)}) collective-permute-start(bf16[224,1024]{1,0:T(8,128)(2,1)} %get-tuple-element.44.refs_1_), channel_id=1, source_target_pairs={{1,2},{2,1},{5,6},{6,5},{9,10},{10,9},{13,14},{14,13},{17,18},{18,... | collective-permute-start | bytes 1376264 | tf_op jit(solution)/shard_map/ppermute | solution.py:550
  232.6 56.6 %collective-permute-start.5 = (bf16[32,1024]{1,0:T(8,128)(2,1)}, bf16[32,1024]{1,0:T(8,128)(2,1)}, u32[]{:S(2)}, u32[]{:S(2)}) collective-permute-start(bf16[32,1024]{1,0:T(8,128)(2,1)} %slice_select_fusion), channel_id=1, source_target_pairs={{0,2},{1,3},{2,0},{3,1},{4,6},{5,7},{6,4},{7,5},{8,10},{9,11},{10,... | collective-permute-start | bytes 196616 | tf_op jit(solution)/shard_map/ppermute | solution.py:551
  408.6 16.0 %copy-start.23 = (f32[224,1024]{1,0:T(8,128)S(1)}, f32[224,1024]{1,0:T(8,128)}, u32[]{:S(2)}) copy-start(f32[224,1024]{1,0:T(8,128)} %copy-done.22) | copy-start | bytes 2752516
  408.6 16.0 %copy-start.48 = (f32[224,1]{1,0:T(8,128)S(1)}, f32[224,1]{1,0:T(8,128)}, u32[]{:S(2)}) copy-start(f32[224,1]{1,0:T(8,128)} %copy-done.47) | copy-start | bytes 2692
  408.6 16.0 %copy-start.58 = (f32[1,1024]{1,0:T(1,128)S(1)}, f32[1,1024]{1,0:T(1,128)}, u32[]{:S(2)}) copy-start(f32[1,1024]{1,0:T(1,128)} %get-tuple-element.135.refs_9_.refs_8_) | copy-start | bytes 12292
  408.6 16.0 %copy-start.64 = (s32[96]{0:T(128)S(1)}, s32[96]{0:T(128)}, u32[]{:S(2)}) copy-start(s32[96]{0:T(128)} %constant.48.clone.refs_0_) | copy-start | bytes 1156
  424.6 13.6 %slice-start.2 = ((s8[6291456]{0:T(1024)(128)(4,1)}), s8[4194304]{0:T(1024)(128)(4,1)S(1)}, s32[]{:S(2)}) async-start(s8[6291456]{0:T(1024)(128)(4,1)} %bitcast.87), calls=%async_computation.9 | async-start | bytes 8388608
  424.6 13.6 %slice-start.3 = ((s8[6291456]{0:T(1024)(128)(4,1)}), s8[2097152]{0:T(1024)(128)(4,1)S(1)}, s32[]{:S(2)}) async-start(s8[6291456]{0:T(1024)(128)(4,1)} %bitcast.87), calls=%async_computation.10 | async-start | bytes 4194304
  424.6 13.6 %copy-start.7 = (bf16[8,768,128]{2,1,0:T(8,128)(2,1)S(1)}, bf16[8,768,128]{2,1,0:T(8,128)(2,1)}, u32[]{:S(2)}) copy-start(bf16[8,768,128]{2,1,0:T(8,128)(2,1)} %copy-done.6) | copy-start | bytes 4718596
  424.6 13.6 %copy-start.9 = (bf16[1024,768]{1,0:T(8,128)(2,1)S(1)}, bf16[1024,768]{1,0:T(8,128)(2,1)}, u32[]{:S(2)}) copy-start(bf16[1024,768]{1,0:T(8,128)(2,1)} %copy-done.8) | copy-start | bytes 4718596
  424.6 13.6 %copy-start.13 = (f32[1024,256]{1,0:T(8,128)S(1)}, f32[1024,256]{1,0:T(8,128)}, u32[]{:S(2)}) copy-start(f32[1024,256]{1,0:T(8,128)} %copy-done.12) | copy-start | bytes 3145732
  424.6 13.6 %copy-start.32 = (bf16[1024,256]{1,0:T(8,128)(2,1)S(1)}, bf16[1024,256]{1,0:T(8,128)(2,1)}, u32[]{:S(2)}) copy-start(bf16[1024,256]{1,0:T(8,128)(2,1)} %copy-done.31) | copy-start | bytes 1572868
  424.7 13.6 %copy-start.61 = (s32[32]{0:T(128)S(1)}, s32[32]{0:T(128)}, u32[]{:S(2)}) copy-start(s32[32]{0:T(128)} %constant.49.clone.refs_0_) | copy-start | bytes 388
  438.2 11.6 %copy-start.16 = (f32[224,1024]{1,0:T(8,128)}, f32[224,1024]{1,0:T(8,128)S(1)}, u32[]{:S(2)}) copy-start(f32[224,1024]{1,0:T(8,128)S(1)} %get-tuple-element.53.refs_1_) | copy-start | bytes 2752516
  449.8 5.9 copy-start.37
  449.8 5.9 copy-start.39
  449.8 10.3 %copy-start.60 = (s32[32]{0:T(128)S(1)}, s32[32]{0:T(128)}, u32[]{:S(2)}) copy-start(s32[32]{0:T(128)} %constant.50.clone.refs_0_) | copy-start | bytes 388
  449.8 10.3 %copy-start.17 = (f32[224,1024]{1,0:T(8,128)S(1)}, f32[224,1024]{1,0:T(8,128)}, u32[]{:S(2)}) copy-start(f32[224,1024]{1,0:T(8,128)} %copy-done.16) | copy-start | bytes 2752516
  450.8 18.8 %collective-permute-start.7 = (bf16[224,1024]{1,0:T(8,128)(2,1)}, bf16[224,1024]{1,0:T(8,128)(2,1)}, u32[]{:S(2)}, u32[]{:S(2)}) collective-permute-start(bf16[224,1024]{1,0:T(8,128)(2,1)} %get-tuple-element.97), channel_id=1, source_target_pairs={{1,2},{2,1},{5,6},{6,5},{9,10},{10,9},{13,14},{14,13},{17,18},{18,... | collective-permute-start | bytes 1376264 | tf_op jit(solution)/shard_map/ppermute | solution.py:617
  452.3 17.4 %collective-permute-start.6 = (bf16[224,1024]{1,0:T(8,128)(2,1)}, bf16[224,1024]{1,0:T(8,128)(2,1)}, u32[]{:S(2)}, u32[]{:S(2)}) collective-permute-start(bf16[224,1024]{1,0:T(8,128)(2,1)} %get-tuple-element.96), channel_id=1, source_target_pairs={{0,1},{1,0},{2,3},{3,2},{4,5},{5,4},{6,7},{7,6},{8,9},{9,8},{10,11... | collective-permute-start | bytes 1376264 | tf_op jit(solution)/shard_map/ppermute | solution.py:616
  454.3 15.4 %collective-permute-start.8 = (bf16[32,1024]{1,0:T(8,128)(2,1)S(1)}, bf16[32,1024]{1,0:T(8,128)(2,1)S(1)}, u32[]{:S(2)}, u32[]{:S(2)}) collective-permute-start(bf16[32,1024]{1,0:T(8,128)(2,1)S(1)} %slice.266), channel_id=1, source_target_pairs={{0,2},{1,3},{2,0},{3,1},{4,6},{5,7},{6,4},{7,5},{8,10},{9,11},{10,... | collective-permute-start | bytes 196616 | tf_op jit(solution)/shard_map/ppermute | solution.py:618
  455.7 48.1 %all-to-all-start.1 = ((f32[4,2,16,1024]{3,2,1,0:T(8,128)}), f32[4,2,16,1024]{3,2,1,0:T(8,128)}, u32[]{:S(2)}, u32[]{:S(2)}) async-start(f32[4,2,16,1024]{3,2,1,0:T(8,128)} %bitcast.94), calls=%async_computation.1 | async-start | bytes 1048576 | tf_op jit(solution)/shard_map/all_to_all | solution.py:630
  460.1 3.4 copy-start.1
  469.6 1.6 copy-start.19
  469.6 1.7 copy-start.21
  469.6 1.7 copy-start.44
  469.6 1.7 copy-start.46
  469.6 1.7 copy-start.51
  469.6 1.7 copy-start.56
  471.2 13.8 %slice-start = ((s8[6291456]{0:T(1024)(128)(4,1)}), s8[4194304]{0:T(1024)(128)(4,1)S(1)}, s32[]{:S(2)}) async-start(s8[6291456]{0:T(1024)(128)(4,1)} %bitcast.85), calls=%async_computation.7 | async-start | bytes 8388608
  471.3 13.6 %slice-start.1 = ((s8[6291456]{0:T(1024)(128)(4,1)}), s8[2097152]{0:T(1024)(128)(4,1)S(1)}, s32[]{:S(2)}) async-start(s8[6291456]{0:T(1024)(128)(4,1)} %bitcast.85), calls=%async_computation.8 | async-start | bytes 4194304
  471.3 13.6 %copy-start.3 = (bf16[8,768,128]{2,1,0:T(8,128)(2,1)S(1)}, bf16[8,768,128]{2,1,0:T(8,128)(2,1)}, u32[]{:S(2)}) copy-start(bf16[8,768,128]{2,1,0:T(8,128)(2,1)} %copy-done.2) | copy-start | bytes 4718596
  471.4 13.6 %copy-start.5 = (bf16[1024,768]{1,0:T(8,128)(2,1)S(1)}, bf16[1024,768]{1,0:T(8,128)(2,1)}, u32[]{:S(2)}) copy-start(bf16[1024,768]{1,0:T(8,128)(2,1)} %copy-done.4) | copy-start | bytes 4718596
  471.4 13.6 %copy-start.11 = (f32[1024,256]{1,0:T(8,128)S(1)}, f32[1024,256]{1,0:T(8,128)}, u32[]{:S(2)}) copy-start(f32[1024,256]{1,0:T(8,128)} %copy-done.10) | copy-start | bytes 3145732
  471.4 13.6 %copy-start.30 = (bf16[1024,256]{1,0:T(8,128)(2,1)S(1)}, bf16[1024,256]{1,0:T(8,128)(2,1)}, u32[]{:S(2)}) copy-start(bf16[1024,256]{1,0:T(8,128)(2,1)} %copy-done.29) | copy-start | bytes 1572868
  484.9 11.6 %copy-start.14 = (f32[224,1024]{1,0:T(8,128)}, f32[224,1024]{1,0:T(8,128)S(1)}, u32[]{:S(2)}) copy-start(f32[224,1024]{1,0:T(8,128)S(1)} %get-tuple-element.69.refs_1_) | copy-start | bytes 2752516
  498.1 13.5 %copy-start.15 = (f32[224,1024]{1,0:T(8,128)S(1)}, f32[224,1024]{1,0:T(8,128)}, u32[]{:S(2)}) copy-start(f32[224,1024]{1,0:T(8,128)} %copy-done.14) | copy-start | bytes 2752516
  499.1 23.8 %collective-permute-start.10 = (bf16[224,1024]{1,0:T(8,128)(2,1)}, bf16[224,1024]{1,0:T(8,128)(2,1)}, u32[]{:S(2)}, u32[]{:S(2)}) collective-permute-start(bf16[224,1024]{1,0:T(8,128)(2,1)} %get-tuple-element.95), channel_id=1, source_target_pairs={{1,2},{2,1},{5,6},{6,5},{9,10},{10,9},{13,14},{14,13},{17,18},{18,... | collective-permute-start | bytes 1376264 | tf_op jit(solution)/shard_map/ppermute | solution.py:617
  500.5 22.4 %collective-permute-start.9 = (bf16[224,1024]{1,0:T(8,128)(2,1)}, bf16[224,1024]{1,0:T(8,128)(2,1)}, u32[]{:S(2)}, u32[]{:S(2)}) collective-permute-start(bf16[224,1024]{1,0:T(8,128)(2,1)} %get-tuple-element.94), channel_id=1, source_target_pairs={{0,1},{1,0},{2,3},{3,2},{4,5},{5,4},{6,7},{7,6},{8,9},{9,8},{10,11... | collective-permute-start | bytes 1376264 | tf_op jit(solution)/shard_map/ppermute | solution.py:616
  503.8 17.4 %all-to-all-start = ((f32[4,2,16,1024]{3,2,1,0:T(8,128)}), f32[4,2,16,1024]{3,2,1,0:T(8,128)}, u32[]{:S(2)}, u32[]{:S(2)}) async-start(f32[4,2,16,1024]{3,2,1,0:T(8,128)} %bitcast.84), calls=%async_computation | async-start | bytes 1048576 | tf_op jit(solution)/shard_map/all_to_all | solution.py:630
  507.9 83.2 %all-reduce.5.cloned.1.call-start = ((), (), s32[]{:S(2)}) async-start(), calls=%async_computation.6 | async-start | bytes 262144 | tf_op jit(solution)/shard_map/psum | solution.py:631
  509.7 11.4 %collective-permute-start.11 = (bf16[32,1024]{1,0:T(8,128)(2,1)S(1)}, bf16[32,1024]{1,0:T(8,128)(2,1)S(1)}, u32[]{:S(2)}, u32[]{:S(2)}) collective-permute-start(bf16[32,1024]{1,0:T(8,128)(2,1)S(1)} %slice.269), channel_id=1, source_target_pairs={{0,2},{1,3},{2,0},{3,1},{4,6},{5,7},{6,4},{7,5},{8,10},{9,11},{10,... | collective-permute-start | bytes 196616 | tf_op jit(solution)/shard_map/ppermute | solution.py:618
  511.6 3.4 copy-start
  (39 other events, 35.8 us)
Sparse Core Ops, SparseCore 0:
  11.4 79.9 all-gather.4
  94.3 113.4 all-gather.6
  210.7 78.4 all-gather.8
  291.9 113.4 all-gather.10
  523.1 68.0 all-reduce.4

commit v2 on v1

--- a/solution.py
+++ b/solution.py
@@ -50,24 +50,17 @@
     )
 
 
-def start_loads(table, pieces, weights, sems):
-    at = 0
-    for piece in pieces:
-        blocks, rows, width = piece.shape
-
-        def start(i, carry, piece=piece, at=at, rows=rows, width=width):
-            row = table[at + i]
-
-            @pl.when(row >= 0)
-            def _():
-                pltpu.make_async_copy(
-                    piece.at[i], weights.at[ds(row, rows)], sems.at[row // width]
-                ).start()
-
+def start_loads(tables, pieces, weights, sems):
+    width = weights.shape[1]
+    for piece, entries in zip(pieces, tables):
+        rows = piece.shape[1]
+
+        def start(i, carry, piece=piece, entries=entries, rows=rows):
+            row = entries[2 * i + 1]
+            pltpu.make_async_copy(piece.at[entries[2 * i]], weights.at[ds(row, rows)], sems.at[row // width]).start()
             return carry
 
-        lax.fori_loop(0, blocks, start, 0)
-        at += blocks
+        lax.fori_loop(0, entries.shape[0] // 2, start, 0)
 
 
 def wait_load(weights, sems, index):
@@ -88,14 +81,14 @@
 
 
 def attention_kernel(count, *refs):
-    (table, own, near, across, edge, residual, bias, prefix_k, prefix_v, gain, shift) = refs[:11]
-    pieces = refs[11 : 11 + count]
-    (middle, normed, inverse, query_t, value8, key_t, attend, heads_t) = refs[11 + count : 19 + count]
-    (weights, window, key8, value_t, scores, sems) = refs[19 + count :]
+    tables, pieces, refs = refs[:count], refs[count : 2 * count], refs[2 * count :]
+    (own, near, across, edge, residual, bias, prefix_k, prefix_v, gain, shift) = refs[:10]
+    (middle, normed, inverse, query_t, value8, key_t, attend, heads_t) = refs[10:18]
+    (weights, window, key8, value_t, scores, sems) = refs[18:]
     tokens, width = own.shape
     span = window.shape[0]
     keys = key8.shape[1]
-    start_loads(table, pieces, weights, sems)
+    start_loads(tables, pieces, weights, sems)
     window[pl.ds(0, tokens)] = own[...]
     window[pl.ds(tokens, tokens)] = near[...]
     window[pl.ds(2 * tokens, tokens)] = across[...]
@@ -159,13 +152,13 @@
 
 
 def forward_kernel(count, *refs):
-    (table, middle, up_bias, gain, shift) = refs[:5]
-    pieces = refs[5 : 5 + count]
-    (output, low, normed, inverse, slope) = refs[5 + count : 10 + count]
-    (weights, middle_low, hidden, sems) = refs[10 + count :]
+    tables, pieces, refs = refs[:count], refs[count : 2 * count], refs[2 * count :]
+    (middle, up_bias, gain, shift) = refs[:4]
+    (output, low, normed, inverse, slope) = refs[4:9]
+    (weights, middle_low, hidden, sems) = refs[9:]
     tokens, width = middle.shape
     wide = up_bias.shape[1]
-    start_loads(table, pieces, weights, sems)
+    start_loads(tables, pieces, weights, sems)
     middle_low[...] = middle[...].astype(BF16)
     for block in range(wide // width):
         wait_load(weights, sems, block)
@@ -197,14 +190,14 @@
 
 
 def forward_back_kernel(count, *refs):
-    (table, grad, normed_two, inverse_two, gain_two, slope, normed_one, inverse_one, gain_one) = refs[:9]
-    pieces = refs[9 : 9 + count]
-    (grad_one, heads_grad) = refs[9 + count : 11 + count]
-    (weights, low, hidden, sems) = refs[11 + count :]
+    tables, pieces, refs = refs[:count], refs[count : 2 * count], refs[2 * count :]
+    (grad, normed_two, inverse_two, gain_two, slope, normed_one, inverse_one, gain_one) = refs[:8]
+    (grad_one, heads_grad) = refs[8:10]
+    (weights, low, hidden, sems) = refs[10:]
     tokens, width = grad.shape
     wide = slope.shape[1]
     many = wide // width
-    start_loads(table, pieces, weights, sems)
+    start_loads(tables, pieces, weights, sems)
     grad_two = norm_back(grad[...], gain_two[...], normed_two[...], inverse_two[...])
     grad_one[...] = grad_two
     low[pl.ds(0, tokens), :] = grad_two.astype(BF16)
@@ -247,17 +240,17 @@
 
 
 def attention_back_kernel(count, *refs):
-    (table, heads_grad, heads_t, query_t, value8, key_t, attend_hbm) = refs[:7]
-    pieces = refs[7 : 7 + count]
-    (query_grad, key_own, value_own, halo, prefix_grad) = refs[7 + count : 12 + count]
-    (weights, attend, key_grad, value_grad, query_grad_t, steps, sems, attend_sems) = refs[12 + count :]
+    tables, pieces, refs = refs[:count], refs[count : 2 * count], refs[2 * count :]
+    (heads_grad, heads_t, query_t, value8, key_t, attend_hbm) = refs[:6]
+    (query_grad, key_own, value_own, halo, prefix_grad) = refs[6:11]
+    (weights, attend, key_grad, value_grad, query_grad_t, steps, sems, attend_sems) = refs[11:]
     tokens, width = query_grad.shape
     keys = attend.shape[1]
     prefix = prefix_grad.shape[1]
     span = keys - prefix
     for p in range(PAIRS):
         pltpu.make_async_copy(attend_hbm.at[p], attend.at[p], attend_sems.at[p]).start()
-    start_loads(table, pieces, weights, sems)
+    start_loads(tables, pieces, weights, sems)
     step = 128
 
     def pair(p, carry):
@@ -304,12 +297,12 @@
 
 
 def input_back_kernel(count, *refs):
-    (table, grad_one, query_grad, key_own, value_own) = refs[:5]
-    pieces = refs[5 : 5 + count]
-    grad_input = refs[5 + count]
-    (weights, sems) = refs[6 + count :]
+    tables, pieces, refs = refs[:count], refs[count : 2 * count], refs[2 * count :]
+    (grad_one, query_grad, key_own, value_own) = refs[:4]
+    grad_input = refs[4]
+    (weights, sems) = refs[5:]
     width = grad_one.shape[1]
-    start_loads(table, pieces, weights, sems)
+    start_loads(tables, pieces, weights, sems)
     for index in range(3):
         wait_load(weights, sems, index)
 
@@ -332,33 +325,35 @@
 ANY = pl.BlockSpec(memory_space=pl.ANY)
 
 
-def call(kernel, table, operands, kept, pieces, outs, scratch, limit, flops, any_outs=()):
-    moved = sum(x.size * x.dtype.itemsize for x in pieces) + sum(x.size * x.dtype.itemsize for x in operands)
+def call(kernel, weights, operands, kept, outs, scratch, limit, flops):
+    tables, pieces = weights
+    moved = sum(x.size * x.dtype.itemsize for x in operands)
+    moved += sum(len(t) * p[0].size * p.dtype.itemsize for t, p in zip(tables, pieces))
+    tables = [jnp.asarray(np.asarray(x).reshape(-1), jnp.int32) for x in tables]
     return pl.pallas_call(
         partial(kernel, len(pieces)),
         out_shape=outs,
-        in_specs=[SMEM] + [VMEM] * len(operands) + [ANY] * (len(kept) + len(pieces)),
-        out_specs=[ANY if i in any_outs else VMEM for i in range(len(outs))],
+        in_specs=[SMEM] * len(tables) + [ANY] * len(pieces) + [VMEM] * len(operands) + [ANY] * len(kept),
+        out_specs=[VMEM] * len(outs),
         scratch_shapes=scratch,
         compiler_params=pltpu.CompilerParams(vmem_limit_bytes=limit * MIB),
         cost_estimate=pl.CostEstimate(flops=flops, bytes_accessed=moved, transcendentals=0),
-    )(table, *operands, *kept, *pieces)
+    )(*tables, *pieces, *operands, *kept)
 
 
 def shape(*sizes, dtype=BF16):
     return jax.ShapeDtypeStruct(sizes, dtype)
 
 
-def attention_forward(inputs, inputs_low, around, bias, prefix_k, prefix_v, gain, shift, table, pieces):
+def attention_forward(inputs, inputs_low, around, bias, prefix_k, prefix_v, gain, shift, weights):
     tokens, width = inputs.shape
     keys = bias.shape[0]
     span = keys - prefix_k.shape[0]
     return call(
         attention_kernel,
-        table,
+        weights,
         [inputs_low, *around, inputs, bias, prefix_k, prefix_v, gain, shift],
         [],
-        pieces,
         [
             shape(tokens, width, dtype=F32),
             shape(tokens, width, dtype=F32),
@@ -382,16 +377,15 @@
     )
 
 
-def feed_forward(middle, up_bias, gain, shift, table, pieces):
+def feed_forward(middle, up_bias, gain, shift, weights):
     tokens, width = middle.shape
     wide = up_bias.shape[1]
     many = wide // width
     return call(
         forward_kernel,
-        table,
+        weights,
         [middle, up_bias, gain, shift],
         [],
-        pieces,
         [
             shape(tokens, width, dtype=F32),
             shape(tokens, width),
@@ -410,16 +404,15 @@
     )
 
 
-def feed_back(grad, saved_two, gain_two, slope, saved_one, gain_one, table, pieces):
+def feed_back(grad, saved_two, gain_two, slope, saved_one, gain_one, weights):
     tokens, width = grad.shape
     wide = slope.shape[1]
     many = wide // width
     return call(
         forward_back_kernel,
-        table,
+        weights,
         [grad, *saved_two, gain_two, slope, *saved_one, gain_one],
         [],
-        pieces,
         [shape(tokens, width, dtype=F32), shape(width, LANES)],
         [
             pltpu.VMEM((2 * wide + width, width), BF16),
@@ -432,16 +425,15 @@
     )
 
 
-def attention_back(heads_grad, heads_t, query_t, value8, key_t, attend, tokens, prefix, table, pieces):
+def attention_back(heads_grad, heads_t, query_t, value8, key_t, attend, tokens, prefix, weights):
     width = heads_grad.shape[0]
     keys = attend.shape[1]
     span = keys - prefix
     return call(
         attention_back_kernel,
-        table,
+        weights,
         [heads_grad, heads_t, query_t, value8, key_t],
         [attend],
-        pieces,
         [
             shape(tokens, width),
             shape(tokens, width),
@@ -464,14 +456,13 @@
     )
 
 
-def input_back(grad_one, query_grad, key_own, value_own, table, pieces):
+def input_back(grad_one, query_grad, key_own, value_own, weights):
     tokens, width = grad_one.shape
     return call(
         input_back_kernel,
-        table,
+        weights,
         [grad_one, query_grad, key_own, value_own],
         [],
-        pieces,
         [shape(tokens, width, dtype=F32)],
         [pltpu.VMEM((3 * width, width), BF16), pltpu.SemaphoreType.DMA((3,))],
         30,
@@ -481,6 +472,27 @@
 
 def xor_pairs(count, bit):
     return [(i, i ^ bit) for i in range(count)]
+
+
+def sum_prefixes(parts):
+    layers, two, prefix, width = parts.shape
+    places = lax.axis_size("keys")
+    place = lax.axis_index("keys")
+    total = parts
+    step = places // 2
+    while step:
+        split = total.reshape(layers, two, 2, -1, width)
+        mine = (place // step) % 2
+        sent = lax.dynamic_index_in_dim(split, 1 - mine, 2, False).astype(BF16)
+        kept = lax.dynamic_index_in_dim(split, mine, 2, False)
+        total = kept + lax.ppermute(sent, "keys", xor_pairs(places, step)).astype(F32)
+        step //= 2
+    count = lax.axis_size("rows")
+    step = 1
+    while step < count:
+        total = total + lax.ppermute(total.astype(BF16), "rows", xor_pairs(count, step)).astype(F32)
+        step *= 2
+    return total
 
 
 def body(
@@ -509,41 +521,57 @@
     prefix = prefix_keys.shape[1] * places
     first_half = place < places // 2
 
-    def blocks_of(layer):
+    def attention_blocks(layer):
+        return jnp.stack([w_query[layer], w_key[layer], w_value[layer], w_out[layer]])
+
+    def feed_blocks(layer):
         up = [w_up[layer][:, i * width : (i + 1) * width] for i in range(ratio)]
         down = [w_down[layer][i * rows : (i + 1) * rows] for i in range(ratio)]
-        return (
-            jnp.stack([w_query[layer], w_key[layer], w_value[layer], w_out[layer]]),
-            jnp.stack(up + down),
-        )
-
-    def gather(blocks):
-        share = blocks.shape[0] // places
-        own = lax.dynamic_slice_in_dim(blocks, place * share, share, 0)
-        return [lax.all_gather(own, ("rows", "keys"), axis=0, tiled=True)]
-
-    packs = [blocks_of(layer) for layer in range(LAYERS)]
-    groups = [[gather(part) for part in pack] for pack in packs]
-
-    owner = np.repeat(np.arange(parts), 4)
-    kind = np.tile(np.arange(4), parts)
-    attention_rows = kind * width + owner * rows
-    owner = np.repeat(np.arange(parts), 2 * ratio)
-    part = np.tile(np.arange(2 * ratio), parts)
-    feed_rows = np.where(
-        part < ratio,
-        part * width + owner * rows,
-        wide + owner * rows * ratio + (part - ratio) * rows,
-    )
-
-    def only(*kinds):
-        table = np.full(4 * parts, -1)
-        for i, which in enumerate(kinds):
-            table = np.where(kind == which, attention_rows + (i - which) * width, table)
-        return table
-
-    def as_table(values):
-        return jnp.asarray(values, jnp.int32)
+        return jnp.stack(up + down)
+
+    def share_of(blocks):
+        count = blocks.shape[0] // places
+        return lax.dynamic_slice_in_dim(blocks, place * count, count, 0)
+
+    def gather(*shares):
+        return lax.all_gather(jnp.concatenate(shares, 0), ("rows", "keys"), axis=0, tiled=True)
+
+    first = gather(share_of(attention_blocks(0)), share_of(feed_blocks(0)), share_of(attention_blocks(1)))
+    second = gather(share_of(feed_blocks(1)))
+    each = 2 * ratio // places
+    many = each + 2
+
+    def attention_table(start, size, kinds):
+        return [
+            ((r * places + kind) * size + start, i * width + r * rows)
+            for i, kind in enumerate(kinds)
+            for r in range(parts)
+        ]
+
+    def feed_table(start, size):
+        return [
+            (
+                (r * places + b // each) * size + start + b % each,
+                b * width + r * rows if b < ratio else wide + (r * ratio + b - ratio) * rows,
+            )
+            for b in range(2 * ratio)
+            for r in range(parts)
+        ]
+
+    attention_places = [(first, 0, many), (first, many - 1, many)]
+    feed_places = [(first, 1, many), (second, 0, each)]
+
+    def attention_weights(layer, *kinds):
+        gathered, start, size = attention_places[layer]
+        return [attention_table(start, size, kinds)], [gathered]
+
+    def feed_weights(layer):
+        gathered, start, size = feed_places[layer]
+        return [feed_table(start, size)], [gathered]
+
+    def joined(left, right, offset):
+        moved = [[(i, row + offset) for i, row in table] for table in right[0]]
+        return left[0] + moved, left[1] + right[1]
 
     def exchange(low):
         near = lax.ppermute(low, "keys", xor_pairs(places, 1))
@@ -584,11 +612,10 @@
             prefixes[1, layer],
             gains[0],
             shifts[0],
-            as_table(attention_rows),
-            groups[layer][0],
+            attention_weights(layer, 0, 1, 2, 3),
         )
         hidden, low, normed_two, inverse_two, slope = feed_forward(
-            middle, ff_bias[layer][None], gains[1], shifts[1], as_table(feed_rows), groups[layer][1]
+            middle, ff_bias[layer][None], gains[1], shifts[1], feed_weights(layer)
         )
         saved.append(
             ((normed_one, inverse_one), (normed_two, inverse_two), slope, heads_t, query_t, value8, key_t, attend)
@@ -607,16 +634,15 @@
             slope,
             saved_one,
             gains[0],
-            as_table(np.concatenate([feed_rows, only(3) + 2 * wide * (only(3) >= 0)])),
-            groups[layer][1] + groups[layer][0],
+            joined(feed_weights(layer), attention_weights(layer, 3), 2 * wide),
         )
         query_grad, key_own, value_own, halo, prefix_grad = attention_back(
-            heads_grad, heads_t, query_t, value8, key_t, attend, tokens, prefix, as_table(only(1, 2)), groups[layer][0]
+            heads_grad, heads_t, query_t, value8, key_t, attend, tokens, prefix, attention_weights(layer, 1, 2)
         )
         near = lax.ppermute(halo[:tokens], "keys", xor_pairs(places, 1))
         across = lax.ppermute(halo[tokens : 2 * tokens], "keys", [(1, 2), (2, 1)])
         edge = lax.ppermute(halo[2 * tokens :], "keys", xor_pairs(places, 2)).astype(F32)
-        gradient = input_back(grad_one, query_grad, key_own, value_own, as_table(only(0, 1, 2)), groups[layer][0])
+        gradient = input_back(grad_one, query_grad, key_own, value_own, attention_weights(layer, 0, 1, 2))
         lead = jnp.where(first_half, 0.0, edge)
         tail = jnp.where(first_half, edge, 0.0)
         gradient = (
@@ -625,15 +651,13 @@
             + across.astype(F32)
             + jnp.concatenate([lead, jnp.zeros((tokens - 2 * EDGE, width), F32), tail], 0)
         )
-        share = prefix // places
-        split = prefix_grad.reshape(2, places, share, width).transpose(1, 0, 2, 3)
-        split = lax.all_to_all(split, "keys", 0, 0)
-        prefix_parts[layer] = lax.psum(jnp.sum(split, 0).astype(BF16), "rows").astype(F32)
+        prefix_parts[layer] = prefix_grad
+    prefix_total = sum_prefixes(jnp.stack(prefix_parts))
     return (
         result[None],
         gradient[None],
-        jnp.stack([part[0] for part in prefix_parts]),
-        jnp.stack([part[1] for part in prefix_parts]),
+        prefix_total[:, 0],
+        prefix_total[:, 1],
     )
 
 

time: 602 us -> 480 us (0.80)
  waiting for transfers between devices: 344 us -> 245 us
  local copies, waits for them, and re-layouts: 58.4 us -> 40.9 us
  other arithmetic: 13.1 us -> 6.73 us
  blocking collectives: 11 us -> 17.2 us
    psum x1 -> x0, waiting for transfers between devices: 65.9 us -> none  [body(): lax.psum(jnp.sum(split, 0).astype(BF16), 'rows').astype(F32)]
    all_gather x4 -> x2, waiting for transfers between devices: 278 us -> 212 us  [gather(): lax.all_gather(jnp.concatenate(shares, 0), ('rows', 'keys'), axis=0, tile...]
    unnamed x178 -> x172, local copies, waits for them, and re-layouts: 45.9 us -> 26.5 us
    ppermute x0 -> x5, waiting for transfers between devices: none -> 17.3 us  [the longest x3 9.97 us: sum_prefixes(): lax.ppermute(total.astype(BF16), 'rows', xor_pairs(count, step)).astype(F32)]
    ppermute x2, waiting for transfers between devices: 0.01 us -> 16 us  [exchange(): lax.ppermute(jnp.where(first_half, low[tokens - EDGE:], low[:EDGE]), 'key...]
    all_to_all x2 -> x0, starting transfers between devices: 8.52 us -> none  [body(): split = lax.all_to_all(split, 'keys', 0, 0)]
    all_gather x1, blocking collectives: 11 us -> 17.2 us  [body(): lax.all_gather(jnp.stack([prefix_keys, prefix_values]), 'keys', axis=2, t...]
  transfers between devices with their start and end apart: 19 -> 19, of which waited for: 5 -> 6; matrix products, arithmetic and copies ran while one was open for 4% -> 1% of each run, Pallas kernels for 15% -> 13%
where the time goes in v2:
time: 480 us; the launch traced here: 479 us
  waiting for transfers between devices  245 us (51%)
  Pallas kernels  132 us (28%)
  local copies, waits for them, and re-layouts  40.9 us (9%)
  starting transfers between devices  21.8 us (5%)
  blocking collectives  17.2 us (4%)
  between operations  15.1 us (3%)
  other arithmetic  6.73 us (1%)
    all_gather x2, waiting for transfers between devices, gather(): lax.all_gather(jnp.concatenate(shares, 0), ('rows', 'keys'), axis=0, tile...  212 us
    pallas_call x10, Pallas kernels, call(): pl.pallas_call(partial(kernel, len(pieces)), out_shape=outs, in_specs=[SM...  132 us
    unnamed x172, local copies, waits for them, and re-layouts  26.5 us
    all_gather x1, blocking collectives, body(): lax.all_gather(jnp.stack([prefix_keys, prefix_values]), 'keys', axis=2, t...  17.2 us
    ppermute x2, waiting for transfers between devices, exchange(): lax.ppermute(jnp.where(first_half, low[tokens - EDGE:], low[:EDGE]), 'key...  16 us
    ppermute x3, waiting for transfers between devices, sum_prefixes(): lax.ppermute(total.astype(BF16), 'rows', xor_pairs(count, step)).astype(F32)  9.97 us
  transfers between devices with their start and end apart: 19, of which 6 were waited for; matrix products, arithmetic and copies ran while one was open for 1% of the time, Pallas kernels for 13%

profile of v2, /device:TPU:0, one launch (start us, length us, event | category | flops | bytes accessed | tf_op | source)
XLA Modules:
  0.0 479.4 jit_solution(43309186762773905)
XLA Ops:
  7.2 1.7 slice_bitcast_fusion
  9.6 0.7 fusion.16
  10.4 0.7 fusion.15
  11.1 0.7 fusion.21
  11.8 0.7 fusion.20
  13.3 1.2 fusion.31
  14.5 1.8 fusion.30
  16.3 1.9 fusion.29
  18.2 0.8 fusion.14
  19.0 0.9 slice_dynamic-update-slice_fusion.3
  19.8 0.8 slice_dynamic-update-slice_fusion.2
  20.7 0.8 slice_dynamic-update-slice_fusion.1
  21.5 0.8 slice_dynamic-update-slice_fusion
  22.4 1.1 constant_dynamic-slice_fusion.4
  23.9 1.1 pad_maximum_fusion
  25.1 1.9 constant_dynamic-slice_fusion.5
  28.3 3.8 collective-permute-start.2
  32.3 17.2 %all_gather.11 = bf16[2,2,64,1024]{3,2,1,0:T(8,128)(2,1)S(1)} all-gather(bf16[2,2,16,1024]{3,2,1,0:T(8,128)(2,1)S(1)} %pad_maximum_fusion.1), channel_id=1, replica_groups=mesh['rows'=8,'keys'=4] {'keys'}, dimensions={2}, use_global_device_ids=true | all-gather | bytes 655360 | tf_op jit(solution)/shard_map/all_gather | solution.py:598
  49.7 0.7 slice_bitcast_fusion.12
  52.0 170.7 %all-gather.5.cloned.1.call-done.refs_1_.refs_3_.refs_2_ = bf16[128,128,1024]{2,1,0:T(8,128)(2,1)} async-done(((bf16[4,128,1024]{2,1,0:T(8,128)(2,1)}), bf16[128,128,1024]{2,1,0:T(8,128)(2,1)}) %all-gather.5.cloned.1.call-update) | async-done | bytes 33554448 | tf_op jit(solution)/shard_map/all_gather | solution.py:537
  222.7 19.8 %shard_map.273 = (f32[224,1024]{1,0:T(8,128)S(1)}, f32[224,1024]{1,0:T(8,128)S(1)}, f32[224,1]{1,0:T(8,128)S(1)}, bf16[1024,256]{1,0:T(8,128)(2,1)S(1)}, bf16[8,...) custom-call(s32[64]{0:T(128)S(1)} %copy-done.64, ...), custom_call_target="tpu_custom_call" | custom-call | flops 3758096384 | bytes 11804672 | tf_op jit(solution)/shard_map/pallas_call | solution.py:333
  242.5 1.0 copy-done.9
  243.6 12.4 %shard_map.274 = (f32[224,1024]{1,0:T(8,128)S(1)}, bf16[224,1024]{1,0:T(8,128)(2,1)S(1)}, f32[224,1024]{1,0:T(8,128)S(1)}, f32[224,1]{1,0:T(8,128)S(1)}, bf16[224,4096]{1,0:T(8,128)(2,1)S(1)}) custom-call(s32[128]{0:T(128)S(1)} %copy-done.55, bf16[128,128,1024]{2,1,0:T(8,128)(2,1)} %all-gather.5.cloned.1.call-done.refs_1_.refs_3_.refs_2_, ...), custom_call_target="tpu_custom_call" | custom-call | flops 3758096384 | bytes 17719296 | tf_op jit(solution)/shard_map/pallas_call | solution.py:333
  256.3 0.9 collective-permute-start.4
  257.2 3.2 collective-permute-start.5
  260.5 16.0 %collective-permute-done.5.refs_5_ = bf16[32,1024]{1,0:T(8,128)(2,1)S(1)} collective-permute-done((bf16[32,1024]{1,0:T(8,128)(2,1)S(1)}, bf16[32,1024]{1,0:T(8,128)(2,1)S(1)}, u32[]{:S(2)}, u32[]{:S(2)}) %collective-permute-start.5) | collective-permute-done | bytes 65568 | tf_op jit(solution)/shard_map/ppermute | solution.py:579
  276.5 19.9 %shard_map.275 = (f32[224,1024]{1,0:T(8,128)S(1)}, f32[224,1024]{1,0:T(8,128)S(1)}, f32[224,1]{1,0:T(8,128)S(1)}, bf16[1024,256]{1,0:T(8,128)(2,1)S(1)}, bf16[8,...) custom-call(s32[64]{0:T(128)S(1)} %copy-done.63, ...), custom_call_target="tpu_custom_call" | custom-call | flops 3758096384 | bytes 11804672 | tf_op jit(solution)/shard_map/pallas_call | solution.py:333
  296.5 1.2 copy-done.5
  297.7 1.2 copy-done.7
  298.9 1.0 copy-done.11
  299.9 1.0 copy-done.21
  300.9 0.9 copy-done.23
  301.8 0.8 copy-done.27
  303.2 41.5 %all-gather.3.cloned.1.call-done.refs_1_.refs_2_ = bf16[64,128,1024]{2,1,0:T(8,128)(2,1)} async-done(((bf16[2,128,1024]{2,1,0:T(8,128)(2,1)}), bf16[64,128,1024]{2,1,0:T(8,128)(2,1)}) %all-gather.3.cloned.1.call-update) | async-done | bytes 16777232 | tf_op jit(solution)/shard_map/all_gather | solution.py:537
  344.7 1.2 copy-done.24
  347.9 12.1 %shard_map.276 = (f32[224,1024]{1,0:T(8,128)}, bf16[224,1024]{1,0:T(8,128)(2,1)}, f32[224,1024]{1,0:T(8,128)S(1)}, f32[224,1]{1,0:T(8,128)S(1)}, bf16[224,4096]{1,0:T(8,128)(2,1)S(1)}) custom-call(s32[128]{0:T(128)S(1)} %copy-done.54, bf16[64,128,1024]{2,1,0:T(8,128)(2,1)} %all-gather.3.cloned.1.call-done.refs_1_.refs_2_, f32[224,1024]{1,0:T(8,128)S(1)} %copy-done.24, ...), custom_call_target="tpu_custom_call" | custom-call | flops 3758096384 | bytes 17719296 | tf_op jit(solution)/shard_map/pallas_call | solution.py:333
  360.2 16.7 %shard_map.277 = (f32[224,1024]{1,0:T(8,128)S(1)}, bf16[1024,256]{1,0:T(8,128)(2,1)S(1)}) custom-call(s32[128]{0:T(128)S(1)} %copy-done.54, s32[16]{0:T(128)S(1)} %copy-done.61, bf16[64,128,1024]{2,1,0:T(8,128)(2,1)} %all-gather.3.cloned.1.call-done.refs_1_.refs_2_, bf16[128,128,1024]{2,1,0:T(8,128)(2,1)} %all-gather.5.cloned.1.call-done.refs_1_.refs_3_.refs_2_, ...), custom_call_target="tpu_custom_call" | custom-call | flops 4227858432 | bytes 23471872 | tf_op jit(solution)/shard_map/pallas_call | solution.py:333
  377.0 0.9 copy-done.19
  377.9 11.3 %shard_map.278 = (bf16[224,1024]{1,0:T(8,128)(2,1)S(1)}, bf16[224,1024]{1,0:T(8,128)(2,1)S(1)}, bf16[224,1024]{1,0:T(8,128)(2,1)S(1)}, bf16[480,1024]{1,0:T(8,128)(2,1)S(1)}, f32[2,64,1024]{2,1,0:T(8,128)S(1)}) custom-call(s32[32]{0:T(128)S(1)} %copy-done.60, bf16[128,128,1024]{2,1,0:T(8,128)(2,1)} %all-gather.5.cloned.1.call-done.refs_1_.refs_3_.refs_2_, ...), custom_call_target="tpu_custom_call" | custom-call | flops 2818572288 | bytes 9437184 | tf_op jit(solution)/shard_map/pallas_call | solution.py:333
  389.3 0.8 copy-done.31
  390.1 0.8 copy-done.33
  390.9 0.8 copy-done.35
  391.6 1.0 fusion.28
  392.7 1.4 collective-permute-start.7
  394.1 2.1 collective-permute-start.6
  396.9 1.2 copy-done.20
  398.1 1.0 copy-done.32
  399.1 1.0 copy-done.34
  400.1 1.0 copy-done.36
  401.2 5.9 %shard_map.279 = f32[224,1024]{1,0:T(8,128)S(1)} custom-call(s32[48]{0:T(128)S(1)} %copy-done.59, bf16[128,128,1024]{2,1,0:T(8,128)(2,1)} %all-gather.5.cloned.1.call-done.refs_1_.refs_3_.refs_2_, f32[224,1024]{1,0:T(8,128)S(1)} %copy-done.20, bf16[224,1024]{1,0:T(8,128)(2,1)S(1)} %copy-done.32, bf16[224,1024]{1,0:T(8,128)(2,1)S(1)} %copy-done.34, ...), custom_call_target="tpu_custom_call" | custom-call | flops 1409286144 | bytes 8585216 | tf_op jit(solution)/shard_map/pallas_call | solution.py:333
  407.2 1.5 maximum_add_fusion.refs_4_
  408.9 16.8 %shard_map.280 = (f32[224,1024]{1,0:T(8,128)S(1)}, bf16[1024,256]{1,0:T(8,128)(2,1)S(1)}) custom-call(s32[128]{0:T(128)S(1)} %copy-done.56, s32[16]{0:T(128)S(1)} %copy-done.62, bf16[128,128,1024]{2,1,0:T(8,128)(2,1)} %all-gather.5.cloned.1.call-done.refs_1_.refs_3_.refs_2_, bf16[128,128,1024]{2,1,0:T(8,128)(2,1)} %all-gather.5.cloned.1.call-done.refs_1_.refs_3_.refs_2_, ...), custom_call_target="tpu_custom_call" | custom-call | flops 4227858432 | bytes 23471872 | tf_op jit(solution)/shard_map/pallas_call | solution.py:333
  425.8 11.3 %shard_map.281 = (bf16[224,1024]{1,0:T(8,128)(2,1)S(1)}, bf16[224,1024]{1,0:T(8,128)(2,1)S(1)}, bf16[224,1024]{1,0:T(8,128)(2,1)S(1)}, bf16[480,1024]{1,0:T(8,128)(2,1)S(1)}, f32[2,64,1024]{2,1,0:T(8,128)S(1)}) custom-call(s32[32]{0:T(128)S(1)} %copy-done.58, bf16[128,128,1024]{2,1,0:T(8,128)(2,1)} %all-gather.5.cloned.1.call-done.refs_1_.refs_3_.refs_2_, ...), custom_call_target="tpu_custom_call" | custom-call | flops 2818572288 | bytes 9437184 | tf_op jit(solution)/shard_map/pallas_call | solution.py:333
  437.2 0.7 fusion.7
  437.9 1.5 collective-permute-start.12
  440.0 7.3 %collective-permute-done.12 = bf16[2,2,32,1024]{3,2,1,0:T(8,128)(2,1)} collective-permute-done((bf16[2,2,32,1024]{3,2,1,0:T(8,128)(2,1)}, bf16[2,2,32,1024]{3,2,1,0:T(8,128)(2,1)}, u32[]{:S(2)}, u32[]{:S(2)}) %collective-permute-start.12) | collective-permute-done | bytes 262176 | tf_op jit(solution)/shard_map/ppermute | solution.py:488
  447.3 1.0 fusion.6
  449.2 2.5 collective-permute-start.9
  451.7 0.9 collective-permute-start.14
  452.6 5.9 %shard_map.282 = f32[224,1024]{1,0:T(8,128)S(1)} custom-call(s32[48]{0:T(128)S(1)} %copy-done.57, bf16[128,128,1024]{2,1,0:T(8,128)(2,1)} %all-gather.5.cloned.1.call-done.refs_1_.refs_3_.refs_2_, f32[224,1024]{1,0:T(8,128)S(1)} %copy-done.18, bf16[224,1024]{1,0:T(8,128)(2,1)S(1)} %get-tuple-element.76.refs_3_, ...), custom_call_target="tpu_custom_call" | custom-call | flops 1409286144 | bytes 8585216 | tf_op jit(solution)/shard_map/pallas_call | solution.py:333
  459.1 4.7 collective-permute-done.15
  463.9 1.5 collective-permute-start.16
  465.4 1.1 fusion
  466.5 5.3 %collective-permute-done.16 = bf16[2,2,16,1024]{3,2,1,0:T(8,128)(2,1)S(1)} collective-permute-done((bf16[2,2,16,1024]{3,2,1,0:T(8,128)(2,1)S(1)}, bf16[2,2,16,1024]{3,2,1,0:T(8,128)(2,1)S(1)}, u32[]{:S(2)}, u32[]{:S(2)}) %collective-permute-start.16) | collective-permute-done | bytes 131104 | tf_op jit(solution)/shard_map/ppermute | solution.py:493
  (203 shorter events, 12.2 us)
Async XLA Ops:
  7.2 215.5 %all-gather.5.cloned.1.call-start = ((), (), s32[]{:S(2)}) async-start(), calls=%async_computation.1 | async-start | bytes 34603008 | tf_op jit(solution)/shard_map/all_gather | solution.py:537
  23.9 8.4 %copy-start.71 = (bf16[2,16,1024]{2,1,0:T(8,128)(2,1)S(1)}, bf16[2,16,1024]{2,1,0:T(8,128)(2,1)}, u32[]{:S(2)}) copy-start(bf16[2,16,1024]{2,1,0:T(8,128)(2,1)} %param.29) | copy-start | bytes 196612
  25.0 25.4 %copy-start.73 = (f32[2,4096]{1,0:T(2,128)S(1)}, f32[2,4096]{1,0:T(2,128)}, u32[]{:S(2)}) copy-start(f32[2,4096]{1,0:T(2,128)} %param.35) | copy-start | bytes 98308
  25.0 26.0 %copy-start.74 = (f32[2,2,1024]{2,1,0:T(2,128)S(1)}, f32[2,2,1024]{2,1,0:T(2,128)}, u32[]{:S(2)}) copy-start(f32[2,2,1024]{2,1,0:T(2,128)} %param.38) | copy-start | bytes 49156
  25.1 26.0 %copy-start.75 = (f32[2,2,1024]{2,1,0:T(2,128)S(1)}, f32[2,2,1024]{2,1,0:T(2,128)}, u32[]{:S(2)}) copy-start(f32[2,2,1024]{2,1,0:T(2,128)} %param.37) | copy-start | bytes 49156
  25.1 319.7 %all-gather.3.cloned.1.call-start = ((), (), s32[]{:S(2)}) async-start(), calls=%async_computation | async-start | bytes 17301504 | tf_op jit(solution)/shard_map/all_gather | solution.py:537
  27.0 24.9 %collective-permute-start = (bf16[224,1024]{1,0:T(8,128)(2,1)S(1)}, bf16[224,1024]{1,0:T(8,128)(2,1)S(1)}, u32[]{:S(2)}, u32[]{:S(2)}) collective-permute-start(bf16[224,1024]{1,0:T(8,128)(2,1)S(1)} %bitcast.114), channel_id=1, source_target_pairs={{0,1},{1,0},{2,3},{3,2},{4,5},{5,4},{6,7},{7,6},{8,9},{9,8},{10,11... | collective-permute-start | bytes 1376264 | tf_op jit(solution)/shard_map/ppermute | solution.py:577
  27.6 24.4 %collective-permute-start.1 = (bf16[224,1024]{1,0:T(8,128)(2,1)S(1)}, bf16[224,1024]{1,0:T(8,128)(2,1)S(1)}, u32[]{:S(2)}, u32[]{:S(2)}) collective-permute-start(bf16[224,1024]{1,0:T(8,128)(2,1)S(1)} %bitcast.115), channel_id=1, source_target_pairs={{1,2},{2,1},{5,6},{6,5},{9,10},{10,9},{13,14},{14,13},{17,18},{18,... | collective-permute-start | bytes 1376264 | tf_op jit(solution)/shard_map/ppermute | solution.py:578
  28.3 23.7 %collective-permute-start.2 = (bf16[32,1024]{1,0:T(8,128)(2,1)S(1)}, bf16[32,1024]{1,0:T(8,128)(2,1)S(1)}, u32[]{:S(2)}, u32[]{:S(2)}) collective-permute-start(bf16[32,1024]{1,0:T(8,128)(2,1)S(1)} %select_bitcast_fusion), channel_id=1, source_target_pairs={{0,2},{1,3},{2,0},{3,1},{4,6},{5,7},{6,4},{7,5},{8,10},{9,11},{10,... | collective-permute-start | bytes 196616 | tf_op jit(solution)/shard_map/ppermute | solution.py:579
  50.5 172.2 %copy-start.64 = (s32[64]{0:T(128)S(1)}, s32[64]{0:T(128)}, u32[]{:S(2)}) copy-start(s32[64]{0:T(128)} %constant.101.clone.refs_0_) | copy-start | bytes 772
  51.7 190.7 %copy-start.44 = (f32[1,1024]{1,0:T(1,128)}, f32[1,1024]{1,0:T(1,128)S(1)}, u32[]{:S(2)}) copy-start(f32[1,1024]{1,0:T(1,128)S(1)} %get-tuple-element.132.refs_10_.refs_11_) | copy-start | bytes 12292
  222.7 20.8 %copy-start.46 = (f32[1,1024]{1,0:T(1,128)S(1)}, f32[1,1024]{1,0:T(1,128)}, u32[]{:S(2)}) copy-start(f32[1,1024]{1,0:T(1,128)} %get-tuple-element.133.refs_4_.refs_7_) | copy-start | bytes 12292
  222.7 20.8 %copy-start.52 = (f32[1,1024]{1,0:T(1,128)S(1)}, f32[1,1024]{1,0:T(1,128)}, u32[]{:S(2)}) copy-start(f32[1,1024]{1,0:T(1,128)} %get-tuple-element.117.refs_5_) | copy-start | bytes 12292
  222.7 20.8 %copy-start.55 = (s32[128]{0:T(128)S(1)}, s32[128]{0:T(128)}, u32[]{:S(2)}) copy-start(s32[128]{0:T(128)} %constant.102.clone.refs_0_) | copy-start | bytes 1540
  243.4 12.5 %copy-start.1 = (bf16[8,768,128]{2,1,0:T(8,128)(2,1)}, bf16[8,768,128]{2,1,0:T(8,128)(2,1)S(1)}, u32[]{:S(2)}) copy-start(bf16[8,768,128]{2,1,0:T(8,128)(2,1)S(1)} %get-tuple-element.73.refs_5_) | copy-start | bytes 4718596
  243.4 12.5 %copy-start.3 = (bf16[1024,768]{1,0:T(8,128)(2,1)}, bf16[1024,768]{1,0:T(8,128)(2,1)S(1)}, u32[]{:S(2)}) copy-start(bf16[1024,768]{1,0:T(8,128)(2,1)S(1)} %get-tuple-element.74.refs_6_) | copy-start | bytes 4718596
  243.4 12.5 %copy-start.13 = (f32[224,1024]{1,0:T(8,128)}, f32[224,1024]{1,0:T(8,128)S(1)}, u32[]{:S(2)}) copy-start(f32[224,1024]{1,0:T(8,128)S(1)} %get-tuple-element.67.refs_9_) | copy-start | bytes 2752516
  243.5 12.5 %copy-start.25 = (bf16[1024,256]{1,0:T(8,128)(2,1)}, bf16[1024,256]{1,0:T(8,128)(2,1)S(1)}, u32[]{:S(2)}) copy-start(bf16[1024,256]{1,0:T(8,128)(2,1)S(1)} %get-tuple-element.72.refs_4_) | copy-start | bytes 1572868
  243.5 12.5 %copy-start.37 = (f32[224,1]{1,0:T(8,128)}, f32[224,1]{1,0:T(8,128)S(1)}, u32[]{:S(2)}) copy-start(f32[224,1]{1,0:T(8,128)S(1)} %get-tuple-element.68.refs_10_) | copy-start | bytes 2692
  243.5 16.9 %copy-start.70 = (bf16[1,224,1024]{2,1,0:T(8,128)(2,1)S(1)}, bf16[1,224,1024]{2,1,0:T(8,128)(2,1)}, u32[]{:S(2)}) copy-start(bf16[1,224,1024]{2,1,0:T(8,128)(2,1)} %param.39) | copy-start | bytes 1376260
  243.5 33.0 %copy-start.29 = (bf16[64,1024]{1,0:T(8,128)(2,1)S(1)}, bf16[64,1024]{1,0:T(8,128)(2,1)}, u32[]{:S(2)}) copy-start(bf16[64,1024]{1,0:T(8,128)(2,1)} %get-tuple-element.96.refs_9_) | copy-start | bytes 393220
  243.5 33.0 %copy-start.30 = (bf16[64,1024]{1,0:T(8,128)(2,1)S(1)}, bf16[64,1024]{1,0:T(8,128)(2,1)}, u32[]{:S(2)}) copy-start(bf16[64,1024]{1,0:T(8,128)(2,1)} %get-tuple-element.97.refs_8_) | copy-start | bytes 393220
  243.5 33.0 %copy-start.48 = (f32[1,1024]{1,0:T(1,128)S(1)}, f32[1,1024]{1,0:T(1,128)}, u32[]{:S(2)}) copy-start(f32[1,1024]{1,0:T(1,128)} %get-tuple-element.131.refs_10_.refs_11_) | copy-start | bytes 12292
  243.5 33.0 %copy-start.51 = (f32[1,1024]{1,0:T(1,128)S(1)}, f32[1,1024]{1,0:T(1,128)}, u32[]{:S(2)}) copy-start(f32[1,1024]{1,0:T(1,128)} %get-tuple-element.119.refs_11_) | copy-start | bytes 12292
  243.6 33.0 %copy-start.63 = (s32[64]{0:T(128)S(1)}, s32[64]{0:T(128)}, u32[]{:S(2)}) copy-start(s32[64]{0:T(128)} %constant.103.clone.refs_0_) | copy-start | bytes 772
  256.0 20.5 %copy-start.15 = (f32[224,1024]{1,0:T(8,128)}, f32[224,1024]{1,0:T(8,128)S(1)}, u32[]{:S(2)}) copy-start(f32[224,1024]{1,0:T(8,128)S(1)} %get-tuple-element.64.refs_5_) | copy-start | bytes 2752516
  256.0 20.5 %copy-start.39 = (f32[224,1]{1,0:T(8,128)}, f32[224,1]{1,0:T(8,128)S(1)}, u32[]{:S(2)}) copy-start(f32[224,1]{1,0:T(8,128)S(1)} %get-tuple-element.65.refs_6_) | copy-start | bytes 2692
  256.0 20.4 %collective-permute-start.3 = (bf16[224,1024]{1,0:T(8,128)(2,1)S(1)}, bf16[224,1024]{1,0:T(8,128)(2,1)S(1)}, u32[]{:S(2)}, u32[]{:S(2)}) collective-permute-start(bf16[224,1024]{1,0:T(8,128)(2,1)S(1)} %get-tuple-element.44.refs_2_), channel_id=1, source_target_pairs={{0,1},{1,0},{2,3},{3,2},{4,5},{5,4},{6,7},{7,6},{8,9},{9,8},{10,11... | collective-permute-start | bytes 1376264 | tf_op jit(solution)/shard_map/ppermute | solution.py:577
  256.3 20.1 %collective-permute-start.4 = (bf16[224,1024]{1,0:T(8,128)(2,1)S(1)}, bf16[224,1024]{1,0:T(8,128)(2,1)S(1)}, u32[]{:S(2)}, u32[]{:S(2)}) collective-permute-start(bf16[224,1024]{1,0:T(8,128)(2,1)S(1)} %get-tuple-element.44.refs_2_), channel_id=1, source_target_pairs={{1,2},{2,1},{5,6},{6,5},{9,10},{10,9},{13,14},{14,13},{17,18},{18,... | collective-permute-start | bytes 1376264 | tf_op jit(solution)/shard_map/ppermute | solution.py:578
  257.2 19.2 %collective-permute-start.5 = (bf16[32,1024]{1,0:T(8,128)(2,1)S(1)}, bf16[32,1024]{1,0:T(8,128)(2,1)S(1)}, u32[]{:S(2)}, u32[]{:S(2)}) collective-permute-start(bf16[32,1024]{1,0:T(8,128)(2,1)S(1)} %slice_select_fusion), channel_id=1, source_target_pairs={{0,2},{1,3},{2,0},{3,1},{4,6},{5,7},{6,4},{7,5},{8,10},{9,11},{10,... | collective-permute-start | bytes 196616 | tf_op jit(solution)/shard_map/ppermute | solution.py:579
  276.5 68.2 %copy-start.43 = (f32[1,4096]{1,0:T(1,128)S(1)}, f32[1,4096]{1,0:T(1,128)}, u32[]{:S(2)}) copy-start(f32[1,4096]{1,0:T(1,128)} %get-tuple-element.114.refs_3_) | copy-start | bytes 49156
  347.9 12.2 %copy-start.22 = (f32[224,1024]{1,0:T(8,128)S(1)}, f32[224,1024]{1,0:T(8,128)}, u32[]{:S(2)}) copy-start(f32[224,1024]{1,0:T(8,128)} %copy-done.21) | copy-start | bytes 2752516
  347.9 12.2 %copy-start.42 = (f32[224,1]{1,0:T(8,128)S(1)}, f32[224,1]{1,0:T(8,128)}, u32[]{:S(2)}) copy-start(f32[224,1]{1,0:T(8,128)} %copy-done.41) | copy-start | bytes 2692
  347.9 12.2 %copy-start.49 = (f32[1,1024]{1,0:T(1,128)S(1)}, f32[1,1024]{1,0:T(1,128)}, u32[]{:S(2)}) copy-start(f32[1,1024]{1,0:T(1,128)} %get-tuple-element.131.refs_10_.refs_11_) | copy-start | bytes 12292
  347.9 12.2 %copy-start.61 = (s32[16]{0:T(128)S(1)}, s32[16]{0:T(128)}, u32[]{:S(2)}) copy-start(s32[16]{0:T(128)} %constant.105.clone.refs_1_) | copy-start | bytes 196
  360.1 17.8 %slice-start.2 = ((s8[6291456]{0:T(1024)(128)(4,1)}), s8[4194304]{0:T(1024)(128)(4,1)S(1)}, s32[]{:S(2)}) async-start(s8[6291456]{0:T(1024)(128)(4,1)} %bitcast.112), calls=%async_computation.4 | async-start | bytes 8388608
  360.1 17.7 %slice-start.3 = ((s8[6291456]{0:T(1024)(128)(4,1)}), s8[2097152]{0:T(1024)(128)(4,1)S(1)}, s32[]{:S(2)}) async-start(s8[6291456]{0:T(1024)(128)(4,1)} %bitcast.112), calls=%async_computation.5 | async-start | bytes 4194304
  360.1 17.7 %copy-start.6 = (bf16[8,768,128]{2,1,0:T(8,128)(2,1)S(1)}, bf16[8,768,128]{2,1,0:T(8,128)(2,1)}, u32[]{:S(2)}) copy-start(bf16[8,768,128]{2,1,0:T(8,128)(2,1)} %copy-done.5) | copy-start | bytes 4718596
  360.2 17.7 %copy-start.8 = (bf16[1024,768]{1,0:T(8,128)(2,1)S(1)}, bf16[1024,768]{1,0:T(8,128)(2,1)}, u32[]{:S(2)}) copy-start(bf16[1024,768]{1,0:T(8,128)(2,1)} %copy-done.7) | copy-start | bytes 4718596
  360.2 17.7 %copy-start.12 = (f32[1024,256]{1,0:T(8,128)S(1)}, f32[1024,256]{1,0:T(8,128)}, u32[]{:S(2)}) copy-start(f32[1024,256]{1,0:T(8,128)} %copy-done.11) | copy-start | bytes 3145732
  360.2 17.7 %copy-start.28 = (bf16[1024,256]{1,0:T(8,128)(2,1)S(1)}, bf16[1024,256]{1,0:T(8,128)(2,1)}, u32[]{:S(2)}) copy-start(bf16[1024,256]{1,0:T(8,128)(2,1)} %copy-done.27) | copy-start | bytes 1572868
  360.2 17.7 %copy-start.60 = (s32[32]{0:T(128)S(1)}, s32[32]{0:T(128)}, u32[]{:S(2)}) copy-start(s32[32]{0:T(128)} %constant.106.clone.refs_0_) | copy-start | bytes 388
  377.9 19.0 %copy-start.59 = (s32[48]{0:T(128)S(1)}, s32[48]{0:T(128)}, u32[]{:S(2)}) copy-start(s32[48]{0:T(128)} %constant.107.clone.refs_0_) | copy-start | bytes 580
  392.7 14.5 %collective-permute-start.7 = (bf16[224,1024]{1,0:T(8,128)(2,1)}, bf16[224,1024]{1,0:T(8,128)(2,1)}, u32[]{:S(2)}, u32[]{:S(2)}) collective-permute-start(bf16[224,1024]{1,0:T(8,128)(2,1)} %get-tuple-element.95), channel_id=1, source_target_pairs={{1,2},{2,1},{5,6},{6,5},{9,10},{10,9},{13,14},{14,13},{17,18},{18,... | collective-permute-start | bytes 1376264 | tf_op jit(solution)/shard_map/ppermute | solution.py:643
  394.1 13.1 %collective-permute-start.6 = (bf16[224,1024]{1,0:T(8,128)(2,1)}, bf16[224,1024]{1,0:T(8,128)(2,1)}, u32[]{:S(2)}, u32[]{:S(2)}) collective-permute-start(bf16[224,1024]{1,0:T(8,128)(2,1)} %get-tuple-element.94), channel_id=1, source_target_pairs={{0,1},{1,0},{2,3},{3,2},{4,5},{5,4},{6,7},{7,6},{8,9},{9,8},{10,11... | collective-permute-start | bytes 1376264 | tf_op jit(solution)/shard_map/ppermute | solution.py:642
  396.4 10.8 %collective-permute-start.8 = (bf16[32,1024]{1,0:T(8,128)(2,1)S(1)}, bf16[32,1024]{1,0:T(8,128)(2,1)S(1)}, u32[]{:S(2)}, u32[]{:S(2)}) collective-permute-start(bf16[32,1024]{1,0:T(8,128)(2,1)S(1)} %slice.260), channel_id=1, source_target_pairs={{0,2},{1,3},{2,0},{3,1},{4,6},{5,7},{6,4},{7,5},{8,10},{9,11},{10,... | collective-permute-start | bytes 196616 | tf_op jit(solution)/shard_map/ppermute | solution.py:644
  408.7 17.0 %slice-start = ((s8[6291456]{0:T(1024)(128)(4,1)}), s8[4194304]{0:T(1024)(128)(4,1)S(1)}, s32[]{:S(2)}) async-start(s8[6291456]{0:T(1024)(128)(4,1)} %bitcast.110), calls=%async_computation.2 | async-start | bytes 8388608
  408.9 16.9 %slice-start.1 = ((s8[6291456]{0:T(1024)(128)(4,1)}), s8[2097152]{0:T(1024)(128)(4,1)S(1)}, s32[]{:S(2)}) async-start(s8[6291456]{0:T(1024)(128)(4,1)} %bitcast.110), calls=%async_computation.3 | async-start | bytes 4194304
  408.9 16.9 %copy-start.2 = (bf16[8,768,128]{2,1,0:T(8,128)(2,1)S(1)}, bf16[8,768,128]{2,1,0:T(8,128)(2,1)}, u32[]{:S(2)}) copy-start(bf16[8,768,128]{2,1,0:T(8,128)(2,1)} %copy-done.1) | copy-start | bytes 4718596
  408.9 16.9 %copy-start.4 = (bf16[1024,768]{1,0:T(8,128)(2,1)S(1)}, bf16[1024,768]{1,0:T(8,128)(2,1)}, u32[]{:S(2)}) copy-start(bf16[1024,768]{1,0:T(8,128)(2,1)} %copy-done.3) | copy-start | bytes 4718596
  408.9 16.9 %copy-start.10 = (f32[1024,256]{1,0:T(8,128)S(1)}, f32[1024,256]{1,0:T(8,128)}, u32[]{:S(2)}) copy-start(f32[1024,256]{1,0:T(8,128)} %copy-done.9) | copy-start | bytes 3145732
  408.9 16.9 %copy-start.26 = (bf16[1024,256]{1,0:T(8,128)(2,1)S(1)}, bf16[1024,256]{1,0:T(8,128)(2,1)}, u32[]{:S(2)}) copy-start(bf16[1024,256]{1,0:T(8,128)(2,1)} %copy-done.25) | copy-start | bytes 1572868
  408.9 16.9 %copy-start.58 = (s32[32]{0:T(128)S(1)}, s32[32]{0:T(128)}, u32[]{:S(2)}) copy-start(s32[32]{0:T(128)} %constant.109.clone.refs_0_) | copy-start | bytes 388
  425.7 11.4 %copy-start.17 = (f32[224,1024]{1,0:T(8,128)}, f32[224,1024]{1,0:T(8,128)S(1)}, u32[]{:S(2)}) copy-start(f32[224,1024]{1,0:T(8,128)S(1)} %get-tuple-element.69.refs_2_) | copy-start | bytes 2752516
  437.9 9.4 %collective-permute-start.12 = (bf16[2,2,32,1024]{3,2,1,0:T(8,128)(2,1)}, bf16[2,2,32,1024]{3,2,1,0:T(8,128)(2,1)}, u32[]{:S(2)}, u32[]{:S(2)}) collective-permute-start(bf16[2,2,32,1024]{3,2,1,0:T(8,128)(2,1)} %fusion.7), channel_id=1, source_target_pairs={{0,2},{1,3},{2,0},{3,1},{4,6},{5,7},{6,4},{7,5},{8,10},{9,11},{10,... | collective-permute-start | bytes 786440 | tf_op jit(solution)/shard_map/ppermute | solution.py:488
  439.4 13.2 %copy-start.18 = (f32[224,1024]{1,0:T(8,128)S(1)}, f32[224,1024]{1,0:T(8,128)}, u32[]{:S(2)}) copy-start(f32[224,1024]{1,0:T(8,128)} %copy-done.17) | copy-start | bytes 2752516
  439.4 13.2 %copy-start.57 = (s32[48]{0:T(128)S(1)}, s32[48]{0:T(128)}, u32[]{:S(2)}) copy-start(s32[48]{0:T(128)} %constant.110.clone.refs_0_) | copy-start | bytes 580
  439.4 19.7 %collective-permute-start.11 = (bf16[32,1024]{1,0:T(8,128)(2,1)S(1)}, bf16[32,1024]{1,0:T(8,128)(2,1)S(1)}, u32[]{:S(2)}, u32[]{:S(2)}) collective-permute-start(bf16[32,1024]{1,0:T(8,128)(2,1)S(1)} %slice.263), channel_id=1, source_target_pairs={{0,2},{1,3},{2,0},{3,1},{4,6},{5,7},{6,4},{7,5},{8,10},{9,11},{10,... | collective-permute-start | bytes 196616 | tf_op jit(solution)/shard_map/ppermute | solution.py:644
  448.4 3.3 collective-permute-start.13
  448.5 16.9 %collective-permute-start.10 = (bf16[224,1024]{1,0:T(8,128)(2,1)S(1)}, bf16[224,1024]{1,0:T(8,128)(2,1)S(1)}, u32[]{:S(2)}, u32[]{:S(2)}) collective-permute-start(bf16[224,1024]{1,0:T(8,128)(2,1)S(1)} %get-tuple-element.93), channel_id=1, source_target_pairs={{1,2},{2,1},{5,6},{6,5},{9,10},{10,9},{13,14},{14,13},{17,18},{18,... | collective-permute-start | bytes 1376264 | tf_op jit(solution)/shard_map/ppermute | solution.py:643
  449.2 16.2 %collective-permute-start.9 = (bf16[224,1024]{1,0:T(8,128)(2,1)S(1)}, bf16[224,1024]{1,0:T(8,128)(2,1)S(1)}, u32[]{:S(2)}, u32[]{:S(2)}) collective-permute-start(bf16[224,1024]{1,0:T(8,128)(2,1)S(1)} %get-tuple-element.92), channel_id=1, source_target_pairs={{0,1},{1,0},{2,3},{3,2},{4,5},{5,4},{6,7},{7,6},{8,9},{9,8},{10,11... | collective-permute-start | bytes 1376264 | tf_op jit(solution)/shard_map/ppermute | solution.py:642
  451.7 6.8 %collective-permute-start.14 = (bf16[2,2,16,1024]{3,2,1,0:T(8,128)(2,1)S(1)}, bf16[2,2,16,1024]{3,2,1,0:T(8,128)(2,1)S(1)}, u32[]{:S(2)}, u32[]{:S(2)}) collective-permute-start(bf16[2,2,16,1024]{3,2,1,0:T(8,128)(2,1)S(1)} %fusion.26), channel_id=1, source_target_pairs={{0,4},{4,0},{8,12},{12,8},{16,20},{20,16},{24,28},{28,24},{1,5},{5... | collective-permute-start | bytes 393224 | tf_op jit(solution)/shard_map/ppermute | solution.py:493
  458.6 5.2 %collective-permute-start.15 = (bf16[2,2,16,1024]{3,2,1,0:T(8,128)(2,1)S(1)}, bf16[2,2,16,1024]{3,2,1,0:T(8,128)(2,1)S(1)}, u32[]{:S(2)}, u32[]{:S(2)}) collective-permute-start(bf16[2,2,16,1024]{3,2,1,0:T(8,128)(2,1)S(1)} %fusion.22), channel_id=1, source_target_pairs={{0,8},{4,12},{8,0},{12,4},{16,24},{20,28},{24,16},{28,20},{1,9},{5... | collective-permute-start | bytes 393224 | tf_op jit(solution)/shard_map/ppermute | solution.py:493
  463.9 7.9 %collective-permute-start.16 = (bf16[2,2,16,1024]{3,2,1,0:T(8,128)(2,1)S(1)}, bf16[2,2,16,1024]{3,2,1,0:T(8,128)(2,1)S(1)}, u32[]{:S(2)}, u32[]{:S(2)}) collective-permute-start(bf16[2,2,16,1024]{3,2,1,0:T(8,128)(2,1)S(1)} %fusion.24), channel_id=1, source_target_pairs={{0,16},{4,20},{8,24},{12,28},{16,0},{20,4},{24,8},{28,12},{1,17},{... | collective-permute-start | bytes 393224 | tf_op jit(solution)/shard_map/ppermute | solution.py:493
  (36 other events, 72.7 us)
Sparse Core Ops, SparseCore 0:
  25.2 197.4 all-gather.4
  225.5 119.1 all-gather.2

commit v3 on v2

v3 whole, which is shorter than its diff:
```python
from functools import partial

import jax
import jax.numpy as jnp
import numpy as np
from jax import lax
from jax.experimental import pallas as pl
from jax.experimental.pallas import tpu as pltpu
from jax.sharding import PartitionSpec as P

H = 16
HD = 64
LAYERS = 2
PAIRS = H // 2
EDGE = 32
LANES = 256
NORM_EPSILON = 1e-05
MASKED_SCORE = -1000000000.0
SCORE_SCALE = 0.125
F32 = jnp.float32
BF16 = jnp.bfloat16
MIB = 1 << 20


def nn(a, b):
    return lax.dot_general(a, b, (((1,), (0,)), ((), ())), preferred_element_type=F32)


def nt(a, b):
    return lax.dot_general(a, b, (((1,), (1,)), ((), ())), preferred_element_type=F32)


def ds(start, size):
    return pl.ds(pl.multiple_of(start, size), size)


def layer_norm(hidden, gain, shift):
    centered = hidden - jnp.mean(hidden, -1, keepdims=True)
    inverse = lax.rsqrt(jnp.mean(centered * centered, -1, keepdims=True) + NORM_EPSILON)
    normed = centered * inverse
    return normed * gain + shift, normed, inverse


def norm_back(grad_out, gain, normed, inverse):
    scaled = grad_out * gain
    return inverse * (
        scaled
        - jnp.mean(scaled, -1, keepdims=True)
        - normed * jnp.mean(scaled * normed, -1, keepdims=True)
    )


class Loads:
    def __init__(self, sems):
        self.sems, self.copies, self.count = sems, {}, 0

    def start(self, name, source, target):
        copy = pltpu.make_async_copy(source, target, self.sems.at[self.count])
        copy.start()
        self.copies[name] = copy
        self.count += 1

    def wait(self, *names):
        for name in names:
            copy = self.copies.pop(name, None)
            if copy is not None:
                copy.wait()


def square(ref, columns=slice(None)):
    block = ref[:, :, columns]
    return block.reshape(block.shape[0] * block.shape[1], block.shape[2])


def load_attention(loads, gathered, start, kinds, weights):
    for i, kind in enumerate(kinds):
        loads.start(("square", kind), gathered.at[:, kind, start], weights.at[i])


def load_up(loads, gathered, start, up):
    each = up.shape[0] // (gathered.shape[1] // 2)
    for b in range(up.shape[0]):
        loads.start(("up", b), gathered.at[:, b // each, start + b % each], up.at[b])


def load_down(loads, gathered, start, down):
    half, each = down.shape[1:3]
    for r in range(down.shape[0]):
        loads.start(("down", r), gathered.at[r, pl.ds(half, half), pl.ds(start, each)], down.at[r])


def pair_blocks(half):
    zero = jnp.zeros((HD, LANES), half.dtype)
    return jnp.concatenate(
        [
            jnp.concatenate([half[:HD], zero], 1),
            jnp.concatenate([zero, half[HD:]], 1),
        ],
        0,
    )


def attention_kernel(start, *refs):
    (gathered, own, near, across, edge, residual, bias, prefix_k, prefix_v, gain, shift) = refs[:11]
    (middle, normed, inverse, query_t, value8, key_t, attend, heads_t) = refs[11:19]
    (weights, window, key8, value_t, scores, sems) = refs[19:]
    tokens, width = own.shape
    keys = key8.shape[1]
    loads = Loads(sems)
    load_attention(loads, gathered, start, range(4), weights)
    window[pl.ds(0, tokens)] = own[...]
    window[pl.ds(tokens, tokens)] = near[...]
    window[pl.ds(2 * tokens, tokens)] = across[...]
    window[pl.ds(3 * tokens, EDGE)] = edge[...]
    pad = jnp.zeros((LANES - tokens, 256), BF16)
    for kind in range(3):
        loads.wait(("square", kind))

    def tile(j, carry):
        columns = ds(j * 256, 256)
        query = (SCORE_SCALE * nn(own[...], square(weights.at[0], columns))).astype(BF16)
        query_t[columns, :] = jnp.concatenate([query, pad], 0).T
        for kind, prefix, split, turned in ((1, prefix_k, key8, key_t), (2, prefix_v, value8, value_t)):
            local = nn(window[...], square(weights.at[kind], columns)).astype(BF16)
            whole = jnp.concatenate([local, prefix[:, columns]], 0)
            split[2 * j] = whole[:, :128]
            split[2 * j + 1] = whole[:, 128:]
            turned[columns, :] = whole.T
        return carry

    lax.fori_loop(0, width // 256, tile, 0, unroll=2)
    wide = jnp.zeros((1, 2 * LANES), F32)
    step = 128

    def pair(p, carry):
        blocks = pair_blocks(query_t[ds(p * 128, 128), :])
        top = wide + 2 * MASKED_SCORE
        for c in range(0, keys, step):
            part = nn(key8[p, pl.ds(c, step), :], blocks)
            mask = bias[pl.ds(c, step), :]
            part = part + jnp.concatenate([mask, mask], 1)
            scores[pl.ds(c, step), :] = part
            top = jnp.maximum(top, jnp.max(part, 0, keepdims=True))
        total = wide
        for c in range(0, keys, step):
            part = jnp.exp(scores[pl.ds(c, step), :] - top)
            scores[pl.ds(c, step), :] = part
            total = total + jnp.sum(part, 0, keepdims=True)
        scale = 1.0 / total
        for c in range(0, keys, step):
            attend[p, pl.ds(c, step), :] = (scores[pl.ds(c, step), :] * scale).astype(BF16)
        for half in range(2):
            rows = pl.ds(pl.multiple_of(p * 128 + half * HD, HD), HD)
            heads_t[rows, :] = nn(value_t[rows, :], attend[p, :, pl.ds(half * LANES, LANES)])
        return carry

    lax.fori_loop(0, PAIRS, pair, 0)
    loads.wait(("square", 3))
    heads = heads_t[...].astype(BF16).T[:tokens]
    for c in range(0, width, 512):
        columns = pl.ds(c, 512)
        middle[:, columns] = residual[:, columns] + nn(heads, square(weights.at[3], columns))
    result, n, r = layer_norm(middle[...], gain[...], shift[...])
    middle[...] = result
    normed[...] = n
    inverse[...] = r


def feed_forward_steps(loads, middle, up_bias, gain, shift, up, down, low, hidden, slope, output):
    tokens, width = middle.shape
    low[pl.ds(0, tokens), :] = middle[...].astype(BF16)
    for b in range(up.shape[0]):
        loads.wait(("up", b))
        for c in range(0, width, 512):
            place = pl.ds(b * width + c, 512)
            u = nn(low[pl.ds(0, tokens), :], square(up.at[b], pl.ds(c, 512))) + up_bias[:, place]
            part = 0.5 + 0.5 * lax.erf(u * (0.5**0.5))
            hidden[:, place] = (u * part).astype(BF16)
            slope[:, place] = (part + u * (jnp.exp(-0.5 * u * u) * ((2 * np.pi) ** -0.5))).astype(BF16)
    for r in range(down.shape[0]):
        loads.wait(("down", r))
    for c in range(0, width, 512):
        columns = pl.ds(c, 512)
        block = down[:, :, :, :, columns].reshape(hidden.shape[1], 512)
        output[:, columns] = middle[:, columns] + nn(hidden[...], block)
    return layer_norm(output[...], gain[...], shift[...])


def forward_kernel(start, *refs):
    (gathered, middle, up_bias, gain, shift) = refs[:5]
    (output, low, normed, inverse, slope) = refs[5:10]
    (up, down, hidden, sems) = refs[10:]
    loads = Loads(sems)
    load_up(loads, gathered, start, up)
    load_down(loads, gathered, start, down)
    result, n, r = feed_forward_steps(loads, middle, up_bias, gain, shift, up, down, low, hidden, slope, output)
    output[...] = result
    low[...] = result.astype(BF16)
    normed[...] = n
    inverse[...] = r


def feed_back_steps(loads, grad_two, slope, normed_one, inverse_one, gain_one, up, down, weights, low, hidden, grad_one, heads_grad):
    tokens, width = grad_two.shape
    low[pl.ds(0, tokens), :] = grad_two.astype(BF16)
    grad_one[...] = grad_two
    size = hidden.shape[1] // down.shape[0]
    for r in range(down.shape[0]):
        loads.wait(("down", r))
        place = pl.ds(r * size, size)
        back = nt(low[pl.ds(0, tokens), :], down[r].reshape(size, width))
        hidden[:, place] = (back * slope[:, place].astype(F32)).astype(BF16)
    for b in range(up.shape[0]):
        loads.wait(("up", b))
    rows = up.shape[2]
    for c in range(0, width, 512):
        total = grad_one[:, pl.ds(c, 512)]
        for b in range(up.shape[0]):
            block = up[b, pl.ds(c // rows, 512 // rows)].reshape(512, width)
            total = total + nt(hidden[:, pl.ds(b * width, width)], block)
        grad_one[:, pl.ds(c, 512)] = total
    loads.wait("normed_one")
    back = norm_back(grad_one[...], gain_one[...], normed_one[...], inverse_one[...])
    grad_one[...] = back
    low[pl.ds(0, tokens), :] = back.astype(BF16)
    low[pl.ds(tokens, LANES - tokens), :] = jnp.zeros((LANES - tokens, width), BF16)
    loads.wait(("square", 3))
    heads_grad[...] = nt(square(weights.at[0]), low[...]).astype(BF16)


def attention_back_steps(loads, heads_grad, heads_t, query_t, value8, key_t, attend, weights, key_grad, value_grad, query_grad_t, steps, outs):
    (query_grad, key_own, value_own, halo, prefix_grad) = outs
    tokens, width = query_grad.shape
    keys = attend.shape[1]
    span = keys - prefix_grad.shape[1]
    loads.wait("heads_t", "query_t", "value8", "key_t")
    step = 128
    for p in range(PAIRS):
        loads.wait(("attend", p))
        rows = pl.ds(p * 128, 128)
        grad_t = heads_grad[rows, :]
        product = grad_t.astype(F32) * heads_t[rows, :]
        dots = jnp.concatenate(
            [jnp.sum(product[:HD], 0, keepdims=True), jnp.sum(product[HD:], 0, keepdims=True)], 1
        )
        blocks = pair_blocks(grad_t)
        grad_v = nt(attend[p], blocks)
        value_grad[:, rows] = grad_v.astype(BF16)
        prefix_grad[1, :, rows] = grad_v[span:]
        here = steps.at[p % 2]
        for c in range(0, keys, step):
            part = nn(value8[p, pl.ds(c, step), :], blocks) - dots
            here[pl.ds(c, step), :] = (attend[p, pl.ds(c, step), :].astype(F32) * part).astype(BF16)
        grad_k = nt(here[...], pair_blocks(query_t[rows, :]))
        key_grad[:, rows] = grad_k.astype(BF16)
        prefix_grad[0, :, rows] = grad_k[span:]
        for half in range(2):
            place = pl.ds(p * 128 + half * HD, HD)
            query_grad_t[place, :] = nn(key_t[place, :], here[:, pl.ds(half * LANES, LANES)]).astype(BF16)
    query_grad[...] = query_grad_t[...].T[:tokens]
    key_own[...] = key_grad[pl.ds(0, tokens), :]
    value_own[...] = value_grad[pl.ds(0, tokens), :]
    loads.wait(("square", 1), ("square", 2))
    outer = pl.ds(tokens, span - tokens)
    rows = weights.shape[2]
    for c in range(0, width, 512):
        part = pl.ds(c // rows, 512 // rows)
        halo[:, pl.ds(c, 512)] = (
            nt(key_grad[outer, :], weights[1, part].reshape(512, width))
            + nt(value_grad[outer, :], weights[2, part].reshape(512, width))
        ).astype(BF16)


def load_saved(loads, gathered, start, saved, weights, buffers):
    load_attention(loads, gathered, start, [3], weights.at[pl.ds(0, 1)])
    for name, source, target in zip(("heads_t", "query_t", "value8", "key_t"), saved, buffers):
        loads.start(name, source, target)
    for p in range(PAIRS):
        loads.start(("attend", p), saved[4].at[p], buffers[4].at[p])
    load_attention(loads, gathered, start, [1, 2], weights.at[pl.ds(1, 2)])


def last_kernel(feed_start, attention_start, *refs):
    (feed, squares, middle, up_bias, gain_two, shift_two, cotangent, inverse_one, gain_one, normed_hbm) = refs[:10]
    saved = refs[10:15]
    low_out, grad_one = refs[15:17]
    outs = refs[17:22]
    (up, down, weights, slope, low, hidden, normed_one, heads_grad) = refs[22:30]
    buffers = refs[30:35]
    (key_grad, value_grad, query_grad_t, steps, sems) = refs[35:]
    loads = Loads(sems)
    load_up(loads, feed, feed_start, up)
    load_down(loads, feed, feed_start, down)
    loads.start("normed_one", normed_hbm, normed_one)
    load_saved(loads, squares, attention_start, saved, weights, buffers)
    result, n, r = feed_forward_steps(
        loads, middle, up_bias, gain_two, shift_two, up, down, low, hidden, slope, grad_one
    )
    low_out[...] = result.astype(BF16)
    grad_two = norm_back(cotangent[...].astype(F32), gain_two[...], n, r)
    feed_back_steps(
        loads, grad_two, slope, normed_one, inverse_one, gain_one, up, down, weights, low, hidden, grad_one, heads_grad
    )
    attention_back_steps(
        loads, heads_grad, *buffers[:5], weights, key_grad, value_grad, query_grad_t, steps, outs
    )


def back_kernel(feed_start, attention_start, *refs):
    (flag, feed, squares, grad, near, across, edge, inverse_two, gain_two, inverse_one, gain_one) = refs[:11]
    (normed_two_hbm, slope_hbm, normed_one_hbm) = refs[11:14]
    saved = refs[14:19]
    grad_one = refs[19]
    outs = refs[20:25]
    (up, down, weights, slope, low, hidden, normed_two, normed_one, heads_grad) = refs[25:34]
    buffers = refs[34:39]
    (key_grad, value_grad, query_grad_t, steps, sems) = refs[39:]
    tokens, width = grad.shape
    loads = Loads(sems)
    loads.start("normed_two", normed_two_hbm, normed_two)
    loads.start("slope", slope_hbm, slope)
    load_down(loads, feed, feed_start, down)
    load_up(loads, feed, feed_start, up)
    loads.start("normed_one", normed_one_hbm, normed_one)
    load_saved(loads, squares, attention_start, saved, weights, buffers)
    grad_one[...] = grad[...] + near[...].astype(F32) + across[...].astype(F32)
    last = flag[0].astype(F32)
    extra = edge[...].astype(F32)
    head, tail = pl.ds(0, EDGE), pl.ds(tokens - EDGE, EDGE)
    grad_one[head, :] = grad_one[head, :] + extra * (1.0 - last)
    grad_one[tail, :] = grad_one[tail, :] + extra * last
    loads.wait("normed_two")
    grad_two = norm_back(grad_one[...], gain_two[...], normed_two[...], inverse_two[...])
    loads.wait("slope")
    feed_back_steps(
        loads, grad_two, slope, normed_one, inverse_one, gain_one, up, down, weights, low, hidden, grad_one, heads_grad
    )
    attention_back_steps(
        loads, heads_grad, *buffers[:5], weights, key_grad, value_grad, query_grad_t, steps, outs
    )


def input_back_kernel(start, *refs):
    (gathered, grad_one, query_grad, key_own, value_own, grad_input, weights, sems) = refs
    width = grad_one.shape[1]
    rows = weights.shape[2]
    loads = Loads(sems)
    load_attention(loads, gathered, start, range(3), weights)
    for kind in range(3):
        loads.wait(("square", kind))
        left, scale = ((query_grad, SCORE_SCALE), (key_own, None), (value_own, None))[kind]
        before = grad_one if kind == 0 else grad_input
        for c in range(0, width, 512):
            columns = pl.ds(c, 512)
            part = nt(left[...], weights[kind, pl.ds(c // rows, 512 // rows)].reshape(512, width))
            grad_input[:, columns] = before[:, columns] + (part if scale is None else scale * part)


def pack_kernel(place, query, key, value, out, up, down, first, second, sems):
    places = 4
    half = places // 2
    rows = query.shape[1]
    width = query.shape[2]
    each = second.shape[0]
    for k in range(places):

        @pl.when(place[0] == k)
        def _():
            matrix = (query, key, value, out)[k]
            jobs = [(matrix.at[0], first.at[0]), (matrix.at[1], first.at[each + 1])]
            for layer, target, begin in ((0, first, 1), (1, second, 0)):
                for i in range(each):
                    b = k * each + i
                    if k < half:
                        source = up.at[layer, :, pl.ds(b * width, width)]
                    else:
                        source = down.at[layer, pl.ds((b - half * each) * rows, rows)]
                    jobs.append((source, target.at[begin + i]))
            copies = [pltpu.make_async_copy(a, b, sems.at[i]) for i, (a, b) in enumerate(jobs)]
            for copy in copies:
                copy.start()
            for copy in copies:
                copy.wait()


VMEM = pl.BlockSpec(memory_space=pltpu.VMEM)
SMEM = pl.BlockSpec(memory_space=pltpu.SMEM)
ANY = pl.BlockSpec(memory_space=pl.ANY)


def call(kernel, numbers, kept, operands, late, outs, scratch, limit, flops, sem_count, small=()):
    moved = sum(x.size * x.dtype.itemsize for x in (*operands, *late)) + 16 * MIB
    return pl.pallas_call(
        partial(kernel, *numbers),
        out_shape=outs,
        in_specs=[SMEM] * len(small) + [ANY] * len(kept) + [VMEM] * len(operands) + [ANY] * len(late),
        out_specs=[VMEM] * len(outs),
        scratch_shapes=[*scratch, pltpu.SemaphoreType.DMA((sem_count,))],
        compiler_params=pltpu.CompilerParams(vmem_limit_bytes=limit * MIB),
        cost_estimate=pl.CostEstimate(flops=flops, bytes_accessed=moved, transcendentals=0),
    )(*small, *kept, *operands, *late)


def shape(*sizes, dtype=BF16):
    return jax.ShapeDtypeStruct(sizes, dtype)


def feed_scratch(gathered, wide):
    parts, places, _, rows, width = gathered.shape
    ratio = wide // width
    return [
        pltpu.VMEM((ratio, parts, rows, width), BF16),
        pltpu.VMEM((parts, places // 2, 2 * ratio // places, rows, width), BF16),
    ]


def squares_scratch(gathered, count):
    parts, _, _, rows, width = gathered.shape
    return pltpu.VMEM((count, parts, rows, width), BF16)


def attention_forward(inputs, inputs_low, around, bias, prefix_k, prefix_v, gain, shift, weights):
    gathered, start = weights
    tokens, width = inputs.shape
    keys = bias.shape[0]
    span = keys - prefix_k.shape[0]
    return call(
        attention_kernel,
        [start],
        [gathered],
        [inputs_low, *around, inputs, bias, prefix_k, prefix_v, gain, shift],
        [],
        [
            shape(tokens, width, dtype=F32),
            shape(tokens, width, dtype=F32),
            shape(tokens, 1, dtype=F32),
            shape(width, LANES),
            shape(PAIRS, keys, 128),
            shape(width, keys),
            shape(PAIRS, keys, 2 * LANES),
            shape(width, LANES, dtype=F32),
        ],
        [
            squares_scratch(gathered, 4),
            pltpu.VMEM((span, width), BF16),
            pltpu.VMEM((PAIRS, keys, 128), BF16),
            pltpu.VMEM((width, keys), BF16),
            pltpu.VMEM((keys, 2 * LANES), F32),
        ],
        40,
        2 * tokens * width * width * 8,
        4,
    )


def feed_forward(middle, up_bias, gain, shift, weights):
    gathered, start = weights
    tokens, width = middle.shape
    wide = up_bias.shape[1]
    return call(
        forward_kernel,
        [start],
        [gathered],
        [middle, up_bias, gain, shift],
        [],
        [
            shape(tokens, width, dtype=F32),
            shape(tokens, width),
            shape(tokens, width, dtype=F32),
            shape(tokens, 1, dtype=F32),
            shape(tokens, wide),
        ],
        [*feed_scratch(gathered, wide), pltpu.VMEM((tokens, wide), BF16)],
        40,
        4 * tokens * width * wide,
        wide // width + gathered.shape[0],
    )


def back_shapes(tokens, width, keys, prefix):
    span = keys - prefix
    return [
        shape(tokens, width, dtype=F32),
        shape(tokens, width),
        shape(tokens, width),
        shape(tokens, width),
        shape(span - tokens, width),
        shape(2, prefix, width, dtype=F32),
    ]


def saved_scratch(saved):
    heads_t, query_t, value8, key_t, attend = saved
    keys = attend.shape[1]
    width = heads_t.shape[0]
    return [pltpu.VMEM(x.shape, x.dtype) for x in saved] + [
        pltpu.VMEM((keys, width), BF16),
        pltpu.VMEM((keys, width), BF16),
        pltpu.VMEM((width, LANES), BF16),
        pltpu.VMEM((2, keys, 2 * LANES), BF16),
    ]


def layer_call(kernel, small, operands, late, outs, kinds, saved, feed, squares, wide, tokens):
    gathered = feed[0]
    parts, _, _, _, width = gathered.shape
    ratio = wide // width
    return call(
        kernel,
        [feed[1], squares[1]],
        [feed[0], squares[0]],
        operands,
        [*late, *saved],
        outs,
        [
            *feed_scratch(gathered, wide),
            squares_scratch(gathered, 3),
            pltpu.VMEM((tokens, wide), BF16),
            pltpu.VMEM((LANES, width), BF16),
            pltpu.VMEM((tokens, wide), BF16),
            *[pltpu.VMEM((tokens, width), F32)] * kinds,
            pltpu.VMEM((width, LANES), BF16),
            *saved_scratch(saved),
        ],
        52,
        8 * tokens * width * wide,
        ratio + parts + 3 + 4 + PAIRS + 3,
        small,
    )


def input_back(grad_one, query_grad, key_own, value_own, weights):
    gathered, start = weights
    tokens, width = grad_one.shape
    return call(
        input_back_kernel,
        [start],
        [gathered],
        [grad_one, query_grad, key_own, value_own],
        [],
        [shape(tokens, width, dtype=F32)],
        [squares_scratch(gathered, 3)],
        30,
        6 * tokens * width * width,
        3,
    )[0]


def pack(place, w_query, w_key, w_value, w_out, w_up, w_down, each):
    rows, width = w_query.shape[1:]
    return pl.pallas_call(
        pack_kernel,
        out_shape=[shape(each + 2, rows, width), shape(each, rows, width)],
        in_specs=[SMEM] + [ANY] * 6,
        out_specs=[VMEM] * 2,
        scratch_shapes=[pltpu.SemaphoreType.DMA((2 * each + 2,))],
    )(place, w_query, w_key, w_value, w_out, w_up, w_down)


def xor_pairs(count, bit):
    return [(i, i ^ bit) for i in range(count)]


def sum_prefixes(parts):
    layers, two, prefix, width = parts.shape
    places = lax.axis_size("keys")
    place = lax.axis_index("keys")
    total = parts
    step = places // 2
    while step:
        split = total.reshape(layers, two, 2, -1, width)
        mine = (place // step) % 2
        sent = lax.dynamic_index_in_dim(split, 1 - mine, 2, False).astype(BF16)
        kept = lax.dynamic_index_in_dim(split, mine, 2, False)
        total = kept + lax.ppermute(sent, "keys", xor_pairs(places, step)).astype(F32)
        step //= 2
    count = lax.axis_size("rows")
    step = 1
    while step < count:
        total = total + lax.ppermute(total.astype(BF16), "rows", xor_pairs(count, step)).astype(F32)
        step *= 2
    return total


def body(
    activations,
    segments,
    prefix_keys,
    prefix_values,
    w_query,
    w_key,
    w_value,
    w_out,
    w_up,
    ff_bias,
    w_down,
    ln_gain,
    ln_bias,
    cotangent,
):
    _, tokens, width = activations.shape
    wide = w_up.shape[2]
    ratio = wide // width
    places = lax.axis_size("keys")
    parts = lax.axis_size("rows")
    rows = width // parts
    place = lax.axis_index("keys")
    prefix = prefix_keys.shape[1] * places
    first_half = place < places // 2

    each = 2 * ratio // places
    shares = pack(place[None], w_query, w_key, w_value, w_out, w_up, w_down, each)

    def gather(share):
        whole = lax.all_gather(share, ("rows", "keys"), axis=0, tiled=True)
        return whole.reshape(parts, places, share.shape[0], rows, width)

    first, second = gather(shares[0]), gather(shares[1])
    squares = [(first, 0), (first, each + 1)]
    feeds = [(first, 1), (second, 0)]

    def exchange(low):
        near = lax.ppermute(low, "keys", xor_pairs(places, 1))
        across = lax.ppermute(low, "keys", [(1, 2), (2, 1)])
        edge = lax.ppermute(
            jnp.where(first_half, low[tokens - EDGE :], low[:EDGE]), "keys", xor_pairs(places, 2)
        )
        return near, across, edge

    line = segments[0]

    def ids(where, start, size):
        return lax.dynamic_slice_in_dim(line, where * tokens + start, size, 0)

    own_ids = ids(place, 0, tokens)
    across_ids = jnp.where(
        (place == 1) | (place == 2), ids(jnp.clip(3 - place, 0, places - 1), 0, tokens), -1
    )
    edge_ids = ids(place ^ 2, jnp.where(first_half, 0, tokens - EDGE), EDGE)
    key_ids = jnp.concatenate([own_ids, ids(place ^ 1, 0, tokens), across_ids, edge_ids])
    allowed = jnp.concatenate([key_ids[:, None] == own_ids[None, :], jnp.ones((prefix, tokens), bool)], 0)
    bias = jnp.pad(jnp.where(allowed, 0.0, MASKED_SCORE).astype(F32), ((0, 0), (0, LANES - tokens)))

    prefixes = lax.all_gather(jnp.stack([prefix_keys, prefix_values]), "keys", axis=2, tiled=True)

    low = activations[0]
    hidden = low.astype(F32)
    kept, kept_feed = [], []
    for layer in range(LAYERS):
        gains, shifts = ln_gain[layer][:, None], ln_bias[layer][:, None]
        around = exchange(low)
        middle, normed_one, inverse_one, query_t, value8, key_t, attend, heads_t = attention_forward(
            hidden,
            low,
            around,
            bias,
            prefixes[0, layer],
            prefixes[1, layer],
            gains[0],
            shifts[0],
            squares[layer],
        )
        saved = (heads_t, query_t, value8, key_t, attend)
        kept.append(((normed_one, inverse_one), saved))
        if layer < LAYERS - 1:
            hidden, low, *second_norm = feed_forward(middle, ff_bias[layer][None], gains[1], shifts[1], feeds[layer])
            kept_feed.append(second_norm)

    flag = first_half.astype(jnp.int32)[None]
    keys = bias.shape[0]
    prefix_parts = [None] * LAYERS
    for layer in range(LAYERS - 1, -1, -1):
        (normed_one, inverse_one), saved = kept[layer]
        gains, shifts = ln_gain[layer][:, None], ln_bias[layer][:, None]
        outs = back_shapes(tokens, width, keys, prefix)
        if layer == LAYERS - 1:
            result, grad_one, query_grad, key_own, value_own, halo, prefix_parts[layer] = layer_call(
                last_kernel,
                (),
                [middle, ff_bias[layer][None], gains[1], shifts[1], cotangent[0], inverse_one, gains[0]],
                [normed_one],
                [shape(tokens, width), *outs],
                1,
                saved,
                feeds[layer],
                squares[layer],
                wide,
                tokens,
            )
        else:
            normed_two, inverse_two, slope = kept_feed[layer]
            grad_one, query_grad, key_own, value_own, halo, prefix_parts[layer] = layer_call(
                back_kernel,
                (flag,),
                [gradient, near, across, edge, inverse_two, gains[1], inverse_one, gains[0]],
                [normed_two, slope, normed_one],
                outs,
                2,
                saved,
                feeds[layer],
                squares[layer],
                wide,
                tokens,
            )
        near = lax.ppermute(halo[:tokens], "keys", xor_pairs(places, 1))
        across = lax.ppermute(halo[tokens : 2 * tokens], "keys", [(1, 2), (2, 1)])
        edge = lax.ppermute(halo[2 * tokens :], "keys", xor_pairs(places, 2))
        gradient = input_back(grad_one, query_grad, key_own, value_own, squares[layer])
    extra = edge.astype(F32)
    lead = jnp.where(first_half, 0.0, extra)
    tail = jnp.where(first_half, extra, 0.0)
    gradient = (
        gradient
        + near.astype(F32)
        + across.astype(F32)
        + jnp.concatenate([lead, jnp.zeros((tokens - 2 * EDGE, width), F32), tail], 0)
    )
    prefix_total = sum_prefixes(jnp.stack(prefix_parts))
    return (
        result[None],
        gradient[None],
        prefix_total[:, 0],
        prefix_total[:, 1],
    )


def solution(mesh):
    placed = (
        P("rows", "keys", None),
        P("rows", None),
        P(None, "keys", None),
        P(None, "keys", None),
        P(None, "rows", None),
        P(None, "rows", None),
        P(None, "rows", None),
        P(None, "rows", None),
        P(None, "rows", None),
        P(),
        P(None, "rows", None),
        P(),
        P(),
        P("rows", "keys", None),
    )
    return jax.shard_map(
        body,
        mesh=mesh,
        in_specs=placed,
        out_specs=(
            P("rows", "keys", None),
            P("rows", "keys", None),
            P(None, "keys", None),
            P(None, "keys", None),
        ),
        check_vma=False,
    )
```

time: 480 us -> 447 us (0.931); the launches traced: 479 us -> 440 us
  local copies, waits for them, and re-layouts: 40.9 us -> 17 us
  Pallas kernels: 132 us -> 111 us
  waiting for transfers between devices: 245 us -> 258 us
    pallas_call x10 -> x8, Pallas kernels: 132 us -> 111 us  [the longest x7 109 us: call(): pl.pallas_call(partial(kernel, *numbers), out_shape=outs, in_specs=[SMEM]...]
    unnamed x172 -> x54, local copies, waits for them, and re-layouts: 26.5 us -> 12 us
    all_gather x2, waiting for transfers between devices: 212 us -> 222 us  [gather(): whole = lax.all_gather(share, ('rows', 'keys'), axis=0, tiled=True)]
  transfers between devices with their start and end apart: 19 -> 19, of which waited for: 6 -> 9; matrix products, arithmetic and copies ran while one was open for 1% -> 1% of each run, Pallas kernels for 13% -> 12%
where the time goes in v3:
time: 447 us; the launch traced here: 440 us
  waiting for transfers between devices  258 us (58%)
  Pallas kernels  111 us (25%)
  starting transfers between devices  21.1 us (5%)
  local copies, waits for them, and re-layouts  17 us (4%)
  between operations  15 us (3%)
  blocking collectives  13.2 us (3%)
    all_gather x2, waiting for transfers between devices, gather(): whole = lax.all_gather(share, ('rows', 'keys'), axis=0, tiled=True)  222 us
    pallas_call x7, Pallas kernels, call(): pl.pallas_call(partial(kernel, *numbers), out_shape=outs, in_specs=[SMEM]...  109 us
    ppermute x2, waiting for transfers between devices, exchange(): lax.ppermute(jnp.where(first_half, low[tokens - EDGE:], low[:EDGE]), 'key...  16.5 us
    all_gather x1, blocking collectives, body(): lax.all_gather(jnp.stack([prefix_keys, prefix_values]), 'keys', axis=2, t...  13.2 us
    unnamed x54, local copies, waits for them, and re-layouts  12 us
  transfers between devices with their start and end apart: 19, of which 9 were waited for; matrix products, arithmetic and copies ran while one was open for 1% of the time, Pallas kernels for 12%

profile of v3, /device:TPU:0, one launch (start us, length us, event | category | flops | bytes accessed | tf_op | source)
XLA Modules:
  0.0 439.7 jit_solution(1413329198696515785)
XLA Ops:
  7.3 2.6 shard_map.165
  10.0 0.7 all-gather.3.cloned.1.call-update
  10.7 0.5 collective-permute-start
  11.3 1.4 collective-permute-start.1
  12.7 3.1 collective-permute-start.2
  15.8 0.1 fusion.11
  15.9 0.1 constant_dynamic-slice_fusion.2
  15.9 0.1 pad_add_fusion
  16.0 13.2 %all_gather.11 = bf16[2,2,64,1024]{3,2,1,0:T(8,128)(2,1)S(1)} all-gather(bf16[2,2,16,1024]{3,2,1,0:T(8,128)(2,1)S(1)} %pad_maximum_fusion), channel_id=1, replica_groups=mesh['rows'=8,'keys'=4] {'keys'}, dimensions={2}, use_global_device_ids=true | all-gather | bytes 655360 | tf_op jit(solution)/shard_map/all_gather | solution.py:644
  29.2 0.2 broadcast_compare_fusion
  29.5 0.1 bitcast_convert_fusion.refs_5_
  29.6 0.1 pad_select_fusion
  29.8 178.6 %all-gather.5.cloned.1.call-done = bf16[128,128,1024]{2,1,0:T(8,128)(2,1)} async-done(((bf16[4,128,1024]{2,1,0:T(8,128)(2,1)}), bf16[128,128,1024]{2,1,0:T(8,128)(2,1)}) %all-gather.5.cloned.1.call-update) | async-done | bytes 33554448 | tf_op jit(solution)/shard_map/all_gather | solution.py:615
  208.4 18.7 %shard_map.166 = (f32[224,1024]{1,0:T(8,128)S(1)}, f32[224,1024]{1,0:T(8,128)S(1)}, f32[224,1]{1,0:T(8,128)S(1)}, bf16[1024,256]{1,0:T(8,128)(2,1)S(1)}, bf16[8,...) custom-call(bf16[8,4,4,128,1024]{4,3,2,1,0:T(8,128)(2,1)} %bitcast.8, ...), custom_call_target="tpu_custom_call" | custom-call | flops 3758096384 | bytes 20193280 | tf_op jit(solution)/shard_map/pallas_call | solution.py:393
  227.1 1.0 copy-done.7
  228.1 1.0 copy-done.9
  229.1 9.6 %shard_map.167 = (f32[224,1024]{1,0:T(8,128)S(1)}, bf16[224,1024]{1,0:T(8,128)(2,1)S(1)}, f32[224,1024]{1,0:T(8,128)S(1)}, f32[224,1]{1,0:T(8,128)S(1)}, bf16[224,4096]{1,0:T(8,128)(2,1)S(1)}) custom-call(bf16[8,4,4,128,1024]{4,3,2,1,0:T(8,128)(2,1)} %bitcast.81, f32[224,1024]{1,0:T(8,128)S(1)} %get-tuple-element.42.refs_1_, ...), custom_call_target="tpu_custom_call" | custom-call | flops 3758096384 | bytes 17719296 | tf_op jit(solution)/shard_map/pallas_call | solution.py:393
  238.7 1.3 copy-done.2
  240.0 1.0 copy-done.10
  241.0 0.3 collective-permute-start.3
  241.2 1.1 collective-permute-start.4
  242.4 3.2 collective-permute-start.5
  245.6 16.5 %collective-permute-done.5.refs_4_ = bf16[32,1024]{1,0:T(8,128)(2,1)S(1)} collective-permute-done((bf16[32,1024]{1,0:T(8,128)(2,1)S(1)}, bf16[32,1024]{1,0:T(8,128)(2,1)S(1)}, u32[]{:S(2)}, u32[]{:S(2)}) %collective-permute-start.5) | collective-permute-done | bytes 65568 | tf_op jit(solution)/shard_map/ppermute | solution.py:625
  262.0 18.8 %shard_map.168 = (f32[224,1024]{1,0:T(8,128)S(1)}, f32[224,1024]{1,0:T(8,128)S(1)}, f32[224,1]{1,0:T(8,128)S(1)}, bf16[1024,256]{1,0:T(8,128)(2,1)S(1)}, bf16[8,...) custom-call(bf16[8,4,4,128,1024]{4,3,2,1,0:T(8,128)(2,1)} %bitcast.8, ...), custom_call_target="tpu_custom_call" | custom-call | flops 3758096384 | bytes 20193280 | tf_op jit(solution)/shard_map/pallas_call | solution.py:393
  280.8 1.2 copy-done.5
  282.0 1.2 copy-done.6
  283.2 1.0 copy-done.8
  284.1 0.9 copy-done.11
  285.1 0.9 copy-done.12
  286.0 0.8 copy-done.16
  286.8 43.8 %all-gather.3.cloned.1.call-done = bf16[64,128,1024]{2,1,0:T(8,128)(2,1)} async-done(((bf16[2,128,1024]{2,1,0:T(8,128)(2,1)}), bf16[64,128,1024]{2,1,0:T(8,128)(2,1)}) %all-gather.3.cloned.1.call-update) | async-done | bytes 16777232 | tf_op jit(solution)/shard_map/all_gather | solution.py:615
  330.6 28.9 %shard_map.169 = (bf16[224,1024]{1,0:T(8,128)(2,1)}, f32[224,1024]{1,0:T(8,128)}, bf16[224,1024]{1,0:T(8,128)(2,1)S(1)}, bf16[224,1024]{1,0:T(8,128)(2,1)S(1)}, ...) custom-call(bf16[8,4,2,128,1024]{4,3,2,1,0:T(8,128)(2,1)} %bitcast.88, ...), custom_call_target="tpu_custom_call" | custom-call | flops 7516192768 | bytes 30110592 | tf_op jit(solution)/shard_map/pallas_call | solution.py:393
  359.5 2.2 fusion.14
  361.8 0.3 collective-permute-start.6
  362.0 1.6 collective-permute-start.7
  363.7 0.8 slice.126
  364.5 2.4 collective-permute-start.8
  366.9 3.9 shard_map.170.refs_3_
  370.8 0.9 copy-done
  371.8 2.1 collective-permute-done.8.refs_6_
  373.9 0.8 copy-done.20
  374.7 25.1 %shard_map.171 = (f32[224,1024]{1,0:T(8,128)}, bf16[224,1024]{1,0:T(8,128)(2,1)S(1)}, bf16[224,1024]{1,0:T(8,128)(2,1)S(1)}, bf16[224,1024]{1,0:T(8,128)(2,1)S(1...) custom-call(s32[1]{0:T(128)} %bitcast.25.refs_0_, bf16[8,4,4,128,1024]{4,3,2,1,0:T(8,128)(2,1)} %bitcast.85, ...), custom_call_target="tpu_custom_call" | custom-call | flops 7516192768 | bytes 33367808 | tf_op jit(solution)/shard_map/pallas_call | solution.py:393
  399.8 1.1 fusion.7
  400.8 0.1 collective-permute-start.12
  401.0 0.1 pad.9.clone
  401.0 0.8 slice.129
  401.9 6.3 %collective-permute-done.12 = bf16[2,2,32,1024]{3,2,1,0:T(8,128)(2,1)} collective-permute-done((bf16[2,2,32,1024]{3,2,1,0:T(8,128)(2,1)S(1)}, bf16[2,2,32,1024]{3,2,1,0:T(8,128)(2,1)}, u32[]{:S(2)}, u32[]{:S(2)}) %collective-permute-start.12) | collective-permute-done | bytes 262176 | tf_op jit(solution)/shard_map/ppermute | solution.py:575
  408.2 1.1 fusion.6
  409.3 0.1 collective-permute-start.13
  409.5 0.7 collective-permute-start.10
  410.2 3.1 collective-permute-start.9
  413.3 0.3 collective-permute-start.11
  413.7 1.0 collective-permute-start.14
  414.7 3.9 shard_map.172
  418.6 0.8 collective-permute-done.14
  419.4 0.4 collective-permute-start.15
  419.8 1.6 collective-permute-done.11
  421.4 3.0 collective-permute-done.15
  424.4 0.1 fusion.10
  424.5 1.5 collective-permute-start.16
  426.0 1.1 fusion
  427.1 4.5 %collective-permute-done.16 = bf16[2,2,16,1024]{3,2,1,0:T(8,128)(2,1)S(1)} collective-permute-done((bf16[2,2,16,1024]{3,2,1,0:T(8,128)(2,1)S(1)}, bf16[2,2,16,1024]{3,2,1,0:T(8,128)(2,1)S(1)}, u32[]{:S(2)}, u32[]{:S(2)}) %collective-permute-start.16) | collective-permute-done | bytes 131104 | tf_op jit(solution)/shard_map/ppermute | solution.py:580
  431.6 0.1 convert_add_fusion
  431.7 0.7 slice_bitcast_fusion
  (68 shorter events, 0.6 us)
Async XLA Ops:
  7.2 201.2 %all-gather.5.cloned.1.call-start = ((), (), s32[]{:S(2)}) async-start(), calls=%async_computation.1 | async-start | bytes 34603008 | tf_op jit(solution)/shard_map/all_gather | solution.py:615
  7.2 3.5 copy-start.1
  7.2 8.6 %copy-start.26 = (s32[1,896]{1,0:T(1,128)S(1)}, s32[1,896]{1,0:T(1,128)}, u32[]{:S(2)}) copy-start(s32[1,896]{1,0:T(1,128)} %param.15) | copy-start | bytes 10756
  7.2 8.8 %copy-start.21 = (bf16[2,16,1024]{2,1,0:T(8,128)(2,1)S(1)}, bf16[2,16,1024]{2,1,0:T(8,128)(2,1)}, u32[]{:S(2)}) copy-start(bf16[2,16,1024]{2,1,0:T(8,128)(2,1)} %param.17) | copy-start | bytes 196612
  7.2 8.8 %copy-start.22 = (bf16[2,16,1024]{2,1,0:T(8,128)(2,1)S(1)}, bf16[2,16,1024]{2,1,0:T(8,128)(2,1)}, u32[]{:S(2)}) copy-start(bf16[2,16,1024]{2,1,0:T(8,128)(2,1)} %param.16) | copy-start | bytes 196612
  9.9 19.5 %copy-start.23 = (f32[2,4096]{1,0:T(2,128)S(1)}, f32[2,4096]{1,0:T(2,128)}, u32[]{:S(2)}) copy-start(f32[2,4096]{1,0:T(2,128)} %param.23) | copy-start | bytes 98308
  9.9 19.6 %copy-start.24 = (f32[2,2,1024]{2,1,0:T(2,128)S(1)}, f32[2,2,1024]{2,1,0:T(2,128)}, u32[]{:S(2)}) copy-start(f32[2,2,1024]{2,1,0:T(2,128)} %param.26) | copy-start | bytes 49156
  9.9 19.6 %copy-start.25 = (f32[2,2,1024]{2,1,0:T(2,128)S(1)}, f32[2,2,1024]{2,1,0:T(2,128)}, u32[]{:S(2)}) copy-start(f32[2,2,1024]{2,1,0:T(2,128)} %param.25) | copy-start | bytes 49156
  10.0 320.7 %all-gather.3.cloned.1.call-start = ((), (), s32[]{:S(2)}) async-start(), calls=%async_computation | async-start | bytes 17301504 | tf_op jit(solution)/shard_map/all_gather | solution.py:615
  10.7 19.1 %collective-permute-start = (bf16[224,1024]{1,0:T(8,128)(2,1)S(1)}, bf16[224,1024]{1,0:T(8,128)(2,1)S(1)}, u32[]{:S(2)}, u32[]{:S(2)}) collective-permute-start(bf16[224,1024]{1,0:T(8,128)(2,1)S(1)} %bitcast.76), channel_id=1, source_target_pairs={{0,1},{1,0},{2,3},{3,2},{4,5},{5,4},{6,7},{7,6},{8,9},{9,8},{10,11... | collective-permute-start | bytes 1376264 | tf_op jit(solution)/shard_map/ppermute | solution.py:623
  11.3 18.6 %collective-permute-start.1 = (bf16[224,1024]{1,0:T(8,128)(2,1)S(1)}, bf16[224,1024]{1,0:T(8,128)(2,1)}, u32[]{:S(2)}, u32[]{:S(2)}) collective-permute-start(bf16[224,1024]{1,0:T(8,128)(2,1)S(1)} %bitcast.77), channel_id=1, source_target_pairs={{1,2},{2,1},{5,6},{6,5},{9,10},{10,9},{13,14},{14,13},{17,18},{18,... | collective-permute-start | bytes 1376264 | tf_op jit(solution)/shard_map/ppermute | solution.py:624
  12.7 17.1 %collective-permute-start.2 = (bf16[32,1024]{1,0:T(8,128)(2,1)S(1)}, bf16[32,1024]{1,0:T(8,128)(2,1)S(1)}, u32[]{:S(2)}, u32[]{:S(2)}) collective-permute-start(bf16[32,1024]{1,0:T(8,128)(2,1)S(1)} %select_bitcast_fusion), channel_id=1, source_target_pairs={{0,2},{1,3},{2,0},{3,1},{4,6},{5,7},{6,4},{7,5},{8,10},{9,11},{10,... | collective-permute-start | bytes 196616 | tf_op jit(solution)/shard_map/ppermute | solution.py:625
  227.1 1.0 copy-start.7
  228.1 1.0 copy-start.9
  229.1 9.6 %copy-start.3 = (bf16[8,768,128]{2,1,0:T(8,128)(2,1)}, bf16[8,768,128]{2,1,0:T(8,128)(2,1)S(1)}, u32[]{:S(2)}) copy-start(bf16[8,768,128]{2,1,0:T(8,128)(2,1)S(1)} %get-tuple-element.66.refs_16_) | copy-start | bytes 4718596
  229.1 9.6 %copy-start.4 = (bf16[1024,768]{1,0:T(8,128)(2,1)}, bf16[1024,768]{1,0:T(8,128)(2,1)S(1)}, u32[]{:S(2)}) copy-start(bf16[1024,768]{1,0:T(8,128)(2,1)S(1)} %get-tuple-element.67.refs_17_) | copy-start | bytes 4718596
  229.1 9.6 %copy-start.15 = (bf16[1024,256]{1,0:T(8,128)(2,1)}, bf16[1024,256]{1,0:T(8,128)(2,1)S(1)}, u32[]{:S(2)}) copy-start(bf16[1024,256]{1,0:T(8,128)(2,1)S(1)} %get-tuple-element.65.refs_15_) | copy-start | bytes 1572868
  238.7 1.3 copy-start.2
  240.0 1.0 copy-start.10
  241.0 21.1 %collective-permute-start.3 = (bf16[224,1024]{1,0:T(8,128)(2,1)S(1)}, bf16[224,1024]{1,0:T(8,128)(2,1)S(1)}, u32[]{:S(2)}, u32[]{:S(2)}) collective-permute-start(bf16[224,1024]{1,0:T(8,128)(2,1)S(1)} %get-tuple-element.43.refs_1_), channel_id=1, source_target_pairs={{0,1},{1,0},{2,3},{3,2},{4,5},{5,4},{6,7},{7,6},{8,9},{9,8},{10,11... | collective-permute-start | bytes 1376264 | tf_op jit(solution)/shard_map/ppermute | solution.py:623
  241.2 20.8 %collective-permute-start.4 = (bf16[224,1024]{1,0:T(8,128)(2,1)S(1)}, bf16[224,1024]{1,0:T(8,128)(2,1)S(1)}, u32[]{:S(2)}, u32[]{:S(2)}) collective-permute-start(bf16[224,1024]{1,0:T(8,128)(2,1)S(1)} %get-tuple-element.43.refs_1_), channel_id=1, source_target_pairs={{1,2},{2,1},{5,6},{6,5},{9,10},{10,9},{13,14},{14,13},{17,18},{18,... | collective-permute-start | bytes 1376264 | tf_op jit(solution)/shard_map/ppermute | solution.py:624
  242.4 19.6 %collective-permute-start.5 = (bf16[32,1024]{1,0:T(8,128)(2,1)S(1)}, bf16[32,1024]{1,0:T(8,128)(2,1)S(1)}, u32[]{:S(2)}, u32[]{:S(2)}) collective-permute-start(bf16[32,1024]{1,0:T(8,128)(2,1)S(1)} %slice_select_fusion), channel_id=1, source_target_pairs={{0,2},{1,3},{2,0},{3,1},{4,6},{5,7},{6,4},{7,5},{8,10},{9,11},{10,... | collective-permute-start | bytes 196616 | tf_op jit(solution)/shard_map/ppermute | solution.py:625
  262.0 68.6 %copy-start.17 = (bf16[1,224,1024]{2,1,0:T(8,128)(2,1)S(1)}, bf16[1,224,1024]{2,1,0:T(8,128)(2,1)}, u32[]{:S(2)}) copy-start(bf16[1,224,1024]{2,1,0:T(8,128)(2,1)} %param.27) | copy-start | bytes 1376260
  280.8 1.2 copy-start.5
  282.0 1.2 copy-start.6
  283.2 1.0 copy-start.8
  284.1 0.9 copy-start.11
  285.1 0.9 copy-start.12
  286.0 0.8 copy-start.16
  359.5 7.4 %copy-start.14 = (f32[224,1024]{1,0:T(8,128)S(1)}, f32[224,1024]{1,0:T(8,128)}, u32[]{:S(2)}) copy-start(f32[224,1024]{1,0:T(8,128)} %get-tuple-element.54.refs_1_) | copy-start | bytes 2752516
  361.8 12.1 %collective-permute-start.6 = (bf16[224,1024]{1,0:T(8,128)(2,1)}, bf16[224,1024]{1,0:T(8,128)(2,1)S(1)}, u32[]{:S(2)}, u32[]{:S(2)}) collective-permute-start(bf16[224,1024]{1,0:T(8,128)(2,1)} %get-tuple-element.79), channel_id=1, source_target_pairs={{0,1},{1,0},{2,3},{3,2},{4,5},{5,4},{6,7},{7,6},{8,9},{9,8},{10,11... | collective-permute-start | bytes 1376264 | tf_op jit(solution)/shard_map/ppermute | solution.py:705
  362.0 11.8 %collective-permute-start.7 = (bf16[224,1024]{1,0:T(8,128)(2,1)}, bf16[224,1024]{1,0:T(8,128)(2,1)}, u32[]{:S(2)}, u32[]{:S(2)}) collective-permute-start(bf16[224,1024]{1,0:T(8,128)(2,1)} %get-tuple-element.78), channel_id=1, source_target_pairs={{1,2},{2,1},{5,6},{6,5},{9,10},{10,9},{13,14},{14,13},{17,18},{18,... | collective-permute-start | bytes 1376264 | tf_op jit(solution)/shard_map/ppermute | solution.py:706
  364.5 9.3 %collective-permute-start.8 = (bf16[32,1024]{1,0:T(8,128)(2,1)S(1)}, bf16[32,1024]{1,0:T(8,128)(2,1)S(1)}, u32[]{:S(2)}, u32[]{:S(2)}) collective-permute-start(bf16[32,1024]{1,0:T(8,128)(2,1)S(1)} %slice.126), channel_id=1, source_target_pairs={{0,2},{1,3},{2,0},{3,1},{4,6},{5,7},{6,4},{7,5},{8,10},{9,11},{10,... | collective-permute-start | bytes 196616 | tf_op jit(solution)/shard_map/ppermute | solution.py:707
  370.8 0.9 copy-start
  373.9 0.8 copy-start.20
  374.7 25.1 %copy-start.18 = (f32[2,64,1024]{2,1,0:T(8,128)S(1)}, f32[2,64,1024]{2,1,0:T(8,128)}, u32[]{:S(2)}) copy-start(f32[2,64,1024]{2,1,0:T(8,128)} %get-tuple-element.75) | copy-start | bytes 1572868
  399.7 9.7 %copy-start.19 = (bf16[480,1024]{1,0:T(8,128)(2,1)S(1)}, bf16[480,1024]{1,0:T(8,128)(2,1)}, u32[]{:S(2)}) copy-start(bf16[480,1024]{1,0:T(8,128)(2,1)} %get-tuple-element.73) | copy-start | bytes 2949124
  400.8 7.4 %collective-permute-start.12 = (bf16[2,2,32,1024]{3,2,1,0:T(8,128)(2,1)S(1)}, bf16[2,2,32,1024]{3,2,1,0:T(8,128)(2,1)}, u32[]{:S(2)}, u32[]{:S(2)}) collective-permute-start(bf16[2,2,32,1024]{3,2,1,0:T(8,128)(2,1)S(1)} %fusion.7), channel_id=1, source_target_pairs={{0,2},{1,3},{2,0},{3,1},{4,6},{5,7},{6,4},{7,5},{8,10},{9,11},{10,... | collective-permute-start | bytes 786440 | tf_op jit(solution)/shard_map/ppermute | solution.py:575
  401.9 12.8 %copy-start.13 = (f32[224,1024]{1,0:T(8,128)S(1)}, f32[224,1024]{1,0:T(8,128)}, u32[]{:S(2)}) copy-start(f32[224,1024]{1,0:T(8,128)} %get-tuple-element.69.refs_1_) | copy-start | bytes 2752516
  409.3 4.3 collective-permute-start.13
  409.5 16.5 %collective-permute-start.10 = (bf16[224,1024]{1,0:T(8,128)(2,1)S(1)}, bf16[224,1024]{1,0:T(8,128)(2,1)S(1)}, u32[]{:S(2)}, u32[]{:S(2)}) collective-permute-start(bf16[224,1024]{1,0:T(8,128)(2,1)S(1)} %get-tuple-element.77), channel_id=1, source_target_pairs={{1,2},{2,1},{5,6},{6,5},{9,10},{10,9},{13,14},{14,13},{17,18},{18,... | collective-permute-start | bytes 1376264 | tf_op jit(solution)/shard_map/ppermute | solution.py:706
  410.2 15.8 %collective-permute-start.9 = (bf16[224,1024]{1,0:T(8,128)(2,1)S(1)}, bf16[224,1024]{1,0:T(8,128)(2,1)S(1)}, u32[]{:S(2)}, u32[]{:S(2)}) collective-permute-start(bf16[224,1024]{1,0:T(8,128)(2,1)S(1)} %get-tuple-element.76), channel_id=1, source_target_pairs={{0,1},{1,0},{2,3},{3,2},{4,5},{5,4},{6,7},{7,6},{8,9},{9,8},{10,11... | collective-permute-start | bytes 1376264 | tf_op jit(solution)/shard_map/ppermute | solution.py:705
  413.3 8.0 %collective-permute-start.11 = (bf16[32,1024]{1,0:T(8,128)(2,1)S(1)}, bf16[32,1024]{1,0:T(8,128)(2,1)S(1)}, u32[]{:S(2)}, u32[]{:S(2)}) collective-permute-start(bf16[32,1024]{1,0:T(8,128)(2,1)S(1)} %slice.129), channel_id=1, source_target_pairs={{0,2},{1,3},{2,0},{3,1},{4,6},{5,7},{6,4},{7,5},{8,10},{9,11},{10,... | collective-permute-start | bytes 196616 | tf_op jit(solution)/shard_map/ppermute | solution.py:707
  413.7 5.6 %collective-permute-start.14 = (bf16[2,2,16,1024]{3,2,1,0:T(8,128)(2,1)S(1)}, bf16[2,2,16,1024]{3,2,1,0:T(8,128)(2,1)S(1)}, u32[]{:S(2)}, u32[]{:S(2)}) collective-permute-start(bf16[2,2,16,1024]{3,2,1,0:T(8,128)(2,1)S(1)} %fusion.12), channel_id=1, source_target_pairs={{0,4},{4,0},{8,12},{12,8},{16,20},{20,16},{24,28},{28,24},{1,5},{5... | collective-permute-start | bytes 393224 | tf_op jit(solution)/shard_map/ppermute | solution.py:580
  419.4 5.0 %collective-permute-start.15 = (bf16[2,2,16,1024]{3,2,1,0:T(8,128)(2,1)S(1)}, bf16[2,2,16,1024]{3,2,1,0:T(8,128)(2,1)S(1)}, u32[]{:S(2)}, u32[]{:S(2)}) collective-permute-start(bf16[2,2,16,1024]{3,2,1,0:T(8,128)(2,1)S(1)} %fusion.8), channel_id=1, source_target_pairs={{0,8},{4,12},{8,0},{12,4},{16,24},{20,28},{24,16},{28,20},{1,9},{5... | collective-permute-start | bytes 393224 | tf_op jit(solution)/shard_map/ppermute | solution.py:580
  424.5 7.1 %collective-permute-start.16 = (bf16[2,2,16,1024]{3,2,1,0:T(8,128)(2,1)S(1)}, bf16[2,2,16,1024]{3,2,1,0:T(8,128)(2,1)S(1)}, u32[]{:S(2)}, u32[]{:S(2)}) collective-permute-start(bf16[2,2,16,1024]{3,2,1,0:T(8,128)(2,1)S(1)} %fusion.10), channel_id=1, source_target_pairs={{0,16},{4,20},{8,24},{12,28},{16,0},{20,4},{24,8},{28,12},{1,17},{... | collective-permute-start | bytes 393224 | tf_op jit(solution)/shard_map/ppermute | solution.py:580
Sparse Core Ops, SparseCore 0:
  10.9 197.4 all-gather.4
  211.2 119.3 all-gather.2

commit v4 on v3

--- a/solution.py
+++ b/solution.py
@@ -62,9 +62,8 @@
 
     def wait(self, *names):
         for name in names:
-            copy = self.copies.pop(name, None)
-            if copy is not None:
-                copy.wait()
+            if name in self.copies:
+                self.copies.pop(name).wait()
 
 
 def square(ref, columns=slice(None)):
@@ -200,7 +199,7 @@
     inverse[...] = r
 
 
-def feed_back_steps(loads, grad_two, slope, normed_one, inverse_one, gain_one, up, down, weights, low, hidden, grad_one, heads_grad):
+def feed_back_steps(loads, grad_two, slope, normed_one, inverse_one, gain_one, up, down, weights, low, hidden, grad_one, heads_grad, grad_out):
     tokens, width = grad_two.shape
     low[pl.ds(0, tokens), :] = grad_two.astype(BF16)
     grad_one[...] = grad_two
@@ -210,29 +209,31 @@
         place = pl.ds(r * size, size)
         back = nt(low[pl.ds(0, tokens), :], down[r].reshape(size, width))
         hidden[:, place] = (back * slope[:, place].astype(F32)).astype(BF16)
-    for b in range(up.shape[0]):
-        loads.wait(("up", b))
     rows = up.shape[2]
-    for c in range(0, width, 512):
-        total = grad_one[:, pl.ds(c, 512)]
-        for b in range(up.shape[0]):
-            block = up[b, pl.ds(c // rows, 512 // rows)].reshape(512, width)
-            total = total + nt(hidden[:, pl.ds(b * width, width)], block)
-        grad_one[:, pl.ds(c, 512)] = total
+    for b in range(0, up.shape[0], 2):
+        loads.wait(("up", b), ("up", b + 1))
+        for c in range(0, width, 512):
+            total = grad_one[:, pl.ds(c, 512)]
+            for i in (b, b + 1):
+                block = up[i, pl.ds(c // rows, 512 // rows)].reshape(512, width)
+                total = total + nt(hidden[:, pl.ds(i * width, width)], block)
+            grad_one[:, pl.ds(c, 512)] = total
     loads.wait("normed_one")
     back = norm_back(grad_one[...], gain_one[...], normed_one[...], inverse_one[...])
     grad_one[...] = back
+    loads.start("grad_out", grad_one, grad_out)
     low[pl.ds(0, tokens), :] = back.astype(BF16)
     low[pl.ds(tokens, LANES - tokens), :] = jnp.zeros((LANES - tokens, width), BF16)
     loads.wait(("square", 3))
     heads_grad[...] = nt(square(weights.at[0]), low[...]).astype(BF16)
 
 
-def attention_back_steps(loads, heads_grad, heads_t, query_t, value8, key_t, attend, weights, key_grad, value_grad, query_grad_t, steps, outs):
-    (query_grad, key_own, value_own, halo, prefix_grad) = outs
-    tokens, width = query_grad.shape
+def attention_back_steps(loads, heads_grad, heads_t, query_t, value8, key_t, attend, weights, key_grad, value_grad, query_grad_t, query_rows, steps, outs):
+    (query_grad, key_own, value_own, near_grad, across_grad, edge_grad, prefix_grad) = outs
+    tokens, width = query_rows.shape
     keys = attend.shape[1]
     span = keys - prefix_grad.shape[1]
+    loads.wait("low_out")
     loads.wait("heads_t", "query_t", "value8", "key_t")
     step = 128
     for p in range(PAIRS):
@@ -257,18 +258,23 @@
         for half in range(2):
             place = pl.ds(p * 128 + half * HD, HD)
             query_grad_t[place, :] = nn(key_t[place, :], here[:, pl.ds(half * LANES, LANES)]).astype(BF16)
-    query_grad[...] = query_grad_t[...].T[:tokens]
-    key_own[...] = key_grad[pl.ds(0, tokens), :]
-    value_own[...] = value_grad[pl.ds(0, tokens), :]
+    query_rows[...] = query_grad_t[...].T[:tokens]
+    loads.start("query_out", query_rows, query_grad)
+    loads.start("key_out", key_grad.at[pl.ds(0, tokens)], key_own)
+    loads.start("value_out", value_grad.at[pl.ds(0, tokens)], value_own)
     loads.wait(("square", 1), ("square", 2))
     outer = pl.ds(tokens, span - tokens)
     rows = weights.shape[2]
     for c in range(0, width, 512):
         part = pl.ds(c // rows, 512 // rows)
-        halo[:, pl.ds(c, 512)] = (
+        outer_grad = (
             nt(key_grad[outer, :], weights[1, part].reshape(512, width))
             + nt(value_grad[outer, :], weights[2, part].reshape(512, width))
         ).astype(BF16)
+        near_grad[:, pl.ds(c, 512)] = outer_grad[:tokens]
+        across_grad[:, pl.ds(c, 512)] = outer_grad[tokens : 2 * tokens]
+        edge_grad[pl.ds(0, EDGE), pl.ds(c, 512)] = outer_grad[2 * tokens :]
+    loads.wait("grad_out", "query_out", "key_out", "value_out")
 
 
 def load_saved(loads, gathered, start, saved, weights, buffers):
@@ -280,14 +286,26 @@
     load_attention(loads, gathered, start, [1, 2], weights.at[pl.ds(1, 2)])
 
 
+def input_back_steps(loads, weights, grad_one, sides, grad_input):
+    width = grad_one.shape[1]
+    rows = weights.shape[2]
+    for kind in range(3):
+        loads.wait(("side", kind), ("square", kind))
+        before = grad_one if kind == 0 else grad_input
+        for c in range(0, width, 512):
+            columns = pl.ds(c, 512)
+            part = nt(sides[kind], weights[kind, pl.ds(c // rows, 512 // rows)].reshape(512, width))
+            grad_input[:, columns] = before[:, columns] + (SCORE_SCALE * part if kind == 0 else part)
+
+
 def last_kernel(feed_start, attention_start, *refs):
-    (feed, squares, middle, up_bias, gain_two, shift_two, cotangent, inverse_one, gain_one, normed_hbm) = refs[:10]
-    saved = refs[10:15]
-    low_out, grad_one = refs[15:17]
-    outs = refs[17:22]
-    (up, down, weights, slope, low, hidden, normed_one, heads_grad) = refs[22:30]
-    buffers = refs[30:35]
-    (key_grad, value_grad, query_grad_t, steps, sems) = refs[35:]
+    (feed, squares, middle, up_bias, gain_two, shift_two, cotangent, inverse_one, gain_one) = refs[:9]
+    normed_hbm, saved = refs[9], refs[10:15]
+    low_out, grad_out = refs[15:17]
+    outs = refs[17:24]
+    (up, down, weights, slope, low, hidden, grad_one, query_rows, normed_one, heads_grad) = refs[24:34]
+    buffers = refs[34:39]
+    (key_grad, value_grad, query_grad_t, steps, sems) = refs[39:]
     loads = Loads(sems)
     load_up(loads, feed, feed_start, up)
     load_down(loads, feed, feed_start, down)
@@ -296,26 +314,29 @@
     result, n, r = feed_forward_steps(
         loads, middle, up_bias, gain_two, shift_two, up, down, low, hidden, slope, grad_one
     )
-    low_out[...] = result.astype(BF16)
+    query_rows[...] = result.astype(BF16)
+    loads.start("low_out", query_rows, low_out)
     grad_two = norm_back(cotangent[...].astype(F32), gain_two[...], n, r)
     feed_back_steps(
-        loads, grad_two, slope, normed_one, inverse_one, gain_one, up, down, weights, low, hidden, grad_one, heads_grad
+        loads, grad_two, slope, normed_one, inverse_one, gain_one, up, down, weights, low, hidden, grad_one, heads_grad, grad_out
     )
     attention_back_steps(
-        loads, heads_grad, *buffers[:5], weights, key_grad, value_grad, query_grad_t, steps, outs
+        loads, heads_grad, *buffers[:5], weights, key_grad, value_grad, query_grad_t, query_rows, steps, outs
     )
 
 
 def back_kernel(feed_start, attention_start, *refs):
-    (flag, feed, squares, grad, near, across, edge, inverse_two, gain_two, inverse_one, gain_one) = refs[:11]
-    (normed_two_hbm, slope_hbm, normed_one_hbm) = refs[11:14]
-    saved = refs[14:19]
-    grad_one = refs[19]
-    outs = refs[20:25]
-    (up, down, weights, slope, low, hidden, normed_two, normed_one, heads_grad) = refs[25:34]
-    buffers = refs[34:39]
-    (key_grad, value_grad, query_grad_t, steps, sems) = refs[39:]
-    tokens, width = grad.shape
+    (flag, feed, squares) = refs[:3]
+    (grad, near, across, edge, inverse_two, gain_two, inverse_one, gain_one, prefix_after) = refs[3:12]
+    (normed_two_hbm, slope_hbm, normed_one_hbm) = refs[12:15]
+    saved = refs[15:20]
+    grad_out = refs[20]
+    outs = refs[21:27]
+    edge_grad, prefix_kept = refs[26:28]
+    (up, down, weights, slope, low, hidden, grad_one, query_rows, normed_two, normed_one, heads_grad) = refs[28:39]
+    buffers = refs[39:44]
+    (key_grad, value_grad, query_grad_t, steps, prefix_grad, sems) = refs[44:]
+    tokens, width = grad_one.shape
     loads = Loads(sems)
     loads.start("normed_two", normed_two_hbm, normed_two)
     loads.start("slope", slope_hbm, slope)
@@ -333,27 +354,30 @@
     grad_two = norm_back(grad_one[...], gain_two[...], normed_two[...], inverse_two[...])
     loads.wait("slope")
     feed_back_steps(
-        loads, grad_two, slope, normed_one, inverse_one, gain_one, up, down, weights, low, hidden, grad_one, heads_grad
+        loads, grad_two, slope, normed_one, inverse_one, gain_one, up, down, weights, low, hidden, grad_one, heads_grad, grad_out
     )
     attention_back_steps(
-        loads, heads_grad, *buffers[:5], weights, key_grad, value_grad, query_grad_t, steps, outs
-    )
-
-
-def input_back_kernel(start, *refs):
-    (gathered, grad_one, query_grad, key_own, value_own, grad_input, weights, sems) = refs
-    width = grad_one.shape[1]
-    rows = weights.shape[2]
+        loads, heads_grad, *buffers[:5], weights, key_grad, value_grad, query_grad_t, query_rows, steps, (*outs, prefix_grad)
+    )
+    half = prefix_kept.shape[1]
+    mine = 1 - flag[0]
+    for layer, part in enumerate((prefix_grad, prefix_after)):
+        for i in range(2):
+            at = 2 * layer + i
+            prefix_kept[at] = part[i, ds(mine * half, half), :]
+            edge_grad[pl.ds(EDGE + at * half, half), :] = part[i, ds((1 - mine) * half, half), :].astype(BF16)
+
+
+def input_back_kernel(start, through, *refs):
+    (gathered, grad_hbm, query_hbm, key_hbm, value_hbm) = refs[:5]
+    (grad_input, weights, grad_one, sides, sems) = refs[5 + 2 * through :]
     loads = Loads(sems)
-    load_attention(loads, gathered, start, range(3), weights)
-    for kind in range(3):
-        loads.wait(("square", kind))
-        left, scale = ((query_grad, SCORE_SCALE), (key_own, None), (value_own, None))[kind]
-        before = grad_one if kind == 0 else grad_input
-        for c in range(0, width, 512):
-            columns = pl.ds(c, 512)
-            part = nt(left[...], weights[kind, pl.ds(c // rows, 512 // rows)].reshape(512, width))
-            grad_input[:, columns] = before[:, columns] + (part if scale is None else scale * part)
+    loads.start("grad", grad_hbm, grad_one)
+    for kind, source in enumerate((query_hbm, key_hbm, value_hbm)):
+        loads.start(("side", kind), source, sides.at[kind])
+        load_attention(loads, gathered, start, [kind], weights.at[pl.ds(kind, 1)])
+    loads.wait("grad")
+    input_back_steps(loads, weights, grad_one, sides, grad_input)
 
 
 def pack_kernel(place, query, key, value, out, up, down, first, second, sems):
@@ -386,15 +410,17 @@
 VMEM = pl.BlockSpec(memory_space=pltpu.VMEM)
 SMEM = pl.BlockSpec(memory_space=pltpu.SMEM)
 ANY = pl.BlockSpec(memory_space=pl.ANY)
-
-
-def call(kernel, numbers, kept, operands, late, outs, scratch, limit, flops, sem_count, small=()):
+HBM = pl.BlockSpec(memory_space=pltpu.HBM)
+
+
+def call(kernel, numbers, kept, operands, late, outs, scratch, limit, flops, sem_count, small=(), copied=0, aliases={}):
     moved = sum(x.size * x.dtype.itemsize for x in (*operands, *late)) + 16 * MIB
     return pl.pallas_call(
         partial(kernel, *numbers),
-        out_shape=outs,
+        out_shape=[shape(*x.shape, dtype=x.dtype) for x in outs],
+        input_output_aliases=aliases,
         in_specs=[SMEM] * len(small) + [ANY] * len(kept) + [VMEM] * len(operands) + [ANY] * len(late),
-        out_specs=[VMEM] * len(outs),
+        out_specs=[HBM] * copied + [VMEM] * (len(outs) - copied),
         scratch_shapes=[*scratch, pltpu.SemaphoreType.DMA((sem_count,))],
         compiler_params=pltpu.CompilerParams(vmem_limit_bytes=limit * MIB),
         cost_estimate=pl.CostEstimate(flops=flops, bytes_accessed=moved, transcendentals=0),
@@ -405,13 +431,10 @@
     return jax.ShapeDtypeStruct(sizes, dtype)
 
 
-def feed_scratch(gathered, wide):
+def feed_shapes(gathered, wide):
     parts, places, _, rows, width = gathered.shape
     ratio = wide // width
-    return [
-        pltpu.VMEM((ratio, parts, rows, width), BF16),
-        pltpu.VMEM((parts, places // 2, 2 * ratio // places, rows, width), BF16),
-    ]
+    return [shape(ratio, parts, rows, width), shape(parts, places // 2, 2 * ratio // places, rows, width)]
 
 
 def squares_scratch(gathered, count):
@@ -470,22 +493,22 @@
             shape(tokens, 1, dtype=F32),
             shape(tokens, wide),
         ],
-        [*feed_scratch(gathered, wide), pltpu.VMEM((tokens, wide), BF16)],
+        [*[pltpu.VMEM(x.shape, BF16) for x in feed_shapes(gathered, wide)], pltpu.VMEM((tokens, wide), BF16)],
         40,
         4 * tokens * width * wide,
         wide // width + gathered.shape[0],
     )
 
 
-def back_shapes(tokens, width, keys, prefix):
-    span = keys - prefix
+def back_shapes(tokens, width):
     return [
         shape(tokens, width, dtype=F32),
         shape(tokens, width),
         shape(tokens, width),
         shape(tokens, width),
-        shape(span - tokens, width),
-        shape(2, prefix, width, dtype=F32),
+        shape(tokens, width),
+        shape(tokens, width),
+        shape(EDGE, width),
     ]
 
 
@@ -501,49 +524,55 @@
     ]
 
 
-def layer_call(kernel, small, operands, late, outs, kinds, saved, feed, squares, wide, tokens):
-    gathered = feed[0]
-    parts, _, _, _, width = gathered.shape
-    ratio = wide // width
+def layer_call(kernel, numbers, small, kept, operands, late, outs, copied, kinds, saved, wide, tokens, limit, extra=()):
+    parts, _, _, _, width = kept[0].shape
     return call(
         kernel,
-        [feed[1], squares[1]],
-        [feed[0], squares[0]],
+        numbers,
+        kept,
         operands,
         [*late, *saved],
         outs,
         [
-            *feed_scratch(gathered, wide),
-            squares_scratch(gathered, 3),
+            *[pltpu.VMEM(x.shape, BF16) for x in feed_shapes(kept[0], wide)],
+            squares_scratch(kept[0], 3),
             pltpu.VMEM((tokens, wide), BF16),
             pltpu.VMEM((LANES, width), BF16),
             pltpu.VMEM((tokens, wide), BF16),
+            pltpu.VMEM((tokens, width), F32),
+            pltpu.VMEM((tokens, width), BF16),
             *[pltpu.VMEM((tokens, width), F32)] * kinds,
             pltpu.VMEM((width, LANES), BF16),
             *saved_scratch(saved),
+            *extra,
         ],
-        52,
+        limit,
         8 * tokens * width * wide,
-        ratio + parts + 3 + 4 + PAIRS + 3,
+        wide // width + parts + 3 + 4 + PAIRS + 6 + 9,
         small,
-    )
-
-
-def input_back(grad_one, query_grad, key_own, value_own, weights):
+        copied,
+    )
+
+
+def input_back(grad_one, query_grad, key_own, value_own, weights, through=()):
     gathered, start = weights
     tokens, width = grad_one.shape
-    return call(
+    outs = call(
         input_back_kernel,
-        [start],
+        [start, len(through)],
         [gathered],
-        [grad_one, query_grad, key_own, value_own],
         [],
-        [shape(tokens, width, dtype=F32)],
-        [squares_scratch(gathered, 3)],
+        [grad_one, query_grad, key_own, value_own, *through],
+        [*through, shape(tokens, width, dtype=F32)],
+        [squares_scratch(gathered, 3), pltpu.VMEM((tokens, width), F32), pltpu.VMEM((3, tokens, width), BF16)],
         30,
         6 * tokens * width * width,
-        3,
-    )[0]
+        7,
+        (),
+        len(through),
+        {5 + i: i for i in range(len(through))},
+    )
+    return outs[-1], *outs[:-1]
 
 
 def pack(place, w_query, w_key, w_value, w_out, w_up, w_down, each):
@@ -561,17 +590,15 @@
     return [(i, i ^ bit) for i in range(count)]
 
 
-def sum_prefixes(parts):
-    layers, two, prefix, width = parts.shape
+def sum_prefixes(total):
+    place = lax.axis_index("keys")
     places = lax.axis_size("keys")
-    place = lax.axis_index("keys")
-    total = parts
-    step = places // 2
+    step = places // 4
     while step:
-        split = total.reshape(layers, two, 2, -1, width)
+        split = total.reshape(total.shape[0], 2, -1, total.shape[2])
         mine = (place // step) % 2
-        sent = lax.dynamic_index_in_dim(split, 1 - mine, 2, False).astype(BF16)
-        kept = lax.dynamic_index_in_dim(split, mine, 2, False)
+        sent = lax.dynamic_index_in_dim(split, 1 - mine, 1, False).astype(BF16)
+        kept = lax.dynamic_index_in_dim(split, mine, 1, False)
         total = kept + lax.ppermute(sent, "keys", xor_pairs(places, step)).astype(F32)
         step //= 2
     count = lax.axis_size("rows")
@@ -627,6 +654,12 @@
         )
         return near, across, edge
 
+    def send_halo(halo):
+        near = lax.ppermute(halo[0], "keys", xor_pairs(places, 1))
+        across = lax.ppermute(halo[1], "keys", [(1, 2), (2, 1)])
+        edge = lax.ppermute(halo[2], "keys", xor_pairs(places, 2))
+        return near, across, edge
+
     line = segments[0]
 
     def ids(where, start, size):
@@ -645,7 +678,7 @@
 
     low = activations[0]
     hidden = low.astype(F32)
-    kept, kept_feed = [], []
+    kept = []
     for layer in range(LAYERS):
         gains, shifts = ln_gain[layer][:, None], ln_bias[layer][:, None]
         around = exchange(low)
@@ -664,48 +697,55 @@
         kept.append(((normed_one, inverse_one), saved))
         if layer < LAYERS - 1:
             hidden, low, *second_norm = feed_forward(middle, ff_bias[layer][None], gains[1], shifts[1], feeds[layer])
-            kept_feed.append(second_norm)
 
     flag = first_half.astype(jnp.int32)[None]
-    keys = bias.shape[0]
-    prefix_parts = [None] * LAYERS
-    for layer in range(LAYERS - 1, -1, -1):
-        (normed_one, inverse_one), saved = kept[layer]
-        gains, shifts = ln_gain[layer][:, None], ln_bias[layer][:, None]
-        outs = back_shapes(tokens, width, keys, prefix)
-        if layer == LAYERS - 1:
-            result, grad_one, query_grad, key_own, value_own, halo, prefix_parts[layer] = layer_call(
-                last_kernel,
-                (),
-                [middle, ff_bias[layer][None], gains[1], shifts[1], cotangent[0], inverse_one, gains[0]],
-                [normed_one],
-                [shape(tokens, width), *outs],
-                1,
-                saved,
-                feeds[layer],
-                squares[layer],
-                wide,
-                tokens,
-            )
-        else:
-            normed_two, inverse_two, slope = kept_feed[layer]
-            grad_one, query_grad, key_own, value_own, halo, prefix_parts[layer] = layer_call(
-                back_kernel,
-                (flag,),
-                [gradient, near, across, edge, inverse_two, gains[1], inverse_one, gains[0]],
-                [normed_two, slope, normed_one],
-                outs,
-                2,
-                saved,
-                feeds[layer],
-                squares[layer],
-                wide,
-                tokens,
-            )
-        near = lax.ppermute(halo[:tokens], "keys", xor_pairs(places, 1))
-        across = lax.ppermute(halo[tokens : 2 * tokens], "keys", [(1, 2), (2, 1)])
-        edge = lax.ppermute(halo[2 * tokens :], "keys", xor_pairs(places, 2))
-        gradient = input_back(grad_one, query_grad, key_own, value_own, squares[layer])
+    back = back_shapes(tokens, width)
+    both = shape(2, prefix, width, dtype=F32)
+    (normed_one, inverse_one), saved = kept[1]
+    gains, shifts = ln_gain[1][:, None], ln_bias[1][:, None]
+    result, grad_one, query_grad, key_own, value_own, *halo, prefix_after = layer_call(
+        last_kernel,
+        [feeds[1][1], squares[1][1]],
+        (),
+        [feeds[1][0], squares[1][0]],
+        [middle, ff_bias[1][None], gains[1], shifts[1], cotangent[0], inverse_one, gains[0]],
+        [normed_one],
+        [shape(tokens, width), *back, both],
+        5,
+        1,
+        saved,
+        wide,
+        tokens,
+        52,
+    )
+    near, across, edge = send_halo(halo)
+    (gradient,) = input_back(grad_one, query_grad, key_own, value_own, squares[1])
+    (normed_one, inverse_one), saved = kept[0]
+    normed_two, inverse_two, slope = second_norm
+    gains = ln_gain[0][:, None]
+    half = prefix // 2
+    back[-1] = shape(EDGE + LAYERS * 2 * half, width)
+    grad_one, query_grad, key_own, value_own, *halo, prefix_kept = layer_call(
+        back_kernel,
+        [feeds[0][1], squares[0][1]],
+        (flag,),
+        [feeds[0][0], squares[0][0]],
+        [gradient, near, across, edge, inverse_two, gains[1], inverse_one, gains[0], prefix_after],
+        [normed_two, slope, normed_one],
+        [*back, shape(LAYERS * 2, half, width, dtype=F32)],
+        4,
+        2,
+        saved,
+        wide,
+        tokens,
+        50,
+        [pltpu.VMEM(both.shape, F32)],
+    )
+    near, across, edge = send_halo(halo)
+    gradient, prefix_kept = input_back(grad_one, query_grad, key_own, value_own, squares[0], [prefix_kept])
+    prefix_total = sum_prefixes(prefix_kept + edge[EDGE:].reshape(LAYERS * 2, half, width).astype(F32))
+    prefix_total = prefix_total.reshape(LAYERS, 2, prefix // places, width)
+    edge = edge[:EDGE]
     extra = edge.astype(F32)
     lead = jnp.where(first_half, 0.0, extra)
     tail = jnp.where(first_half, extra, 0.0)
@@ -715,7 +755,6 @@
         + across.astype(F32)
         + jnp.concatenate([lead, jnp.zeros((tokens - 2 * EDGE, width), F32), tail], 0)
     )
-    prefix_total = sum_prefixes(jnp.stack(prefix_parts))
     return (
         result[None],
         gradient[None],

time: 447 us -> 443 us (level)
    ppermute x2 -> x1, waiting for transfers between devices: 6.32 us -> 1.33 us  [sum_prefixes(): lax.ppermute(sent, 'keys', xor_pairs(places, step)).astype(F32)]
    unnamed x54 -> x52, local copies, waits for them, and re-layouts: 12 us -> 15.3 us
  transfers between devices with their start and end apart: 19 -> 18, of which waited for: 9 -> 9; matrix products, arithmetic and copies ran while one was open for 1% -> 0% of each run, Pallas kernels for 12% -> 13%
where the time goes in v4:
time: 443 us; the launch traced here: 435 us
  waiting for transfers between devices  255 us (58%)
  Pallas kernels  113 us (26%)
  starting transfers between devices  20.6 us (5%)
  local copies, waits for them, and re-layouts  16.4 us (4%)
  between operations  14.9 us (3%)
  blocking collectives  13.2 us (3%)
    all_gather x2, waiting for transfers between devices, gather(): whole = lax.all_gather(share, ('rows', 'keys'), axis=0, tiled=True)  222 us
    pallas_call x7, Pallas kernels, call(): pl.pallas_call(partial(kernel, *numbers), out_shape=[shape(*x.shape, dtyp...  111 us
    ppermute x2, waiting for transfers between devices, exchange(): lax.ppermute(jnp.where(first_half, low[tokens - EDGE:], low[:EDGE]), 'key...  16.5 us
    unnamed x52, local copies, waits for them, and re-layouts  15.3 us
    all_gather x1, blocking collectives, body(): lax.all_gather(jnp.stack([prefix_keys, prefix_values]), 'keys', axis=2, t...  13.2 us
    ppermute x3, waiting for transfers between devices, sum_prefixes(): lax.ppermute(total.astype(BF16), 'rows', xor_pairs(count, step)).astype(F32)  10 us
  transfers between devices with their start and end apart: 18, of which 9 were waited for; matrix products, arithmetic and copies ran while one was open for 0% of the time, Pallas kernels for 13%

profile of v4, /device:TPU:0, one launch (start us, length us, event | category | flops | bytes accessed | tf_op | source)
XLA Modules:
  0.0 435.1 jit_solution(5067428895464538262)
XLA Ops:
  7.3 2.6 shard_map.165
  10.0 0.0 all-gather.3.cloned.1.call-start
  10.0 0.7 all-gather.3.cloned.1.call-update
  10.7 0.5 collective-permute-start
  11.3 1.4 collective-permute-start.1
  12.7 3.1 collective-permute-start.2
  15.8 0.1 fusion.4
  15.9 0.1 constant_dynamic-slice_fusion.2
  15.9 0.1 pad_add_fusion
  16.0 13.2 %all_gather.11 = bf16[2,2,64,1024]{3,2,1,0:T(8,128)(2,1)S(1)} all-gather(bf16[2,2,16,1024]{3,2,1,0:T(8,128)(2,1)S(1)} %pad_maximum_fusion), channel_id=1, replica_groups=mesh['rows'=8,'keys'=4] {'keys'}, dimensions={2}, use_global_device_ids=true | all-gather | bytes 655360 | tf_op jit(solution)/shard_map/all_gather | solution.py:677
  29.2 0.2 broadcast_compare_fusion
  29.6 0.1 bitcast_convert_fusion.1.refs_5_
  29.7 0.1 pad_select_fusion
  29.8 0.1 pad.5.refs_6_
  29.9 178.5 %all-gather.5.cloned.1.call-done = bf16[128,128,1024]{2,1,0:T(8,128)(2,1)} async-done(((bf16[4,128,1024]{2,1,0:T(8,128)(2,1)}), bf16[128,128,1024]{2,1,0:T(8,128)(2,1)}) %all-gather.5.cloned.1.call-update) | async-done | bytes 33554448 | tf_op jit(solution)/shard_map/all_gather | solution.py:642
  208.4 18.7 %shard_map.166 = (f32[224,1024]{1,0:T(8,128)S(1)}, f32[224,1024]{1,0:T(8,128)S(1)}, f32[224,1]{1,0:T(8,128)S(1)}, bf16[1024,256]{1,0:T(8,128)(2,1)S(1)}, bf16[8,...) custom-call(bf16[8,4,4,128,1024]{4,3,2,1,0:T(8,128)(2,1)} %bitcast.7, ...), custom_call_target="tpu_custom_call" | custom-call | flops 3758096384 | bytes 20193280 | tf_op jit(solution)/shard_map/pallas_call | solution.py:418
  227.1 1.0 copy-done.8
  228.1 1.0 copy-done.10
  229.1 9.6 %shard_map.167 = (f32[224,1024]{1,0:T(8,128)S(1)}, bf16[224,1024]{1,0:T(8,128)(2,1)S(1)}, f32[224,1024]{1,0:T(8,128)S(1)}, f32[224,1]{1,0:T(8,128)S(1)}, bf16[224,4096]{1,0:T(8,128)(2,1)S(1)}) custom-call(bf16[8,4,4,128,1024]{4,3,2,1,0:T(8,128)(2,1)} %bitcast.71, f32[224,1024]{1,0:T(8,128)S(1)} %get-tuple-element.48.refs_1_, ...), custom_call_target="tpu_custom_call" | custom-call | flops 3758096384 | bytes 17719296 | tf_op jit(solution)/shard_map/pallas_call | solution.py:418
  238.7 1.2 copy-done.3
  240.0 0.9 copy-done.11
  240.9 0.3 collective-permute-start.3
  241.2 1.1 collective-permute-start.4
  242.3 3.2 collective-permute-start.5
  245.5 16.5 %collective-permute-done.5.refs_4_ = bf16[32,1024]{1,0:T(8,128)(2,1)S(1)} collective-permute-done((bf16[32,1024]{1,0:T(8,128)(2,1)S(1)}, bf16[32,1024]{1,0:T(8,128)(2,1)S(1)}, u32[]{:S(2)}, u32[]{:S(2)}) %collective-permute-start.5) | collective-permute-done | bytes 65568 | tf_op jit(solution)/shard_map/ppermute | solution.py:652
  262.0 18.8 %shard_map.168 = (f32[224,1024]{1,0:T(8,128)S(1)}, f32[224,1024]{1,0:T(8,128)S(1)}, f32[224,1]{1,0:T(8,128)S(1)}, bf16[1024,256]{1,0:T(8,128)(2,1)S(1)}, bf16[8,...) custom-call(bf16[8,4,4,128,1024]{4,3,2,1,0:T(8,128)(2,1)} %bitcast.7, ...), custom_call_target="tpu_custom_call" | custom-call | flops 3758096384 | bytes 20193280 | tf_op jit(solution)/shard_map/pallas_call | solution.py:418
  280.8 1.2 copy-done.6
  282.0 1.2 copy-done.7
  283.1 1.0 copy-done.9
  284.1 0.9 copy-done.12
  285.1 1.0 copy-done.13
  286.0 0.8 copy-done.17
  286.9 43.8 %all-gather.3.cloned.1.call-done = bf16[64,128,1024]{2,1,0:T(8,128)(2,1)} async-done(((bf16[2,128,1024]{2,1,0:T(8,128)(2,1)}), bf16[64,128,1024]{2,1,0:T(8,128)(2,1)}) %all-gather.3.cloned.1.call-update) | async-done | bytes 16777232 | tf_op jit(solution)/shard_map/all_gather | solution.py:642
  330.6 30.0 %shard_map.169 = (bf16[224,1024]{1,0:T(8,128)(2,1)}, f32[224,1024]{1,0:T(8,128)}, bf16[224,1024]{1,0:T(8,128)(2,1)S(1)}, bf16[224,1024]{1,0:T(8,128)(2,1)S(1)}, ...) custom-call(bf16[8,4,2,128,1024]{4,3,2,1,0:T(8,128)(2,1)} %bitcast.7, ...), custom_call_target="tpu_custom_call" | custom-call | flops 7516192768 | bytes 30110592 | tf_op jit(solution)/shard_map/pallas_call | solution.py:418
  360.6 0.3 collective-permute-start.6
  360.9 0.7 collective-permute-start.7
  361.6 3.2 collective-permute-start.8
  364.8 1.2 copy-done.15
  365.9 4.4 %shard_map.170.refs_3_ = f32[224,1024]{1,0:T(8,128)S(1)} custom-call(bf16[8,4,4,128,1024]{4,3,2,1,0:T(8,128)(2,1)} %bitcast.74, f32[224,1024]{1,0:T(8,128)S(1)} %copy-done.15, bf16[224,1024]{1,0:T(8,128)(2,1)S(1)} %get-tuple-element.61.refs_2_, bf16[224,1024]{1,0:T(8,128)(2,1)S(1)} %get-tuple-element.62.refs_3_, bf16[224,1024]{1,0:T(8,128)(2,1)S(1)} %get-tuple-element.63.refs_4_), custom_call_target="tpu_custom_call" | custom-call | flops 1409286144 | bytes 19070976 | tf_op jit(solution)/shard_map/pallas_call | solution.py:418
  370.3 0.9 copy-done
  371.3 1.5 collective-permute-done.8.refs_6_
  372.7 25.0 %shard_map.171 = (f32[224,1024]{1,0:T(8,128)}, bf16[224,1024]{1,0:T(8,128)(2,1)S(1)}, bf16[224,1024]{1,0:T(8,128)(2,1)S(1)}, bf16[224,1024]{1,0:T(8,128)(2,1)S(1...) custom-call(s32[1]{0:T(128)} %bitcast.25.refs_0_, ...), custom_call_target="tpu_custom_call" | custom-call | flops 7516192768 | bytes 33892096 | tf_op jit(solution)/shard_map/pallas_call | solution.py:418
  397.8 0.8 copy-done.18
  398.5 0.1 collective-permute-start.11
  398.7 1.0 copy-done.2
  399.7 1.2 copy-done.14
  400.9 4.4 %shard_map.172 = (f32[4,32,1024]{2,1,0:T(8,128)S(1)}, f32[224,1024]{1,0:T(8,128)S(1)}) custom-call(bf16[8,4,4,128,1024]{4,3,2,1,0:T(8,128)(2,1)} %bitcast.77, f32[224,1024]{1,0:T(8,128)S(1)} %copy-done.14, bf16[224,1024]{1,0:T(8,128)(2,1)S(1)} %get-tuple-element.79.refs_2_, ...), custom_call_target="tpu_custom_call", output_to_operand_aliasing={{0}: (5, {})} | custom-call | flops 1409286144 | bytes 19595264 | tf_op jit(solution)/shard_map/pallas_call | solution.py:418
  405.3 2.2 collective-permute-done.11
  407.5 0.1 convert_add_fusion
  407.6 0.1 collective-permute-start.12
  407.7 1.3 collective-permute-done.12
  409.0 1.3 collective-permute-start.13
  410.4 0.1 pad.7.clone
  410.5 0.7 collective-permute-start.10
  411.1 2.5 collective-permute-start.9
  413.6 1.0 collective-permute-done.13
  414.7 0.5 collective-permute-start.14
  415.2 4.5 %collective-permute-done.14 = bf16[4,16,1024]{2,1,0:T(8,128)(2,1)S(1)} collective-permute-done((bf16[4,16,1024]{2,1,0:T(8,128)(2,1)S(1)}, bf16[4,16,1024]{2,1,0:T(8,128)(2,1)S(1)}, u32[]{:S(2)}, u32[]{:S(2)}) %collective-permute-start.14) | collective-permute-done | bytes 131104 | tf_op jit(solution)/shard_map/ppermute | solution.py:607
  419.7 0.1 fusion.3
  419.8 1.6 collective-permute-start.15
  421.4 1.1 fusion
  422.5 4.5 %collective-permute-done.15 = bf16[4,16,1024]{2,1,0:T(8,128)(2,1)S(1)} collective-permute-done((bf16[4,16,1024]{2,1,0:T(8,128)(2,1)S(1)}, bf16[4,16,1024]{2,1,0:T(8,128)(2,1)S(1)}, u32[]{:S(2)}, u32[]{:S(2)}) %collective-permute-start.15) | collective-permute-done | bytes 131104 | tf_op jit(solution)/shard_map/ppermute | solution.py:607
  427.0 0.1 convert_add_fusion.1
  427.1 0.7 slice_bitcast_fusion
  (60 shorter events, 0.4 us)
Async XLA Ops:
  7.2 201.2 %all-gather.5.cloned.1.call-start = ((), (), s32[]{:S(2)}) async-start(), calls=%async_computation.1 | async-start | bytes 34603008 | tf_op jit(solution)/shard_map/all_gather | solution.py:642
  7.2 3.5 copy-start.1
  7.2 8.6 %copy-start.25 = (s32[1,896]{1,0:T(1,128)S(1)}, s32[1,896]{1,0:T(1,128)}, u32[]{:S(2)}) copy-start(s32[1,896]{1,0:T(1,128)} %param.15) | copy-start | bytes 10756
  7.2 8.8 %copy-start.20 = (bf16[2,16,1024]{2,1,0:T(8,128)(2,1)S(1)}, bf16[2,16,1024]{2,1,0:T(8,128)(2,1)}, u32[]{:S(2)}) copy-start(bf16[2,16,1024]{2,1,0:T(8,128)(2,1)} %param.17) | copy-start | bytes 196612
  7.2 8.8 %copy-start.21 = (bf16[2,16,1024]{2,1,0:T(8,128)(2,1)S(1)}, bf16[2,16,1024]{2,1,0:T(8,128)(2,1)}, u32[]{:S(2)}) copy-start(bf16[2,16,1024]{2,1,0:T(8,128)(2,1)} %param.16) | copy-start | bytes 196612
  9.9 19.6 %copy-start.22 = (f32[2,4096]{1,0:T(2,128)S(1)}, f32[2,4096]{1,0:T(2,128)}, u32[]{:S(2)}) copy-start(f32[2,4096]{1,0:T(2,128)} %param.23) | copy-start | bytes 98308
  9.9 19.6 %copy-start.23 = (f32[2,2,1024]{2,1,0:T(2,128)S(1)}, f32[2,2,1024]{2,1,0:T(2,128)}, u32[]{:S(2)}) copy-start(f32[2,2,1024]{2,1,0:T(2,128)} %param.26) | copy-start | bytes 49156
  9.9 19.6 %copy-start.24 = (f32[2,2,1024]{2,1,0:T(2,128)S(1)}, f32[2,2,1024]{2,1,0:T(2,128)}, u32[]{:S(2)}) copy-start(f32[2,2,1024]{2,1,0:T(2,128)} %param.25) | copy-start | bytes 49156
  10.0 320.6 %all-gather.3.cloned.1.call-start = ((), (), s32[]{:S(2)}) async-start(), calls=%async_computation | async-start | bytes 17301504 | tf_op jit(solution)/shard_map/all_gather | solution.py:642
  10.7 19.1 %collective-permute-start = (bf16[224,1024]{1,0:T(8,128)(2,1)S(1)}, bf16[224,1024]{1,0:T(8,128)(2,1)S(1)}, u32[]{:S(2)}, u32[]{:S(2)}) collective-permute-start(bf16[224,1024]{1,0:T(8,128)(2,1)S(1)} %bitcast.67), channel_id=1, source_target_pairs={{0,1},{1,0},{2,3},{3,2},{4,5},{5,4},{6,7},{7,6},{8,9},{9,8},{10,11... | collective-permute-start | bytes 1376264 | tf_op jit(solution)/shard_map/ppermute | solution.py:650
  11.3 18.6 %collective-permute-start.1 = (bf16[224,1024]{1,0:T(8,128)(2,1)S(1)}, bf16[224,1024]{1,0:T(8,128)(2,1)}, u32[]{:S(2)}, u32[]{:S(2)}) collective-permute-start(bf16[224,1024]{1,0:T(8,128)(2,1)S(1)} %bitcast.68), channel_id=1, source_target_pairs={{1,2},{2,1},{5,6},{6,5},{9,10},{10,9},{13,14},{14,13},{17,18},{18,... | collective-permute-start | bytes 1376264 | tf_op jit(solution)/shard_map/ppermute | solution.py:651
  12.7 17.1 %collective-permute-start.2 = (bf16[32,1024]{1,0:T(8,128)(2,1)S(1)}, bf16[32,1024]{1,0:T(8,128)(2,1)S(1)}, u32[]{:S(2)}, u32[]{:S(2)}) collective-permute-start(bf16[32,1024]{1,0:T(8,128)(2,1)S(1)} %select_bitcast_fusion), channel_id=1, source_target_pairs={{0,2},{1,3},{2,0},{3,1},{4,6},{5,7},{6,4},{7,5},{8,10},{9,11},{10,... | collective-permute-start | bytes 196616 | tf_op jit(solution)/shard_map/ppermute | solution.py:652
  227.1 1.0 copy-start.8
  228.1 1.0 copy-start.10
  229.1 9.6 %copy-start.4 = (bf16[8,768,128]{2,1,0:T(8,128)(2,1)}, bf16[8,768,128]{2,1,0:T(8,128)(2,1)S(1)}, u32[]{:S(2)}) copy-start(bf16[8,768,128]{2,1,0:T(8,128)(2,1)S(1)} %get-tuple-element.75.refs_17_) | copy-start | bytes 4718596
  229.1 9.6 %copy-start.5 = (bf16[1024,768]{1,0:T(8,128)(2,1)}, bf16[1024,768]{1,0:T(8,128)(2,1)S(1)}, u32[]{:S(2)}) copy-start(bf16[1024,768]{1,0:T(8,128)(2,1)S(1)} %get-tuple-element.76.refs_18_) | copy-start | bytes 4718596
  229.1 9.6 %copy-start.16 = (bf16[1024,256]{1,0:T(8,128)(2,1)}, bf16[1024,256]{1,0:T(8,128)(2,1)S(1)}, u32[]{:S(2)}) copy-start(bf16[1024,256]{1,0:T(8,128)(2,1)S(1)} %get-tuple-element.74.refs_16_) | copy-start | bytes 1572868
  238.7 1.3 copy-start.3
  240.0 0.9 copy-start.11
  240.9 21.1 %collective-permute-start.3 = (bf16[224,1024]{1,0:T(8,128)(2,1)S(1)}, bf16[224,1024]{1,0:T(8,128)(2,1)S(1)}, u32[]{:S(2)}, u32[]{:S(2)}) collective-permute-start(bf16[224,1024]{1,0:T(8,128)(2,1)S(1)} %get-tuple-element.49.refs_1_), channel_id=1, source_target_pairs={{0,1},{1,0},{2,3},{3,2},{4,5},{5,4},{6,7},{7,6},{8,9},{9,8},{10,11... | collective-permute-start | bytes 1376264 | tf_op jit(solution)/shard_map/ppermute | solution.py:650
  241.2 20.9 %collective-permute-start.4 = (bf16[224,1024]{1,0:T(8,128)(2,1)S(1)}, bf16[224,1024]{1,0:T(8,128)(2,1)S(1)}, u32[]{:S(2)}, u32[]{:S(2)}) collective-permute-start(bf16[224,1024]{1,0:T(8,128)(2,1)S(1)} %get-tuple-element.49.refs_1_), channel_id=1, source_target_pairs={{1,2},{2,1},{5,6},{6,5},{9,10},{10,9},{13,14},{14,13},{17,18},{18,... | collective-permute-start | bytes 1376264 | tf_op jit(solution)/shard_map/ppermute | solution.py:651
  242.3 19.7 %collective-permute-start.5 = (bf16[32,1024]{1,0:T(8,128)(2,1)S(1)}, bf16[32,1024]{1,0:T(8,128)(2,1)S(1)}, u32[]{:S(2)}, u32[]{:S(2)}) collective-permute-start(bf16[32,1024]{1,0:T(8,128)(2,1)S(1)} %slice_select_fusion), channel_id=1, source_target_pairs={{0,2},{1,3},{2,0},{3,1},{4,6},{5,7},{6,4},{7,5},{8,10},{9,11},{10,... | collective-permute-start | bytes 196616 | tf_op jit(solution)/shard_map/ppermute | solution.py:652
  280.8 1.2 copy-start.6
  282.0 1.2 copy-start.7
  283.1 1.0 copy-start.9
  284.1 0.9 copy-start.12
  285.1 1.0 copy-start.13
  286.0 0.8 copy-start.17
  360.6 12.2 %collective-permute-start.6 = (bf16[224,1024]{1,0:T(8,128)(2,1)}, bf16[224,1024]{1,0:T(8,128)(2,1)S(1)}, u32[]{:S(2)}, u32[]{:S(2)}) collective-permute-start(bf16[224,1024]{1,0:T(8,128)(2,1)} %get-tuple-element.64), channel_id=1, source_target_pairs={{0,1},{1,0},{2,3},{3,2},{4,5},{5,4},{6,7},{7,6},{8,9},{9,8},{10,11... | collective-permute-start | bytes 1376264 | tf_op jit(solution)/shard_map/ppermute | solution.py:658
  360.9 11.8 %collective-permute-start.7 = (bf16[224,1024]{1,0:T(8,128)(2,1)}, bf16[224,1024]{1,0:T(8,128)(2,1)S(1)}, u32[]{:S(2)}, u32[]{:S(2)}) collective-permute-start(bf16[224,1024]{1,0:T(8,128)(2,1)} %get-tuple-element.65), channel_id=1, source_target_pairs={{1,2},{2,1},{5,6},{6,5},{9,10},{10,9},{13,14},{14,13},{17,18},{18,... | collective-permute-start | bytes 1376264 | tf_op jit(solution)/shard_map/ppermute | solution.py:659
  361.6 11.1 %collective-permute-start.8 = (bf16[32,1024]{1,0:T(8,128)(2,1)S(1)}, bf16[32,1024]{1,0:T(8,128)(2,1)S(1)}, u32[]{:S(2)}, u32[]{:S(2)}) collective-permute-start(bf16[32,1024]{1,0:T(8,128)(2,1)S(1)} %get-tuple-element.66), channel_id=1, source_target_pairs={{0,2},{1,3},{2,0},{3,1},{4,6},{5,7},{6,4},{7,5},{8,10},{9,11},{10,... | collective-permute-start | bytes 196616 | tf_op jit(solution)/shard_map/ppermute | solution.py:660
  364.8 1.2 copy-start.15
  370.3 0.9 copy-start
  397.8 0.8 copy-start.18
  398.5 8.9 %collective-permute-start.11 = (bf16[160,1024]{1,0:T(8,128)(2,1)}, bf16[160,1024]{1,0:T(8,128)(2,1)S(1)}, u32[]{:S(2)}, u32[]{:S(2)}) collective-permute-start(bf16[160,1024]{1,0:T(8,128)(2,1)} %get-tuple-element.86), channel_id=1, source_target_pairs={{0,2},{1,3},{2,0},{3,1},{4,6},{5,7},{6,4},{7,5},{8,10},{9,11},{10,... | collective-permute-start | bytes 983048 | tf_op jit(solution)/shard_map/ppermute | solution.py:660
  398.7 1.0 copy-start.2
  399.7 1.2 copy-start.14
  405.3 5.2 %copy-start.19 = (bf16[224,1024]{1,0:T(8,128)(2,1)S(1)}, bf16[224,1024]{1,0:T(8,128)(2,1)}, u32[]{:S(2)}) copy-start(bf16[224,1024]{1,0:T(8,128)(2,1)} %copy-done.18) | copy-start | bytes 1376260
  407.6 1.4 collective-permute-start.12
  409.0 5.6 %collective-permute-start.13 = (bf16[4,16,1024]{2,1,0:T(8,128)(2,1)S(1)}, bf16[4,16,1024]{2,1,0:T(8,128)(2,1)S(1)}, u32[]{:S(2)}, u32[]{:S(2)}) collective-permute-start(bf16[4,16,1024]{2,1,0:T(8,128)(2,1)S(1)} %fusion.5), channel_id=1, source_target_pairs={{0,4},{4,0},{8,12},{12,8},{16,20},{20,16},{24,28},{28,24},{1,5},{5... | collective-permute-start | bytes 393224 | tf_op jit(solution)/shard_map/ppermute | solution.py:607
  410.5 10.9 %collective-permute-start.10 = (bf16[224,1024]{1,0:T(8,128)(2,1)S(1)}, bf16[224,1024]{1,0:T(8,128)(2,1)S(1)}, u32[]{:S(2)}, u32[]{:S(2)}) collective-permute-start(bf16[224,1024]{1,0:T(8,128)(2,1)S(1)} %copy-done.19), channel_id=1, source_target_pairs={{1,2},{2,1},{5,6},{6,5},{9,10},{10,9},{13,14},{14,13},{17,18},{18,... | collective-permute-start | bytes 1376264 | tf_op jit(solution)/shard_map/ppermute | solution.py:659
  411.1 10.2 %collective-permute-start.9 = (bf16[224,1024]{1,0:T(8,128)(2,1)S(1)}, bf16[224,1024]{1,0:T(8,128)(2,1)S(1)}, u32[]{:S(2)}, u32[]{:S(2)}) collective-permute-start(bf16[224,1024]{1,0:T(8,128)(2,1)S(1)} %get-tuple-element.84), channel_id=1, source_target_pairs={{0,1},{1,0},{2,3},{3,2},{4,5},{5,4},{6,7},{7,6},{8,9},{9,8},{10,11... | collective-permute-start | bytes 1376264 | tf_op jit(solution)/shard_map/ppermute | solution.py:658
  414.7 5.0 %collective-permute-start.14 = (bf16[4,16,1024]{2,1,0:T(8,128)(2,1)S(1)}, bf16[4,16,1024]{2,1,0:T(8,128)(2,1)S(1)}, u32[]{:S(2)}, u32[]{:S(2)}) collective-permute-start(bf16[4,16,1024]{2,1,0:T(8,128)(2,1)S(1)} %fusion.1), channel_id=1, source_target_pairs={{0,8},{4,12},{8,0},{12,4},{16,24},{20,28},{24,16},{28,20},{1,9},{5... | collective-permute-start | bytes 393224 | tf_op jit(solution)/shard_map/ppermute | solution.py:607
  419.8 7.2 %collective-permute-start.15 = (bf16[4,16,1024]{2,1,0:T(8,128)(2,1)S(1)}, bf16[4,16,1024]{2,1,0:T(8,128)(2,1)S(1)}, u32[]{:S(2)}, u32[]{:S(2)}) collective-permute-start(bf16[4,16,1024]{2,1,0:T(8,128)(2,1)S(1)} %fusion.3), channel_id=1, source_target_pairs={{0,16},{4,20},{8,24},{12,28},{16,0},{20,4},{24,8},{28,12},{1,17},{... | collective-permute-start | bytes 393224 | tf_op jit(solution)/shard_map/ppermute | solution.py:607
Sparse Core Ops, SparseCore 0:
  10.9 197.4 all-gather.4
  211.2 119.3 all-gather.2

commit v5 on v4

--- a/solution.py
+++ b/solution.py
@@ -566,7 +566,7 @@
         [*through, shape(tokens, width, dtype=F32)],
         [squares_scratch(gathered, 3), pltpu.VMEM((tokens, width), F32), pltpu.VMEM((3, tokens, width), BF16)],
         30,
-        6 * tokens * width * width,
+        1 << 36,
         7,
         (),
         len(through),
@@ -655,9 +655,9 @@
         return near, across, edge
 
     def send_halo(halo):
-        near = lax.ppermute(halo[0], "keys", xor_pairs(places, 1))
         across = lax.ppermute(halo[1], "keys", [(1, 2), (2, 1)])
         edge = lax.ppermute(halo[2], "keys", xor_pairs(places, 2))
+        near = lax.ppermute(halo[0], "keys", xor_pairs(places, 1))
         return near, across, edge
 
     line = segments[0]

time: 443 us -> 442 us (level)
    unnamed x52 -> x60, local copies, waits for them, and re-layouts: 15.3 us -> 16.6 us
  transfers between devices with their start and end apart: 18 -> 18, of which waited for: 9 -> 9; matrix products, arithmetic and copies ran while one was open for 0% -> 1% of each run, Pallas kernels for 13% -> 13%
where the time goes in v5:
time: 442 us; the launch traced here: 434 us
  waiting for transfers between devices  253 us (57%)
  Pallas kernels  113 us (26%)
  starting transfers between devices  20.6 us (5%)
  local copies, waits for them, and re-layouts  18.3 us (4%)
  between operations  14.9 us (3%)
  blocking collectives  13.1 us (3%)
    all_gather x2, waiting for transfers between devices, gather(): whole = lax.all_gather(share, ('rows', 'keys'), axis=0, tiled=True)  222 us
    pallas_call x7, Pallas kernels, call(): pl.pallas_call(partial(kernel, *numbers), out_shape=[shape(*x.shape, dtyp...  110 us
    unnamed x60, local copies, waits for them, and re-layouts  16.6 us
    ppermute x2, waiting for transfers between devices, exchange(): lax.ppermute(jnp.where(first_half, low[tokens - EDGE:], low[:EDGE]), 'key...  15.8 us
    all_gather x1, blocking collectives, body(): lax.all_gather(jnp.stack([prefix_keys, prefix_values]), 'keys', axis=2, t...  13.1 us
    ppermute x3, waiting for transfers between devices, sum_prefixes(): lax.ppermute(total.astype(BF16), 'rows', xor_pairs(count, step)).astype(F32)  10.1 us
  transfers between devices with their start and end apart: 18, of which 9 were waited for; matrix products, arithmetic and copies ran while one was open for 1% of the time, Pallas kernels for 13%

profile of v5, /device:TPU:0, one launch (start us, length us, event | category | flops | bytes accessed | tf_op | source)
XLA Modules:
  0.0 434.5 jit_solution(13957124094324766659)
XLA Ops:
  7.3 2.6 shard_map.165
  10.0 0.7 all-gather.3.cloned.1.call-update
  10.7 0.5 collective-permute-start
  11.2 1.4 collective-permute-start.1
  12.7 3.1 collective-permute-start.2
  15.8 0.1 fusion.4
  15.8 0.1 constant_dynamic-slice_fusion.2
  15.9 0.1 pad_add_fusion
  16.0 13.1 %all_gather.11 = bf16[2,2,64,1024]{3,2,1,0:T(8,128)(2,1)S(1)} all-gather(bf16[2,2,16,1024]{3,2,1,0:T(8,128)(2,1)S(1)} %pad_maximum_fusion), channel_id=1, replica_groups=mesh['rows'=8,'keys'=4] {'keys'}, dimensions={2}, use_global_device_ids=true | all-gather | bytes 655360 | tf_op jit(solution)/shard_map/all_gather | solution.py:677
  29.2 0.2 broadcast_compare_fusion
  29.4 0.6 slice_bitcast_fusion.6
  30.1 0.1 bitcast_convert_fusion.1.refs_5_
  30.2 0.1 pad_select_fusion
  30.4 178.0 %all-gather.5.cloned.1.call-done = bf16[128,128,1024]{2,1,0:T(8,128)(2,1)} async-done(((bf16[4,128,1024]{2,1,0:T(8,128)(2,1)}), bf16[128,128,1024]{2,1,0:T(8,128)(2,1)}) %all-gather.5.cloned.1.call-update) | async-done | bytes 33554448 | tf_op jit(solution)/shard_map/all_gather | solution.py:642
  208.4 18.7 %shard_map.166 = (f32[224,1024]{1,0:T(8,128)S(1)}, f32[224,1024]{1,0:T(8,128)S(1)}, f32[224,1]{1,0:T(8,128)S(1)}, bf16[1024,256]{1,0:T(8,128)(2,1)S(1)}, bf16[8,...) custom-call(bf16[8,4,4,128,1024]{4,3,2,1,0:T(8,128)(2,1)} %bitcast.7, ...), custom_call_target="tpu_custom_call" | custom-call | flops 3758096384 | bytes 20193280 | tf_op jit(solution)/shard_map/pallas_call | solution.py:418
  227.1 1.0 copy-done.6
  228.1 1.0 copy-done.8
  229.1 9.6 %shard_map.167 = (f32[224,1024]{1,0:T(8,128)S(1)}, bf16[224,1024]{1,0:T(8,128)(2,1)S(1)}, f32[224,1024]{1,0:T(8,128)S(1)}, f32[224,1]{1,0:T(8,128)S(1)}, bf16[224,4096]{1,0:T(8,128)(2,1)S(1)}) custom-call(bf16[8,4,4,128,1024]{4,3,2,1,0:T(8,128)(2,1)} %bitcast.71, f32[224,1024]{1,0:T(8,128)S(1)} %get-tuple-element.48.refs_1_, ...), custom_call_target="tpu_custom_call" | custom-call | flops 3758096384 | bytes 17719296 | tf_op jit(solution)/shard_map/pallas_call | solution.py:418
  238.8 1.3 copy-done.1
  240.1 0.9 copy-done.9
  241.0 0.6 copy-done.18
  241.6 0.2 collective-permute-start.3
  241.9 1.1 collective-permute-start.4
  243.1 3.2 collective-permute-start.5
  246.2 15.8 %collective-permute-done.5.refs_4_ = bf16[32,1024]{1,0:T(8,128)(2,1)S(1)} collective-permute-done((bf16[32,1024]{1,0:T(8,128)(2,1)S(1)}, bf16[32,1024]{1,0:T(8,128)(2,1)S(1)}, u32[]{:S(2)}, u32[]{:S(2)}) %collective-permute-start.5) | collective-permute-done | bytes 65568 | tf_op jit(solution)/shard_map/ppermute | solution.py:652
  262.0 0.7 copy-done.21
  262.7 18.0 %shard_map.168 = (f32[224,1024]{1,0:T(8,128)S(1)}, f32[224,1024]{1,0:T(8,128)S(1)}, f32[224,1]{1,0:T(8,128)S(1)}, bf16[1024,256]{1,0:T(8,128)(2,1)S(1)}, bf16[8,...) custom-call(bf16[8,4,4,128,1024]{4,3,2,1,0:T(8,128)(2,1)} %bitcast.7, ...), custom_call_target="tpu_custom_call" | custom-call | flops 3758096384 | bytes 20193280 | tf_op jit(solution)/shard_map/pallas_call | solution.py:418
  280.7 1.2 copy-done.4
  281.9 1.2 copy-done.5
  283.0 1.0 copy-done.7
  284.0 0.9 copy-done.11
  285.0 1.0 copy-done.12
  285.9 0.8 copy-done.14
  286.7 43.6 %all-gather.3.cloned.1.call-done = bf16[64,128,1024]{2,1,0:T(8,128)(2,1)} async-done(((bf16[2,128,1024]{2,1,0:T(8,128)(2,1)}), bf16[64,128,1024]{2,1,0:T(8,128)(2,1)}) %all-gather.3.cloned.1.call-update) | async-done | bytes 16777232 | tf_op jit(solution)/shard_map/all_gather | solution.py:642
  330.3 0.7 copy-done.20
  331.0 30.0 %shard_map.169 = (bf16[224,1024]{1,0:T(8,128)(2,1)}, f32[224,1024]{1,0:T(8,128)}, bf16[224,1024]{1,0:T(8,128)(2,1)S(1)}, bf16[224,1024]{1,0:T(8,128)(2,1)S(1)}, ...) custom-call(bf16[8,4,2,128,1024]{4,3,2,1,0:T(8,128)(2,1)} %bitcast.7, ...), custom_call_target="tpu_custom_call" | custom-call | flops 7516192768 | bytes 30110592 | tf_op jit(solution)/shard_map/pallas_call | solution.py:418
  361.0 0.3 collective-permute-start.6
  361.3 0.7 collective-permute-start.7
  362.0 3.1 collective-permute-start.8
  365.2 1.2 copy-done.22
  366.4 4.4 %shard_map.170.refs_3_ = f32[224,1024]{1,0:T(8,128)S(1)} custom-call(bf16[8,4,4,128,1024]{4,3,2,1,0:T(8,128)(2,1)} %bitcast.74, f32[224,1024]{1,0:T(8,128)S(1)} %copy-done.22, bf16[224,1024]{1,0:T(8,128)(2,1)S(1)} %get-tuple-element.61.refs_2_, bf16[224,1024]{1,0:T(8,128)(2,1)S(1)} %get-tuple-element.62.refs_3_, bf16[224,1024]{1,0:T(8,128)(2,1)S(1)} %get-tuple-element.63.refs_4_), custom_call_target="tpu_custom_call" | custom-call | flops 68719476736 | bytes 19070976 | tf_op jit(solution)/shard_map/pallas_call | solution.py:418
  370.8 0.9 copy-done.10
  371.7 1.5 collective-permute-done.8.refs_6_
  373.2 24.9 %shard_map.171 = (f32[224,1024]{1,0:T(8,128)}, bf16[224,1024]{1,0:T(8,128)(2,1)S(1)}, bf16[224,1024]{1,0:T(8,128)(2,1)S(1)}, bf16[224,1024]{1,0:T(8,128)(2,1)S(1...) custom-call(s32[1]{0:T(128)} %bitcast.25.refs_0_, ...), custom_call_target="tpu_custom_call" | custom-call | flops 7516192768 | bytes 33892096 | tf_op jit(solution)/shard_map/pallas_call | solution.py:418
  398.1 0.1 collective-permute-start.11
  398.2 1.0 copy-done.15
  399.3 1.2 copy-done.23
  400.5 4.4 %shard_map.172 = (f32[4,32,1024]{2,1,0:T(8,128)S(1)}, f32[224,1024]{1,0:T(8,128)S(1)}) custom-call(bf16[8,4,4,128,1024]{4,3,2,1,0:T(8,128)(2,1)} %bitcast.77, f32[224,1024]{1,0:T(8,128)S(1)} %copy-done.23, bf16[224,1024]{1,0:T(8,128)(2,1)S(1)} %get-tuple-element.79.refs_2_, ...), custom_call_target="tpu_custom_call", output_to_operand_aliasing={{0}: (5, {})} | custom-call | flops 68719476736 | bytes 19595264 | tf_op jit(solution)/shard_map/pallas_call | solution.py:418
  404.9 2.0 collective-permute-done.11
  407.0 0.1 collective-permute-start.12
  407.1 1.3 collective-permute-done.12
  408.4 1.3 collective-permute-start.13
  409.7 0.1 pad.7.clone
  409.8 0.7 collective-permute-start.10
  410.5 2.5 collective-permute-start.9
  413.0 1.0 collective-permute-done.13
  414.1 0.5 collective-permute-start.14
  414.6 4.5 %collective-permute-done.14 = bf16[4,16,1024]{2,1,0:T(8,128)(2,1)S(1)} collective-permute-done((bf16[4,16,1024]{2,1,0:T(8,128)(2,1)S(1)}, bf16[4,16,1024]{2,1,0:T(8,128)(2,1)S(1)}, u32[]{:S(2)}, u32[]{:S(2)}) %collective-permute-start.14) | collective-permute-done | bytes 131104 | tf_op jit(solution)/shard_map/ppermute | solution.py:607
  419.1 0.1 fusion.3
  419.2 1.6 collective-permute-start.15
  420.8 1.1 fusion
  421.9 4.5 %collective-permute-done.15 = bf16[4,16,1024]{2,1,0:T(8,128)(2,1)S(1)} collective-permute-done((bf16[4,16,1024]{2,1,0:T(8,128)(2,1)S(1)}, bf16[4,16,1024]{2,1,0:T(8,128)(2,1)S(1)}, u32[]{:S(2)}, u32[]{:S(2)}) %collective-permute-start.15) | collective-permute-done | bytes 131104 | tf_op jit(solution)/shard_map/ppermute | solution.py:607
  426.4 0.1 convert_add_fusion.1
  426.5 0.7 slice_bitcast_fusion
  (68 shorter events, 0.6 us)
Async XLA Ops:
  7.2 201.2 %all-gather.5.cloned.1.call-start = ((), (), s32[]{:S(2)}) async-start(), calls=%async_computation.1 | async-start | bytes 34603008 | tf_op jit(solution)/shard_map/all_gather | solution.py:642
  7.2 3.5 copy-start
  7.2 8.5 %copy-start.29 = (s32[1,896]{1,0:T(1,128)S(1)}, s32[1,896]{1,0:T(1,128)}, u32[]{:S(2)}) copy-start(s32[1,896]{1,0:T(1,128)} %param.15) | copy-start | bytes 10756
  7.2 8.8 %copy-start.24 = (bf16[2,16,1024]{2,1,0:T(8,128)(2,1)S(1)}, bf16[2,16,1024]{2,1,0:T(8,128)(2,1)}, u32[]{:S(2)}) copy-start(bf16[2,16,1024]{2,1,0:T(8,128)(2,1)} %param.17) | copy-start | bytes 196612
  7.2 8.8 %copy-start.25 = (bf16[2,16,1024]{2,1,0:T(8,128)(2,1)S(1)}, bf16[2,16,1024]{2,1,0:T(8,128)(2,1)}, u32[]{:S(2)}) copy-start(bf16[2,16,1024]{2,1,0:T(8,128)(2,1)} %param.16) | copy-start | bytes 196612
  9.9 19.5 %copy-start.26 = (f32[2,4096]{1,0:T(2,128)S(1)}, f32[2,4096]{1,0:T(2,128)}, u32[]{:S(2)}) copy-start(f32[2,4096]{1,0:T(2,128)} %param.23) | copy-start | bytes 98308
  9.9 19.5 %copy-start.27 = (f32[2,2,1024]{2,1,0:T(2,128)S(1)}, f32[2,2,1024]{2,1,0:T(2,128)}, u32[]{:S(2)}) copy-start(f32[2,2,1024]{2,1,0:T(2,128)} %param.26) | copy-start | bytes 49156
  9.9 19.5 %copy-start.28 = (f32[2,2,1024]{2,1,0:T(2,128)S(1)}, f32[2,2,1024]{2,1,0:T(2,128)}, u32[]{:S(2)}) copy-start(f32[2,2,1024]{2,1,0:T(2,128)} %param.25) | copy-start | bytes 49156
  9.9 320.4 %all-gather.3.cloned.1.call-start = ((), (), s32[]{:S(2)}) async-start(), calls=%async_computation | async-start | bytes 17301504 | tf_op jit(solution)/shard_map/all_gather | solution.py:642
  10.7 19.6 %collective-permute-start = (bf16[224,1024]{1,0:T(8,128)(2,1)S(1)}, bf16[224,1024]{1,0:T(8,128)(2,1)S(1)}, u32[]{:S(2)}, u32[]{:S(2)}) collective-permute-start(bf16[224,1024]{1,0:T(8,128)(2,1)S(1)} %bitcast.67), channel_id=1, source_target_pairs={{0,1},{1,0},{2,3},{3,2},{4,5},{5,4},{6,7},{7,6},{8,9},{9,8},{10,11... | collective-permute-start | bytes 1376264 | tf_op jit(solution)/shard_map/ppermute | solution.py:650
  11.2 19.1 %collective-permute-start.1 = (bf16[224,1024]{1,0:T(8,128)(2,1)S(1)}, bf16[224,1024]{1,0:T(8,128)(2,1)}, u32[]{:S(2)}, u32[]{:S(2)}) collective-permute-start(bf16[224,1024]{1,0:T(8,128)(2,1)S(1)} %bitcast.68), channel_id=1, source_target_pairs={{1,2},{2,1},{5,6},{6,5},{9,10},{10,9},{13,14},{14,13},{17,18},{18,... | collective-permute-start | bytes 1376264 | tf_op jit(solution)/shard_map/ppermute | solution.py:651
  12.7 17.6 %collective-permute-start.2 = (bf16[32,1024]{1,0:T(8,128)(2,1)S(1)}, bf16[32,1024]{1,0:T(8,128)(2,1)S(1)}, u32[]{:S(2)}, u32[]{:S(2)}) collective-permute-start(bf16[32,1024]{1,0:T(8,128)(2,1)S(1)} %select_bitcast_fusion), channel_id=1, source_target_pairs={{0,2},{1,3},{2,0},{3,1},{4,6},{5,7},{6,4},{7,5},{8,10},{9,11},{10,... | collective-permute-start | bytes 196616 | tf_op jit(solution)/shard_map/ppermute | solution.py:652
  227.1 1.0 copy-start.6
  228.1 1.0 copy-start.8
  229.1 9.6 %copy-start.2 = (bf16[8,768,128]{2,1,0:T(8,128)(2,1)}, bf16[8,768,128]{2,1,0:T(8,128)(2,1)S(1)}, u32[]{:S(2)}) copy-start(bf16[8,768,128]{2,1,0:T(8,128)(2,1)S(1)} %get-tuple-element.75.refs_17_) | copy-start | bytes 4718596
  229.1 9.7 %copy-start.3 = (bf16[1024,768]{1,0:T(8,128)(2,1)}, bf16[1024,768]{1,0:T(8,128)(2,1)S(1)}, u32[]{:S(2)}) copy-start(bf16[1024,768]{1,0:T(8,128)(2,1)S(1)} %get-tuple-element.76.refs_18_) | copy-start | bytes 4718596
  229.1 9.7 %copy-start.13 = (bf16[1024,256]{1,0:T(8,128)(2,1)}, bf16[1024,256]{1,0:T(8,128)(2,1)S(1)}, u32[]{:S(2)}) copy-start(bf16[1024,256]{1,0:T(8,128)(2,1)S(1)} %get-tuple-element.74.refs_16_) | copy-start | bytes 1572868
  229.1 9.7 %copy-start.16 = (f32[224,1]{1,0:T(8,128)}, f32[224,1]{1,0:T(8,128)S(1)}, u32[]{:S(2)}) copy-start(f32[224,1]{1,0:T(8,128)S(1)} %get-tuple-element.68.refs_9_) | copy-start | bytes 2692
  238.8 1.3 copy-start.1
  240.1 0.9 copy-start.9
  241.0 0.6 copy-start.18
  241.6 20.4 %collective-permute-start.3 = (bf16[224,1024]{1,0:T(8,128)(2,1)S(1)}, bf16[224,1024]{1,0:T(8,128)(2,1)S(1)}, u32[]{:S(2)}, u32[]{:S(2)}) collective-permute-start(bf16[224,1024]{1,0:T(8,128)(2,1)S(1)} %get-tuple-element.49.refs_1_), channel_id=1, source_target_pairs={{0,1},{1,0},{2,3},{3,2},{4,5},{5,4},{6,7},{7,6},{8,9},{9,8},{10,11... | collective-permute-start | bytes 1376264 | tf_op jit(solution)/shard_map/ppermute | solution.py:650
  241.9 20.1 %collective-permute-start.4 = (bf16[224,1024]{1,0:T(8,128)(2,1)S(1)}, bf16[224,1024]{1,0:T(8,128)(2,1)S(1)}, u32[]{:S(2)}, u32[]{:S(2)}) collective-permute-start(bf16[224,1024]{1,0:T(8,128)(2,1)S(1)} %get-tuple-element.49.refs_1_), channel_id=1, source_target_pairs={{1,2},{2,1},{5,6},{6,5},{9,10},{10,9},{13,14},{14,13},{17,18},{18,... | collective-permute-start | bytes 1376264 | tf_op jit(solution)/shard_map/ppermute | solution.py:651
  243.1 19.0 %collective-permute-start.5 = (bf16[32,1024]{1,0:T(8,128)(2,1)S(1)}, bf16[32,1024]{1,0:T(8,128)(2,1)S(1)}, u32[]{:S(2)}, u32[]{:S(2)}) collective-permute-start(bf16[32,1024]{1,0:T(8,128)(2,1)S(1)} %slice_select_fusion), channel_id=1, source_target_pairs={{0,2},{1,3},{2,0},{3,1},{4,6},{5,7},{6,4},{7,5},{8,10},{9,11},{10,... | collective-permute-start | bytes 196616 | tf_op jit(solution)/shard_map/ppermute | solution.py:652
  262.0 0.7 copy-start.21
  280.7 1.2 copy-start.4
  281.9 1.2 copy-start.5
  283.0 1.0 copy-start.7
  284.0 0.9 copy-start.11
  285.0 1.0 copy-start.12
  285.9 0.8 copy-start.14
  330.3 0.7 copy-start.20
  361.0 12.2 %collective-permute-start.6 = (bf16[224,1024]{1,0:T(8,128)(2,1)}, bf16[224,1024]{1,0:T(8,128)(2,1)S(1)}, u32[]{:S(2)}, u32[]{:S(2)}) collective-permute-start(bf16[224,1024]{1,0:T(8,128)(2,1)} %get-tuple-element.64), channel_id=1, source_target_pairs={{0,1},{1,0},{2,3},{3,2},{4,5},{5,4},{6,7},{7,6},{8,9},{9,8},{10,11... | collective-permute-start | bytes 1376264 | tf_op jit(solution)/shard_map/ppermute | solution.py:660
  361.3 11.8 %collective-permute-start.7 = (bf16[224,1024]{1,0:T(8,128)(2,1)}, bf16[224,1024]{1,0:T(8,128)(2,1)S(1)}, u32[]{:S(2)}, u32[]{:S(2)}) collective-permute-start(bf16[224,1024]{1,0:T(8,128)(2,1)} %get-tuple-element.65), channel_id=1, source_target_pairs={{1,2},{2,1},{5,6},{6,5},{9,10},{10,9},{13,14},{14,13},{17,18},{18,... | collective-permute-start | bytes 1376264 | tf_op jit(solution)/shard_map/ppermute | solution.py:658
  362.0 11.1 %collective-permute-start.8 = (bf16[32,1024]{1,0:T(8,128)(2,1)S(1)}, bf16[32,1024]{1,0:T(8,128)(2,1)S(1)}, u32[]{:S(2)}, u32[]{:S(2)}) collective-permute-start(bf16[32,1024]{1,0:T(8,128)(2,1)S(1)} %get-tuple-element.66), channel_id=1, source_target_pairs={{0,2},{1,3},{2,0},{3,1},{4,6},{5,7},{6,4},{7,5},{8,10},{9,11},{10,... | collective-permute-start | bytes 196616 | tf_op jit(solution)/shard_map/ppermute | solution.py:659
  365.2 1.2 copy-start.22
  366.4 6.8 %copy-start.17 = (f32[224,1]{1,0:T(8,128)S(1)}, f32[224,1]{1,0:T(8,128)}, u32[]{:S(2)}) copy-start(f32[224,1]{1,0:T(8,128)} %copy-done.16) | copy-start | bytes 2692
  366.4 6.8 %copy-start.19 = (f32[224,1]{1,0:T(8,128)S(1)}, f32[224,1]{1,0:T(8,128)}, u32[]{:S(2)}) copy-start(f32[224,1]{1,0:T(8,128)} %copy-done.18) | copy-start | bytes 2692
  370.7 0.9 copy-start.10
  398.1 8.8 %collective-permute-start.11 = (bf16[160,1024]{1,0:T(8,128)(2,1)S(1)}, bf16[160,1024]{1,0:T(8,128)(2,1)S(1)}, u32[]{:S(2)}, u32[]{:S(2)}) collective-permute-start(bf16[160,1024]{1,0:T(8,128)(2,1)S(1)} %get-tuple-element.86), channel_id=1, source_target_pairs={{0,2},{1,3},{2,0},{3,1},{4,6},{5,7},{6,4},{7,5},{8,10},{9,11},{10,... | collective-permute-start | bytes 983048 | tf_op jit(solution)/shard_map/ppermute | solution.py:659
  398.2 1.0 copy-start.15
  399.3 1.2 copy-start.23
  407.0 1.4 collective-permute-start.12
  408.4 5.6 %collective-permute-start.13 = (bf16[4,16,1024]{2,1,0:T(8,128)(2,1)S(1)}, bf16[4,16,1024]{2,1,0:T(8,128)(2,1)S(1)}, u32[]{:S(2)}, u32[]{:S(2)}) collective-permute-start(bf16[4,16,1024]{2,1,0:T(8,128)(2,1)S(1)} %fusion.5), channel_id=1, source_target_pairs={{0,4},{4,0},{8,12},{12,8},{16,20},{20,16},{24,28},{28,24},{1,5},{5... | collective-permute-start | bytes 393224 | tf_op jit(solution)/shard_map/ppermute | solution.py:607
  409.8 11.0 %collective-permute-start.10 = (bf16[224,1024]{1,0:T(8,128)(2,1)S(1)}, bf16[224,1024]{1,0:T(8,128)(2,1)S(1)}, u32[]{:S(2)}, u32[]{:S(2)}) collective-permute-start(bf16[224,1024]{1,0:T(8,128)(2,1)S(1)} %get-tuple-element.85), channel_id=1, source_target_pairs={{1,2},{2,1},{5,6},{6,5},{9,10},{10,9},{13,14},{14,13},{17,18},{18,... | collective-permute-start | bytes 1376264 | tf_op jit(solution)/shard_map/ppermute | solution.py:658
  410.5 10.3 %collective-permute-start.9 = (bf16[224,1024]{1,0:T(8,128)(2,1)S(1)}, bf16[224,1024]{1,0:T(8,128)(2,1)S(1)}, u32[]{:S(2)}, u32[]{:S(2)}) collective-permute-start(bf16[224,1024]{1,0:T(8,128)(2,1)S(1)} %get-tuple-element.84), channel_id=1, source_target_pairs={{0,1},{1,0},{2,3},{3,2},{4,5},{5,4},{6,7},{7,6},{8,9},{9,8},{10,11... | collective-permute-start | bytes 1376264 | tf_op jit(solution)/shard_map/ppermute | solution.py:660
  414.1 5.0 %collective-permute-start.14 = (bf16[4,16,1024]{2,1,0:T(8,128)(2,1)S(1)}, bf16[4,16,1024]{2,1,0:T(8,128)(2,1)S(1)}, u32[]{:S(2)}, u32[]{:S(2)}) collective-permute-start(bf16[4,16,1024]{2,1,0:T(8,128)(2,1)S(1)} %fusion.1), channel_id=1, source_target_pairs={{0,8},{4,12},{8,0},{12,4},{16,24},{20,28},{24,16},{28,20},{1,9},{5... | collective-permute-start | bytes 393224 | tf_op jit(solution)/shard_map/ppermute | solution.py:607
  419.2 7.2 %collective-permute-start.15 = (bf16[4,16,1024]{2,1,0:T(8,128)(2,1)S(1)}, bf16[4,16,1024]{2,1,0:T(8,128)(2,1)S(1)}, u32[]{:S(2)}, u32[]{:S(2)}) collective-permute-start(bf16[4,16,1024]{2,1,0:T(8,128)(2,1)S(1)} %fusion.3), channel_id=1, source_target_pairs={{0,16},{4,20},{8,24},{12,28},{16,0},{20,4},{24,8},{28,12},{1,17},{... | collective-permute-start | bytes 393224 | tf_op jit(solution)/shard_map/ppermute | solution.py:607
Sparse Core Ops, SparseCore 0:
  10.9 197.4 all-gather.4
  211.2 119.0 all-gather.2

commit v6 on v4

--- a/solution.py
+++ b/solution.py
@@ -602,10 +602,10 @@
         total = kept + lax.ppermute(sent, "keys", xor_pairs(places, step)).astype(F32)
         step //= 2
     count = lax.axis_size("rows")
-    step = 1
-    while step < count:
+    step = count // 2
+    while step:
         total = total + lax.ppermute(total.astype(BF16), "rows", xor_pairs(count, step)).astype(F32)
-        step *= 2
+        step //= 2
     return total
 
 

time: 443 us -> 445 us (level)
  no operation moved by 1% of the time
where the time goes in v6:
time: 445 us; the launch traced here: 437 us
  waiting for transfers between devices  256 us (58%)
  Pallas kernels  113 us (25%)
  starting transfers between devices  20.6 us (5%)
  local copies, waits for them, and re-layouts  16.4 us (4%)
  between operations  14.9 us (3%)
  blocking collectives  13.2 us (3%)
    all_gather x2, waiting for transfers between devices, gather(): whole = lax.all_gather(share, ('rows', 'keys'), axis=0, tiled=True)  222 us
    pallas_call x7, Pallas kernels, call(): pl.pallas_call(partial(kernel, *numbers), out_shape=[shape(*x.shape, dtyp...  111 us
    ppermute x2, waiting for transfers between devices, exchange(): lax.ppermute(jnp.where(first_half, low[tokens - EDGE:], low[:EDGE]), 'key...  16.5 us
    unnamed x52, local copies, waits for them, and re-layouts  15.3 us
    all_gather x1, blocking collectives, body(): lax.all_gather(jnp.stack([prefix_keys, prefix_values]), 'keys', axis=2, t...  13.2 us
    ppermute x3, waiting for transfers between devices, sum_prefixes(): lax.ppermute(total.astype(BF16), 'rows', xor_pairs(count, step)).astype(F32)  11.9 us
  transfers between devices with their start and end apart: 18, of which 9 were waited for; matrix products, arithmetic and copies ran while one was open for 0% of the time, Pallas kernels for 13%

profile of v6, /device:TPU:0, one launch (start us, length us, event | category | flops | bytes accessed | tf_op | source)
XLA Modules:
  0.0 437.0 jit_solution(2739644316225073645)
XLA Ops:
  7.3 2.6 shard_map.165
  10.0 0.0 all-gather.3.cloned.1.call-start
  10.0 0.7 all-gather.3.cloned.1.call-update
  10.7 0.5 collective-permute-start
  11.3 1.4 collective-permute-start.1
  12.7 3.1 collective-permute-start.2
  15.8 0.1 fusion.4
  15.9 0.1 constant_dynamic-slice_fusion.2
  15.9 0.1 pad_add_fusion
  16.0 13.2 %all_gather.11 = bf16[2,2,64,1024]{3,2,1,0:T(8,128)(2,1)S(1)} all-gather(bf16[2,2,16,1024]{3,2,1,0:T(8,128)(2,1)S(1)} %pad_maximum_fusion), channel_id=1, replica_groups=mesh['rows'=8,'keys'=4] {'keys'}, dimensions={2}, use_global_device_ids=true | all-gather | bytes 655360 | tf_op jit(solution)/shard_map/all_gather | solution.py:677
  29.2 0.2 broadcast_compare_fusion
  29.6 0.1 bitcast_convert_fusion.1.refs_5_
  29.7 0.1 pad_select_fusion
  29.8 0.1 pad.5.refs_6_
  29.9 178.5 %all-gather.5.cloned.1.call-done = bf16[128,128,1024]{2,1,0:T(8,128)(2,1)} async-done(((bf16[4,128,1024]{2,1,0:T(8,128)(2,1)}), bf16[128,128,1024]{2,1,0:T(8,128)(2,1)}) %all-gather.5.cloned.1.call-update) | async-done | bytes 33554448 | tf_op jit(solution)/shard_map/all_gather | solution.py:642
  208.4 18.7 %shard_map.166 = (f32[224,1024]{1,0:T(8,128)S(1)}, f32[224,1024]{1,0:T(8,128)S(1)}, f32[224,1]{1,0:T(8,128)S(1)}, bf16[1024,256]{1,0:T(8,128)(2,1)S(1)}, bf16[8,...) custom-call(bf16[8,4,4,128,1024]{4,3,2,1,0:T(8,128)(2,1)} %bitcast.7, ...), custom_call_target="tpu_custom_call" | custom-call | flops 3758096384 | bytes 20193280 | tf_op jit(solution)/shard_map/pallas_call | solution.py:418
  227.1 1.0 copy-done.8
  228.1 1.0 copy-done.10
  229.1 9.6 %shard_map.167 = (f32[224,1024]{1,0:T(8,128)S(1)}, bf16[224,1024]{1,0:T(8,128)(2,1)S(1)}, f32[224,1024]{1,0:T(8,128)S(1)}, f32[224,1]{1,0:T(8,128)S(1)}, bf16[224,4096]{1,0:T(8,128)(2,1)S(1)}) custom-call(bf16[8,4,4,128,1024]{4,3,2,1,0:T(8,128)(2,1)} %bitcast.71, f32[224,1024]{1,0:T(8,128)S(1)} %get-tuple-element.48.refs_1_, ...), custom_call_target="tpu_custom_call" | custom-call | flops 3758096384 | bytes 17719296 | tf_op jit(solution)/shard_map/pallas_call | solution.py:418
  238.7 1.2 copy-done.3
  240.0 0.9 copy-done.11
  240.9 0.3 collective-permute-start.3
  241.2 1.1 collective-permute-start.4
  242.3 3.2 collective-permute-start.5
  245.5 16.5 %collective-permute-done.5.refs_4_ = bf16[32,1024]{1,0:T(8,128)(2,1)S(1)} collective-permute-done((bf16[32,1024]{1,0:T(8,128)(2,1)S(1)}, bf16[32,1024]{1,0:T(8,128)(2,1)S(1)}, u32[]{:S(2)}, u32[]{:S(2)}) %collective-permute-start.5) | collective-permute-done | bytes 65568 | tf_op jit(solution)/shard_map/ppermute | solution.py:652
  262.0 18.8 %shard_map.168 = (f32[224,1024]{1,0:T(8,128)S(1)}, f32[224,1024]{1,0:T(8,128)S(1)}, f32[224,1]{1,0:T(8,128)S(1)}, bf16[1024,256]{1,0:T(8,128)(2,1)S(1)}, bf16[8,...) custom-call(bf16[8,4,4,128,1024]{4,3,2,1,0:T(8,128)(2,1)} %bitcast.7, ...), custom_call_target="tpu_custom_call" | custom-call | flops 3758096384 | bytes 20193280 | tf_op jit(solution)/shard_map/pallas_call | solution.py:418
  280.8 1.2 copy-done.6
  282.0 1.2 copy-done.7
  283.1 1.0 copy-done.9
  284.1 0.9 copy-done.12
  285.1 1.0 copy-done.13
  286.0 0.8 copy-done.17
  286.9 43.8 %all-gather.3.cloned.1.call-done = bf16[64,128,1024]{2,1,0:T(8,128)(2,1)} async-done(((bf16[2,128,1024]{2,1,0:T(8,128)(2,1)}), bf16[64,128,1024]{2,1,0:T(8,128)(2,1)}) %all-gather.3.cloned.1.call-update) | async-done | bytes 16777232 | tf_op jit(solution)/shard_map/all_gather | solution.py:642
  330.6 30.0 %shard_map.169 = (bf16[224,1024]{1,0:T(8,128)(2,1)}, f32[224,1024]{1,0:T(8,128)}, bf16[224,1024]{1,0:T(8,128)(2,1)S(1)}, bf16[224,1024]{1,0:T(8,128)(2,1)S(1)}, ...) custom-call(bf16[8,4,2,128,1024]{4,3,2,1,0:T(8,128)(2,1)} %bitcast.7, ...), custom_call_target="tpu_custom_call" | custom-call | flops 7516192768 | bytes 30110592 | tf_op jit(solution)/shard_map/pallas_call | solution.py:418
  360.6 0.3 collective-permute-start.6
  360.9 0.7 collective-permute-start.7
  361.6 3.2 collective-permute-start.8
  364.8 1.2 copy-done.15
  365.9 4.4 %shard_map.170.refs_3_ = f32[224,1024]{1,0:T(8,128)S(1)} custom-call(bf16[8,4,4,128,1024]{4,3,2,1,0:T(8,128)(2,1)} %bitcast.74, f32[224,1024]{1,0:T(8,128)S(1)} %copy-done.15, bf16[224,1024]{1,0:T(8,128)(2,1)S(1)} %get-tuple-element.61.refs_2_, bf16[224,1024]{1,0:T(8,128)(2,1)S(1)} %get-tuple-element.62.refs_3_, bf16[224,1024]{1,0:T(8,128)(2,1)S(1)} %get-tuple-element.63.refs_4_), custom_call_target="tpu_custom_call" | custom-call | flops 1409286144 | bytes 19070976 | tf_op jit(solution)/shard_map/pallas_call | solution.py:418
  370.3 0.9 copy-done
  371.3 1.5 collective-permute-done.8.refs_6_
  372.7 25.0 %shard_map.171 = (f32[224,1024]{1,0:T(8,128)}, bf16[224,1024]{1,0:T(8,128)(2,1)S(1)}, bf16[224,1024]{1,0:T(8,128)(2,1)S(1)}, bf16[224,1024]{1,0:T(8,128)(2,1)S(1...) custom-call(s32[1]{0:T(128)} %bitcast.25.refs_0_, ...), custom_call_target="tpu_custom_call" | custom-call | flops 7516192768 | bytes 33892096 | tf_op jit(solution)/shard_map/pallas_call | solution.py:418
  397.8 0.8 copy-done.18
  398.5 0.1 collective-permute-start.11
  398.7 1.0 copy-done.2
  399.7 1.2 copy-done.14
  400.9 4.4 %shard_map.172 = (f32[4,32,1024]{2,1,0:T(8,128)S(1)}, f32[224,1024]{1,0:T(8,128)S(1)}) custom-call(bf16[8,4,4,128,1024]{4,3,2,1,0:T(8,128)(2,1)} %bitcast.77, f32[224,1024]{1,0:T(8,128)S(1)} %copy-done.14, bf16[224,1024]{1,0:T(8,128)(2,1)S(1)} %get-tuple-element.79.refs_2_, ...), custom_call_target="tpu_custom_call", output_to_operand_aliasing={{0}: (5, {})} | custom-call | flops 1409286144 | bytes 19595264 | tf_op jit(solution)/shard_map/pallas_call | solution.py:418
  405.3 2.2 collective-permute-done.11
  407.5 0.1 convert_add_fusion
  407.6 0.1 collective-permute-start.12
  407.7 1.3 collective-permute-done.12
  409.0 1.6 collective-permute-start.13
  410.6 0.1 pad.7.clone
  410.7 0.7 collective-permute-start.10
  411.4 2.9 collective-permute-start.9
  414.3 3.9 collective-permute-done.13
  418.2 0.1 collective-permute-start.14
  418.4 5.4 %collective-permute-done.14 = bf16[4,16,1024]{2,1,0:T(8,128)(2,1)S(1)} collective-permute-done((bf16[4,16,1024]{2,1,0:T(8,128)(2,1)S(1)}, bf16[4,16,1024]{2,1,0:T(8,128)(2,1)S(1)}, u32[]{:S(2)}, u32[]{:S(2)}) %collective-permute-start.14) | collective-permute-done | bytes 131104 | tf_op jit(solution)/shard_map/ppermute | solution.py:607
  423.8 0.1 fusion.3
  423.8 1.3 collective-permute-start.15
  425.1 1.1 fusion
  426.2 2.6 collective-permute-done.15
  428.9 0.1 convert_add_fusion.1
  429.0 0.7 slice_bitcast_fusion
  (60 shorter events, 0.4 us)
Async XLA Ops:
  7.2 201.2 %all-gather.5.cloned.1.call-start = ((), (), s32[]{:S(2)}) async-start(), calls=%async_computation.1 | async-start | bytes 34603008 | tf_op jit(solution)/shard_map/all_gather | solution.py:642
  7.2 3.5 copy-start.1
  7.2 8.6 %copy-start.25 = (s32[1,896]{1,0:T(1,128)S(1)}, s32[1,896]{1,0:T(1,128)}, u32[]{:S(2)}) copy-start(s32[1,896]{1,0:T(1,128)} %param.15) | copy-start | bytes 10756
  7.2 8.8 %copy-start.20 = (bf16[2,16,1024]{2,1,0:T(8,128)(2,1)S(1)}, bf16[2,16,1024]{2,1,0:T(8,128)(2,1)}, u32[]{:S(2)}) copy-start(bf16[2,16,1024]{2,1,0:T(8,128)(2,1)} %param.17) | copy-start | bytes 196612
  7.2 8.8 %copy-start.21 = (bf16[2,16,1024]{2,1,0:T(8,128)(2,1)S(1)}, bf16[2,16,1024]{2,1,0:T(8,128)(2,1)}, u32[]{:S(2)}) copy-start(bf16[2,16,1024]{2,1,0:T(8,128)(2,1)} %param.16) | copy-start | bytes 196612
  9.9 19.6 %copy-start.22 = (f32[2,4096]{1,0:T(2,128)S(1)}, f32[2,4096]{1,0:T(2,128)}, u32[]{:S(2)}) copy-start(f32[2,4096]{1,0:T(2,128)} %param.23) | copy-start | bytes 98308
  9.9 19.6 %copy-start.23 = (f32[2,2,1024]{2,1,0:T(2,128)S(1)}, f32[2,2,1024]{2,1,0:T(2,128)}, u32[]{:S(2)}) copy-start(f32[2,2,1024]{2,1,0:T(2,128)} %param.26) | copy-start | bytes 49156
  9.9 19.6 %copy-start.24 = (f32[2,2,1024]{2,1,0:T(2,128)S(1)}, f32[2,2,1024]{2,1,0:T(2,128)}, u32[]{:S(2)}) copy-start(f32[2,2,1024]{2,1,0:T(2,128)} %param.25) | copy-start | bytes 49156
  10.0 320.6 %all-gather.3.cloned.1.call-start = ((), (), s32[]{:S(2)}) async-start(), calls=%async_computation | async-start | bytes 17301504 | tf_op jit(solution)/shard_map/all_gather | solution.py:642
  10.7 19.1 %collective-permute-start = (bf16[224,1024]{1,0:T(8,128)(2,1)S(1)}, bf16[224,1024]{1,0:T(8,128)(2,1)S(1)}, u32[]{:S(2)}, u32[]{:S(2)}) collective-permute-start(bf16[224,1024]{1,0:T(8,128)(2,1)S(1)} %bitcast.67), channel_id=1, source_target_pairs={{0,1},{1,0},{2,3},{3,2},{4,5},{5,4},{6,7},{7,6},{8,9},{9,8},{10,11... | collective-permute-start | bytes 1376264 | tf_op jit(solution)/shard_map/ppermute | solution.py:650
  11.3 18.6 %collective-permute-start.1 = (bf16[224,1024]{1,0:T(8,128)(2,1)S(1)}, bf16[224,1024]{1,0:T(8,128)(2,1)}, u32[]{:S(2)}, u32[]{:S(2)}) collective-permute-start(bf16[224,1024]{1,0:T(8,128)(2,1)S(1)} %bitcast.68), channel_id=1, source_target_pairs={{1,2},{2,1},{5,6},{6,5},{9,10},{10,9},{13,14},{14,13},{17,18},{18,... | collective-permute-start | bytes 1376264 | tf_op jit(solution)/shard_map/ppermute | solution.py:651
  12.7 17.1 %collective-permute-start.2 = (bf16[32,1024]{1,0:T(8,128)(2,1)S(1)}, bf16[32,1024]{1,0:T(8,128)(2,1)S(1)}, u32[]{:S(2)}, u32[]{:S(2)}) collective-permute-start(bf16[32,1024]{1,0:T(8,128)(2,1)S(1)} %select_bitcast_fusion), channel_id=1, source_target_pairs={{0,2},{1,3},{2,0},{3,1},{4,6},{5,7},{6,4},{7,5},{8,10},{9,11},{10,... | collective-permute-start | bytes 196616 | tf_op jit(solution)/shard_map/ppermute | solution.py:652
  227.1 1.0 copy-start.8
  228.1 1.0 copy-start.10
  229.1 9.6 %copy-start.4 = (bf16[8,768,128]{2,1,0:T(8,128)(2,1)}, bf16[8,768,128]{2,1,0:T(8,128)(2,1)S(1)}, u32[]{:S(2)}) copy-start(bf16[8,768,128]{2,1,0:T(8,128)(2,1)S(1)} %get-tuple-element.75.refs_17_) | copy-start | bytes 4718596
  229.1 9.6 %copy-start.5 = (bf16[1024,768]{1,0:T(8,128)(2,1)}, bf16[1024,768]{1,0:T(8,128)(2,1)S(1)}, u32[]{:S(2)}) copy-start(bf16[1024,768]{1,0:T(8,128)(2,1)S(1)} %get-tuple-element.76.refs_18_) | copy-start | bytes 4718596
  229.1 9.6 %copy-start.16 = (bf16[1024,256]{1,0:T(8,128)(2,1)}, bf16[1024,256]{1,0:T(8,128)(2,1)S(1)}, u32[]{:S(2)}) copy-start(bf16[1024,256]{1,0:T(8,128)(2,1)S(1)} %get-tuple-element.74.refs_16_) | copy-start | bytes 1572868
  238.7 1.3 copy-start.3
  240.0 0.9 copy-start.11
  240.9 21.1 %collective-permute-start.3 = (bf16[224,1024]{1,0:T(8,128)(2,1)S(1)}, bf16[224,1024]{1,0:T(8,128)(2,1)S(1)}, u32[]{:S(2)}, u32[]{:S(2)}) collective-permute-start(bf16[224,1024]{1,0:T(8,128)(2,1)S(1)} %get-tuple-element.49.refs_1_), channel_id=1, source_target_pairs={{0,1},{1,0},{2,3},{3,2},{4,5},{5,4},{6,7},{7,6},{8,9},{9,8},{10,11... | collective-permute-start | bytes 1376264 | tf_op jit(solution)/shard_map/ppermute | solution.py:650
  241.2 20.9 %collective-permute-start.4 = (bf16[224,1024]{1,0:T(8,128)(2,1)S(1)}, bf16[224,1024]{1,0:T(8,128)(2,1)S(1)}, u32[]{:S(2)}, u32[]{:S(2)}) collective-permute-start(bf16[224,1024]{1,0:T(8,128)(2,1)S(1)} %get-tuple-element.49.refs_1_), channel_id=1, source_target_pairs={{1,2},{2,1},{5,6},{6,5},{9,10},{10,9},{13,14},{14,13},{17,18},{18,... | collective-permute-start | bytes 1376264 | tf_op jit(solution)/shard_map/ppermute | solution.py:651
  242.3 19.7 %collective-permute-start.5 = (bf16[32,1024]{1,0:T(8,128)(2,1)S(1)}, bf16[32,1024]{1,0:T(8,128)(2,1)S(1)}, u32[]{:S(2)}, u32[]{:S(2)}) collective-permute-start(bf16[32,1024]{1,0:T(8,128)(2,1)S(1)} %slice_select_fusion), channel_id=1, source_target_pairs={{0,2},{1,3},{2,0},{3,1},{4,6},{5,7},{6,4},{7,5},{8,10},{9,11},{10,... | collective-permute-start | bytes 196616 | tf_op jit(solution)/shard_map/ppermute | solution.py:652
  280.8 1.2 copy-start.6
  282.0 1.2 copy-start.7
  283.1 1.0 copy-start.9
  284.1 0.9 copy-start.12
  285.1 1.0 copy-start.13
  286.0 0.8 copy-start.17
  360.6 12.2 %collective-permute-start.6 = (bf16[224,1024]{1,0:T(8,128)(2,1)}, bf16[224,1024]{1,0:T(8,128)(2,1)S(1)}, u32[]{:S(2)}, u32[]{:S(2)}) collective-permute-start(bf16[224,1024]{1,0:T(8,128)(2,1)} %get-tuple-element.64), channel_id=1, source_target_pairs={{0,1},{1,0},{2,3},{3,2},{4,5},{5,4},{6,7},{7,6},{8,9},{9,8},{10,11... | collective-permute-start | bytes 1376264 | tf_op jit(solution)/shard_map/ppermute | solution.py:658
  360.9 11.8 %collective-permute-start.7 = (bf16[224,1024]{1,0:T(8,128)(2,1)}, bf16[224,1024]{1,0:T(8,128)(2,1)S(1)}, u32[]{:S(2)}, u32[]{:S(2)}) collective-permute-start(bf16[224,1024]{1,0:T(8,128)(2,1)} %get-tuple-element.65), channel_id=1, source_target_pairs={{1,2},{2,1},{5,6},{6,5},{9,10},{10,9},{13,14},{14,13},{17,18},{18,... | collective-permute-start | bytes 1376264 | tf_op jit(solution)/shard_map/ppermute | solution.py:659
  361.6 11.1 %collective-permute-start.8 = (bf16[32,1024]{1,0:T(8,128)(2,1)S(1)}, bf16[32,1024]{1,0:T(8,128)(2,1)S(1)}, u32[]{:S(2)}, u32[]{:S(2)}) collective-permute-start(bf16[32,1024]{1,0:T(8,128)(2,1)S(1)} %get-tuple-element.66), channel_id=1, source_target_pairs={{0,2},{1,3},{2,0},{3,1},{4,6},{5,7},{6,4},{7,5},{8,10},{9,11},{10,... | collective-permute-start | bytes 196616 | tf_op jit(solution)/shard_map/ppermute | solution.py:660
  364.8 1.2 copy-start.15
  370.3 0.9 copy-start
  397.8 0.8 copy-start.18
  398.5 8.9 %collective-permute-start.11 = (bf16[160,1024]{1,0:T(8,128)(2,1)}, bf16[160,1024]{1,0:T(8,128)(2,1)S(1)}, u32[]{:S(2)}, u32[]{:S(2)}) collective-permute-start(bf16[160,1024]{1,0:T(8,128)(2,1)} %get-tuple-element.86), channel_id=1, source_target_pairs={{0,2},{1,3},{2,0},{3,1},{4,6},{5,7},{6,4},{7,5},{8,10},{9,11},{10,... | collective-permute-start | bytes 983048 | tf_op jit(solution)/shard_map/ppermute | solution.py:660
  398.7 1.0 copy-start.2
  399.7 1.2 copy-start.14
  405.3 5.4 %copy-start.19 = (bf16[224,1024]{1,0:T(8,128)(2,1)S(1)}, bf16[224,1024]{1,0:T(8,128)(2,1)}, u32[]{:S(2)}) copy-start(bf16[224,1024]{1,0:T(8,128)(2,1)} %copy-done.18) | copy-start | bytes 1376260
  407.6 1.4 collective-permute-start.12
  409.0 9.2 %collective-permute-start.13 = (bf16[4,16,1024]{2,1,0:T(8,128)(2,1)S(1)}, bf16[4,16,1024]{2,1,0:T(8,128)(2,1)S(1)}, u32[]{:S(2)}, u32[]{:S(2)}) collective-permute-start(bf16[4,16,1024]{2,1,0:T(8,128)(2,1)S(1)} %fusion.5), channel_id=1, source_target_pairs={{0,16},{4,20},{8,24},{12,28},{16,0},{20,4},{24,8},{28,12},{1,17},{... | collective-permute-start | bytes 393224 | tf_op jit(solution)/shard_map/ppermute | solution.py:607
  410.7 14.4 %collective-permute-start.10 = (bf16[224,1024]{1,0:T(8,128)(2,1)S(1)}, bf16[224,1024]{1,0:T(8,128)(2,1)S(1)}, u32[]{:S(2)}, u32[]{:S(2)}) collective-permute-start(bf16[224,1024]{1,0:T(8,128)(2,1)S(1)} %copy-done.19), channel_id=1, source_target_pairs={{1,2},{2,1},{5,6},{6,5},{9,10},{10,9},{13,14},{14,13},{17,18},{18,... | collective-permute-start | bytes 1376264 | tf_op jit(solution)/shard_map/ppermute | solution.py:659
  411.4 13.7 %collective-permute-start.9 = (bf16[224,1024]{1,0:T(8,128)(2,1)S(1)}, bf16[224,1024]{1,0:T(8,128)(2,1)S(1)}, u32[]{:S(2)}, u32[]{:S(2)}) collective-permute-start(bf16[224,1024]{1,0:T(8,128)(2,1)S(1)} %get-tuple-element.84), channel_id=1, source_target_pairs={{0,1},{1,0},{2,3},{3,2},{4,5},{5,4},{6,7},{7,6},{8,9},{9,8},{10,11... | collective-permute-start | bytes 1376264 | tf_op jit(solution)/shard_map/ppermute | solution.py:658
  418.2 5.5 %collective-permute-start.14 = (bf16[4,16,1024]{2,1,0:T(8,128)(2,1)S(1)}, bf16[4,16,1024]{2,1,0:T(8,128)(2,1)S(1)}, u32[]{:S(2)}, u32[]{:S(2)}) collective-permute-start(bf16[4,16,1024]{2,1,0:T(8,128)(2,1)S(1)} %fusion.1), channel_id=1, source_target_pairs={{0,8},{4,12},{8,0},{12,4},{16,24},{20,28},{24,16},{28,20},{1,9},{5... | collective-permute-start | bytes 393224 | tf_op jit(solution)/shard_map/ppermute | solution.py:607
  423.8 5.0 %collective-permute-start.15 = (bf16[4,16,1024]{2,1,0:T(8,128)(2,1)S(1)}, bf16[4,16,1024]{2,1,0:T(8,128)(2,1)S(1)}, u32[]{:S(2)}, u32[]{:S(2)}) collective-permute-start(bf16[4,16,1024]{2,1,0:T(8,128)(2,1)S(1)} %fusion.3), channel_id=1, source_target_pairs={{0,4},{4,0},{8,12},{12,8},{16,20},{20,16},{24,28},{28,24},{1,5},{5... | collective-permute-start | bytes 393224 | tf_op jit(solution)/shard_map/ppermute | solution.py:607
Sparse Core Ops, SparseCore 0:
  10.9 197.4 all-gather.4
  211.2 119.3 all-gather.2
